TPU v7x, 32 devices: a whole 2x2x4 slice. The times are simulated.
32 devices in a mesh: dp: 16 (over z, y, core), seq: 2 (over x).
Axes of the slice: x: 2, y: 2, z: 4, core: 2. Of those that a mesh axis runs over, the one named last changes fastest.
Arguments:
- tokens: bfloat16 [16, 256, 8192], P('dp', None, 'seq'), may hold values from -6 to 6
- queries: bfloat16 [16, 256, 1024], P('dp', 'seq'), may hold values from -96 to 96
- grad_out: bfloat16 [16, 256, 1024], P('dp', 'seq'), may hold values from -6 to 6
- w_kv: bfloat16 [8192, 256], P('seq'), may hold values from -0.0625 to 0.0625
- doc_ids: int32 [16, 256], P('dp'), may hold values from 0 to 5, never falling along the last dimension, each value on 1 to 85 neighbouring positions
- span_order: int32 [2], replicated, may hold values from 0 to 1, each once
Outputs:
- attention: bfloat16 [16, 256, 1024], P('dp', 'seq')
- query_grad: bfloat16 [16, 256, 1024], P('dp', 'seq')
- weight_grad: bfloat16 [8192, 256], P('seq')
Inputs may be any that keep to these rules, and one draw needn't show every extreme that they name: `doc_ids`: document ids never fall along positions; every id is used; a document holds at most 85 positions. `span_order`: each block index appears once.
All inputs are finite; a program needn't handle non-finite values.
Results may differ from a plain program's by a relative error of at most 0.007.
The roundings to bfloat16 on the way count: a program that leaves them out, or rounds other values in their place, can miss the bound.
Values may be sent and summed in bfloat16 or wider, within the bound.
No kernel may reach another device: no remote copies, remote signals or barrier semaphores. Data moves between devices by JAX's collectives and lax.ppermute only.
A program may use at most 64 MiB of HBM per device.

v0:
```python
import functools
import math

import jax
import jax.numpy as jnp
from jax import lax
from jax.experimental import pallas as pl
from jax.experimental.pallas import tpu as pltpu
from jax.sharding import PartitionSpec as P

HEAD = 128
QH = 8
GROUP = 2
F32 = jnp.float32
BF16 = jnp.bfloat16
NT = (((1,), (1,)), ((), ()))
TN = (((0,), (0,)), ((), ()))
NN = (((1,), (0,)), ((), ()))


def _mm(a, b, dims):
    return lax.dot_general(a, b, dims, preferred_element_type=F32)


ANY = pl.BlockSpec(memory_space=pl.ANY)
VMEM = pl.BlockSpec(memory_space=pltpu.VMEM)
LIMIT = pltpu.CompilerParams(vmem_limit_bytes=48 * 1024 * 1024)


def terms_kernel(parts, own, order_ref, docs_ref, q_ref, g_ref, *refs):
    kv_refs = refs[:parts]
    kv_ref, low_ref, ds_ref, terms_ref = refs[-4:]
    rows = q_ref.shape[0]
    seq_len = kv_refs[0].shape[0]
    spans = seq_len // rows
    if parts == 1:
        kv = kv_refs[0][...]
    else:
        kv = (kv_refs[0][...] + kv_refs[1][...]).astype(BF16)
    kv_ref[...] = kv
    keys = kv[:, :HEAD]
    values = kv[:, HEAD:]
    scale = 1.0 / math.sqrt(HEAD)
    me = lax.axis_index(own)

    def row_docs(span):
        return docs_ref[pl.ds(order_ref[span], 1), :]

    masks = []
    q_docs = row_docs(me)
    q_span = order_ref[me]
    q_pos = lax.broadcasted_iota(jnp.int32, (rows, rows), 1)
    k_pos = lax.broadcasted_iota(jnp.int32, (rows, rows), 0)
    for span in range(spans):
        k_docs = jnp.broadcast_to(row_docs(span), (rows, rows)).T
        gap = (order_ref[span] - q_span) * rows
        masks.append((k_pos + gap <= q_pos) & (k_docs == q_docs))
    allowed = jnp.concatenate(masks, axis=0)
    allowed = jnp.concatenate([allowed] * GROUP, axis=1)

    key_grad = jnp.zeros((seq_len, HEAD), F32)
    value_grad = jnp.zeros((seq_len, HEAD), F32)
    for first in range(0, QH, GROUP):
        heads = range(first, first + GROUP)
        q = jnp.concatenate([q_ref[:, h * HEAD : (h + 1) * HEAD] for h in heads], axis=0)
        g = jnp.concatenate([g_ref[:, h * HEAD : (h + 1) * HEAD] for h in heads], axis=0)
        scores = jnp.where(allowed, _mm(keys, q, NT) * scale, F32(-1e30))
        expo = jnp.exp(scores - jnp.max(scores, axis=0, keepdims=True))
        probs = expo * (1.0 / jnp.sum(expo, axis=0, keepdims=True))
        low = probs.astype(BF16)
        grad_probs = _mm(values, g, NT)
        delta = jnp.sum(probs * grad_probs, axis=0, keepdims=True)
        grad_scores = (probs * (grad_probs - delta) * scale).astype(BF16)
        low_ref[:, first * rows : (first + GROUP) * rows] = low
        ds_ref[:, first * rows : (first + GROUP) * rows] = grad_scores
        key_grad += _mm(grad_scores, q, NN)
        value_grad += _mm(low, g, NN)
    terms_ref[:HEAD, :] = key_grad.T
    terms_ref[HEAD:, :] = value_grad.T


def outputs_kernel(kv_ref, low_ref, ds_ref, att_ref, qg_ref, done_ref):
    rows = att_ref.shape[0]
    done_ref[...] = jnp.zeros_like(done_ref)
    keys_t = kv_ref[:, :HEAD].T
    values_t = kv_ref[:, HEAD:].T
    for first in range(0, QH, GROUP):
        cols = slice(first * rows, (first + GROUP) * rows)
        att = _mm(values_t, low_ref[:, cols], NN)
        qg = _mm(keys_t, ds_ref[:, cols], NN)
        for i in range(GROUP):
            head = slice((first + i) * HEAD, (first + i + 1) * HEAD)
            att_ref[:, head] = att[:, i * rows : (i + 1) * rows].T.astype(BF16)
            qg_ref[:, head] = qg[:, i * rows : (i + 1) * rows].T.astype(BF16)


def attend(order, docs, q, g, kvs):
    seq_len, rows = kvs[0].shape[0], q.shape[0]
    kv, low, grad_scores, terms = pl.pallas_call(
        functools.partial(terms_kernel, len(kvs), "seq"),
        out_shape=(
            jax.ShapeDtypeStruct((seq_len, 2 * HEAD), BF16),
            jax.ShapeDtypeStruct((seq_len, QH * rows), BF16),
            jax.ShapeDtypeStruct((seq_len, QH * rows), BF16),
            jax.ShapeDtypeStruct((2 * HEAD, seq_len), F32),
        ),
        in_specs=[pl.BlockSpec(memory_space=pltpu.SMEM)] + [VMEM] * (3 + len(kvs)),
        out_specs=[VMEM] * 4,
        compiler_params=LIMIT,
        name="attention_terms",
    )(order, docs, q, g, *kvs)
    attention, query_grad, done = pl.pallas_call(
        outputs_kernel,
        out_shape=[jax.ShapeDtypeStruct(q.shape, BF16)] * 2 + [jax.ShapeDtypeStruct((8, HEAD), F32)],
        in_specs=[VMEM] * 3,
        out_specs=[VMEM] * 3,
        compiler_params=LIMIT,
        name="attention_outputs",
    )(kv, low, grad_scores)
    return attention, query_grad, terms, done


CORE, Y, Z1, Z2 = 1, 2, 4, 8
CORES = 2
BLOCK = 4


def block_of(device):
    return lax.rem(device // CORES, BLOCK)


def half_cols(device, k, core, far_half, width):
    high = device // (CORES * BLOCK)
    high = 1 - high if far_half else high
    return pl.multiple_of((((block_of(device) ^ k) * CORES + core) * 2 + high) * width, width)


def slice_kernel(wanted, tok_ref, *refs):
    slices, sems = refs[-1 - len(wanted) : -1], refs[-1]
    me = lax.axis_index("dp")
    copies = []
    for (k, halves), ref in zip(wanted, slices):
        width = ref.shape[1] // (CORES * len(halves))
        for n, far_half in enumerate(halves):
            for core in range(CORES):
                copy = pltpu.make_async_copy(
                    tok_ref.at[:, pl.ds(half_cols(me, k, core, far_half, width), width)],
                    ref.at[:, pl.ds((n * CORES + core) * width, width)],
                    sems.at[len(copies)],
                )
                copy.start()
                copies.append(copy)
    for copy in copies:
        copy.wait()


def slice_tokens(tokens, wanted, name, after=()):
    rows, features = tokens.shape
    half = features // (2 * BLOCK)
    return pl.pallas_call(
        functools.partial(slice_kernel, wanted),
        out_shape=[jax.ShapeDtypeStruct((rows, half * len(halves)), BF16) for _, halves in wanted],
        in_specs=[ANY] * (1 + len(after)),
        out_specs=[VMEM] * len(wanted),
        scratch_shapes=[pltpu.SemaphoreType.DMA((sum(2 * len(halves) for _, halves in wanted),))],
        compiler_params=LIMIT,
        name=name,
    )(tokens, *after)


def project_kernel(tok_ref, w_ref, out_ref):
    out_ref[...] = _mm(tok_ref[...], w_ref[...], NN)


def project(tokens, w_kv):
    return pl.pallas_call(
        project_kernel,
        out_shape=jax.ShapeDtypeStruct((tokens.shape[0], w_kv.shape[1]), F32),
        in_specs=[VMEM, VMEM],
        out_specs=VMEM,
        compiler_params=LIMIT,
        name="project",
    )(tokens, w_kv)


def after_kernel(in_ref, *refs):
    refs[-1][...] = in_ref[...]


def after(value, arrived):
    return pl.pallas_call(
        after_kernel,
        out_shape=jax.ShapeDtypeStruct(value.shape, value.dtype),
        in_specs=[VMEM] + [ANY] * len(arrived),
        out_specs=VMEM,
        compiler_params=LIMIT,
        name="after",
    )(value, *arrived)


def round_kernel(a_ref, b_ref, *refs):
    refs[-1][...] = (a_ref[...] + b_ref[...]).astype(BF16)


def round_grad(a, b, arrived):
    return pl.pallas_call(
        round_kernel,
        out_shape=jax.ShapeDtypeStruct(a.shape, BF16),
        in_specs=[VMEM, VMEM] + [ANY] * len(arrived),
        out_specs=VMEM,
        compiler_params=LIMIT,
        name="round_grad",
    )(a, b, *arrived)


def weight_kernel(packs, starts, *refs):
    toks, grads = refs[:BLOCK], refs[BLOCK : 2 * BLOCK]
    keep_ref, send_ref = refs[2 * BLOCK :]
    width = keep_ref.shape[1]
    starts = [start * width for start in starts]
    core = lax.rem(lax.axis_index("dp"), CORES)
    for ref, which in ((send_ref, 1 - core), (keep_ref, core)):
        acc = None
        for k in range(BLOCK):
            first = pl.multiple_of(starts[k] + which * width, width)
            term = _mm(grads[k][...], toks[k][:, pl.ds(first, width)], NN)
            acc = term if acc is None else acc + term
        ref[...] = acc * (1.0 / packs)


def weight_part(toks, grads, packs, starts):
    part = jax.ShapeDtypeStruct((grads[0].shape[0], toks[0].shape[1] // CORES), F32)
    return pl.pallas_call(
        functools.partial(weight_kernel, packs, starts),
        out_shape=[part, part],
        in_specs=[VMEM] * (2 * BLOCK),
        out_specs=[VMEM, VMEM],
        compiler_params=LIMIT,
        name="weight_part",
    )(*toks, *grads)


def fold_kernel(a_ref, b_ref, out_ref):
    out_ref[...] = a_ref[...] + b_ref[...]


def fold(a, b):
    return pl.pallas_call(
        fold_kernel,
        out_shape=jax.ShapeDtypeStruct(a.shape, F32),
        in_specs=[VMEM, VMEM],
        out_specs=VMEM,
        compiler_params=LIMIT,
        name="weight_fold",
    )(a, b)


def finish_kernel(a_ref, b_ref, out_ref):
    out_ref[...] = (a_ref[...] + b_ref[...]).T.astype(BF16)


def finish(a, b):
    return pl.pallas_call(
        finish_kernel,
        out_shape=jax.ShapeDtypeStruct((a.shape[1], a.shape[0]), BF16),
        in_specs=[VMEM] * 2,
        out_specs=VMEM,
        compiler_params=LIMIT,
        name="weight_finish",
    )(a, b)


def stack_kernel(count, *refs):
    out_ref = refs[-1]
    first = 0
    for ref in refs[:count]:
        out_ref[first : first + ref.shape[0], :] = ref[...]
        first += ref.shape[0]


def stack(parts, after=()):
    rows = sum(part.shape[0] for part in parts)
    return pl.pallas_call(
        functools.partial(stack_kernel, len(parts)),
        out_shape=jax.ShapeDtypeStruct((rows, parts[0].shape[1]), BF16),
        in_specs=[VMEM] * len(parts) + [ANY] * len(after),
        out_specs=VMEM,
        compiler_params=LIMIT,
        name="stack",
    )(*parts, *after)


def assemble_kernel(held, rows, *refs):
    arrays, out_ref, sems = refs[: len(held)], refs[-2], refs[-1]
    me = lax.axis_index("dp")
    copies = []
    for array, bits in zip(arrays, held):
        for n, bit in enumerate(bits):
            source = me ^ bit
            high = source // (CORES * BLOCK)
            place = (block_of(source) * CORES + lax.rem(source, CORES)) * 2 + high
            first = pl.multiple_of(place * rows, rows)
            copy = pltpu.make_async_copy(
                array.at[pl.ds(n * rows, rows), :],
                out_ref.at[pl.ds(first, rows), :],
                sems.at[len(copies)],
            )
            copy.start()
            copies.append(copy)
    for copy in copies:
        copy.wait()


def assemble(pieces, total, begun=None):
    arrays = [array for array, _ in pieces]
    held = [bits for _, bits in pieces]
    rows = arrays[0].shape[0] // len(held[0])
    count = len(arrays)
    if begun is not None:
        arrays.append(begun)
    return pl.pallas_call(
        functools.partial(assemble_kernel, held, rows),
        out_shape=jax.ShapeDtypeStruct((total * rows, arrays[0].shape[1]), BF16),
        in_specs=[ANY] * len(arrays),
        out_specs=ANY,
        scratch_shapes=[pltpu.SemaphoreType.DMA((sum(len(bits) for bits in held),))],
        input_output_aliases={} if begun is None else {count: 0},
        compiler_params=LIMIT,
        name="weight_assemble" if begun is None else "weight_complete",
    )(*arrays)


def hop(value, bits):
    count = lax.axis_size("dp")
    return lax.ppermute(value, "dp", [(i, i ^ bits) for i in range(count)])


def per_device_16x2(tokens, queries, grad_out, w_kv, doc_ids, span_order):
    dp_size = lax.axis_size("dp")
    rows_dev = queries.shape[1]
    swap = [(0, 1), (1, 0)]
    near = (Y, Z1, Y | Z1)
    flat = tokens[0]
    far_own, far_y, far_z, diagonal = slice_tokens(
        flat, [(0, (True,)), (1, (True,)), (2, (True,)), (3, (True, False))], "slice_far"
    )
    far_y, far_z, diagonal = hop(far_y, Y), hop(far_z, Z1), hop(diagonal, Y | Z1)
    partial = project(flat, w_kv)
    other = lax.ppermute(partial, "seq", swap)
    docs = doc_ids.reshape(-1, rows_dev)
    attention, query_grad, terms, done = attend(
        span_order, docs, queries[0], grad_out[0], [partial, other]
    )
    terms = after(terms, [far_y, far_z])
    grad = round_grad(terms, lax.ppermute(terms, "seq", swap), [done])
    grads = [grad] + [hop(grad, bits) for bits in near]
    keep, send = weight_part([far_own, far_y, far_z, diagonal], grads, dp_size, [0, 0, 0, 0])
    part = fold(keep, hop(send, CORE))
    far = hop(part, Z2)
    near_own, near_y, near_z = slice_tokens(
        flat, [(0, (False,)), (1, (False,)), (2, (False,))], "slice_near", []
    )
    near_y, near_z = hop(near_y, Y), hop(near_z, Z1)
    keep, send = weight_part([near_own, near_y, near_z, diagonal], grads, dp_size, [0, 0, 0, 2])
    own = finish(fold(keep, far), hop(send, CORE))
    z1, z2, y = hop(own, Z1), hop(own, Z2), hop(own, Y)
    z12 = hop(z2, Z1)
    zy = hop(stack([z1, z2], [y]), Y)
    z12y = hop(z12, Y)
    first = hop(stack([own, z1, z2, y]), CORE)
    last = hop(stack([zy, z12, z12y]), CORE)
    pieces = [
        (own, [0]),
        (z1, [Z1]),
        (z2, [Z2]),
        (y, [Y]),
        (zy, [Z1 | Y, Z2 | Y]),
        (z12, [Z1 | Z2]),
        (z12y, [Z1 | Z2 | Y]),
    ]
    held = [[bit | CORE for _, bits in part for bit in bits] for part in (pieces[:4], pieces[4:])]
    weight_grad = assemble(pieces + [(first, held[0])], dp_size)
    weight_grad = assemble([(last, held[1])], dp_size, weight_grad)
    return (attention[None], query_grad[None], weight_grad)


def per_device(tokens, queries, grad_out, w_kv, doc_ids, span_order):
    dp_size = lax.axis_size("dp")
    rows_dev = queries.shape[1]
    flat = tokens[0]
    spread = lax.all_to_all(flat, "dp", split_axis=1, concat_axis=0, tiled=True)
    partial = jnp.dot(flat, w_kv, preferred_element_type=F32)
    own = lax.psum_scatter(partial, "seq", scatter_dimension=0, tiled=True).astype(BF16)
    kvs = [lax.all_gather(own, "seq", axis=0, tiled=True)]
    docs = doc_ids.reshape(-1, rows_dev)
    attention, query_grad, terms, done = attend(span_order, docs, queries[0], grad_out[0], kvs)
    grad_kv = lax.psum(terms.T, "seq").astype(BF16)
    all_grads = lax.all_gather(grad_kv, "dp", axis=0, tiled=True)
    piece = (_mm(spread, all_grads, TN) * (1.0 / dp_size)).astype(BF16)
    weight_grad = lax.all_gather(piece, "dp", axis=0, tiled=True)
    return (attention[None], query_grad[None], weight_grad)


def solution(mesh):
    small = mesh.shape["dp"] == 16 and mesh.shape["seq"] == 2
    return jax.shard_map(
        per_device_16x2 if small else per_device,
        mesh=mesh,
        in_specs=(
            P("dp", None, "seq"),
            P("dp", "seq", None),
            P("dp", "seq", None),
            P("seq", None),
            P("dp", None),
            P(),
        ),
        out_specs=(P("dp", "seq", None), P("dp", "seq", None), P("seq", None)),
        check_vma=False,
    )
```

profile of v0, /device:TPU:0, one launch (start us, length us, event | category | flops | bytes accessed | tf_op | source)
XLA Modules:
  0.0 75.2 jit_solution(14021000658983782957)
XLA Ops:
  0.6 1.6 %copy-done = bf16[1,256,4096]{2,1,0:T(8,128)(2,1)S(1)} copy-done((bf16[1,256,4096]{2,1,0:T(8,128)(2,1)S(1)}, bf16[1,256,4096]{2,1,0:T(8,128)(2,1)}, u32[]{:S(2)}) %copy-start) | copy-done | bytes 2097176
  2.2 1.6 %copy-done.2 = bf16[4096,256]{1,0:T(8,128)(2,1)S(1)} copy-done((bf16[4096,256]{1,0:T(8,128)(2,1)S(1)}, bf16[4096,256]{1,0:T(8,128)(2,1)}, u32[]{:S(2)}) %copy-start.2) | copy-done | bytes 2097176
  3.8 0.7 project.1.refs_0_
  4.6 3.0 %collective-permute-start = (f32[256,256]{1,0:T(8,128)S(1)}, f32[256,256]{1,0:T(8,128)S(1)}, u32[]{:S(2)}, u32[]{:S(2)}) collective-permute-start(f32[256,256]{1,0:T(8,128)S(1)} %project.1.refs_0_), channel_id=1, source_target_pairs={{0,1},{1,0},{2,3},{3,2},{4,5},{5,4},{6,7},{7,6},{8,9},{9,8},{10,11... | collective-permute-start | bytes 786440 | tf_op jit(solution)/shard_map/ppermute | solution.py:349
  7.9 1.6 %collective-permute-start.4 = (bf16[256,512]{1,0:T(8,128)(2,1)S(1)}, bf16[256,512]{1,0:T(8,128)(2,1)S(1)}, u32[]{:S(2)}, u32[]{:S(2)}) collective-permute-start(bf16[256,512]{1,0:T(8,128)(2,1)S(1)} %get-tuple-element.31), channel_id=1, source_target_pairs={{0,4},{2,6},{4,0},{6,2},{8,12},{10,14},{12,8},{14,10},{16,20},{18,... | collective-permute-start | bytes 786440 | tf_op jit(solution)/shard_map/ppermute | solution.py:335
  9.5 1.6 %collective-permute-start.5 = (bf16[256,512]{1,0:T(8,128)(2,1)S(1)}, bf16[256,512]{1,0:T(8,128)(2,1)S(1)}, u32[]{:S(2)}, u32[]{:S(2)}) collective-permute-start(bf16[256,512]{1,0:T(8,128)(2,1)S(1)} %get-tuple-element.32), channel_id=1, source_target_pairs={{0,8},{2,10},{4,12},{6,14},{8,0},{10,2},{12,4},{14,6},{16,24},{18,... | collective-permute-start | bytes 786440 | tf_op jit(solution)/shard_map/ppermute | solution.py:335
  11.5 2.4 %collective-permute-done.refs_1_ = f32[256,256]{1,0:T(8,128)S(1)} collective-permute-done((f32[256,256]{1,0:T(8,128)S(1)}, f32[256,256]{1,0:T(8,128)S(1)}, u32[]{:S(2)}, u32[]{:S(2)}) %collective-permute-start) | collective-permute-done | bytes 262176 | tf_op jit(solution)/shard_map/ppermute | solution.py:349
  13.9 2.3 %attention_terms.1 = (bf16[256,256]{1,0:T(8,128)(2,1)S(1)}, bf16[256,1024]{1,0:T(8,128)(2,1)S(1)}, bf16[256,1024]{1,0:T(8,128)(2,1)S(1)}, f32[256,256]{1,0:T(8,128)S(1)}) custom-call(s32[2]{0:T(128)S(1)} %copy-done.6, s32[2,128]{1,0:T(2,128)S(1)} %bitcast.11, bf16[128,1024]{1,0:T(8,128)(2,1)S(1)} %bitcast.9, bf16[128,1024]{1,0:T(8,128)(2,1)S(1)} %bitcast.10, ...), custom_call_target="tpu_custom_call" | custom-call | tf_op jit(solution)/shard_map/attention_terms/pallas_call | solution.py:99
  16.3 2.4 %collective-permute-done.5.refs_1_.refs_2_ = bf16[256,512]{1,0:T(8,128)(2,1)S(1)} collective-permute-done((bf16[256,512]{1,0:T(8,128)(2,1)S(1)}, bf16[256,512]{1,0:T(8,128)(2,1)S(1)}, u32[]{:S(2)}, u32[]{:S(2)}) %collective-permute-start.5) | collective-permute-done | bytes 262176 | tf_op jit(solution)/shard_map/ppermute | solution.py:335
  19.4 1.2 %attention_outputs.1 = (bf16[128,1024]{1,0:T(8,128)(2,1)}, bf16[128,1024]{1,0:T(8,128)(2,1)}, f32[8,128]{1,0:T(8,128)S(1)}) custom-call(bf16[256,256]{1,0:T(8,128)(2,1)S(1)} %get-tuple-element.21.kv_ref, bf16[256,1024]{1,0:T(8,128)(2,1)S(1)} %get-tuple-element.22.low_ref, bf16[256,1024]{1,0:T(8,128)(2,1)S(1)} %get-tuple-element.23.ds_ref), custom_call_target="tpu_custom_call" | custom-call | tf_op jit(solution)/shard_map/attention_outputs/pallas_call | solution.py:112
  20.6 4.6 %collective-permute-done.6.b_ref = f32[256,256]{1,0:T(8,128)S(1)} collective-permute-done((f32[256,256]{1,0:T(8,128)S(1)}, f32[256,256]{1,0:T(8,128)S(1)}, u32[]{:S(2)}, u32[]{:S(2)}) %collective-permute-start.6) | collective-permute-done | bytes 262176 | tf_op jit(solution)/shard_map/ppermute | solution.py:355
  25.2 1.6 %collective-permute-start.9 = (bf16[256,256]{1,0:T(8,128)(2,1)S(1)}, bf16[256,256]{1,0:T(8,128)(2,1)S(1)}, u32[]{:S(2)}, u32[]{:S(2)}) collective-permute-start(bf16[256,256]{1,0:T(8,128)(2,1)S(1)} %round_grad.1.refs_4_), channel_id=1, source_target_pairs={{0,12},{2,14},{4,8},{6,10},{8,4},{10,6},{12,0},{14,2},{16,28},{18,... | collective-permute-start | bytes 393224 | tf_op jit(solution)/shard_map/ppermute | solution.py:335
  27.3 1.5 %collective-permute-start.7 = (bf16[256,256]{1,0:T(8,128)(2,1)S(1)}, bf16[256,256]{1,0:T(8,128)(2,1)S(1)}, u32[]{:S(2)}, u32[]{:S(2)}) collective-permute-start(bf16[256,256]{1,0:T(8,128)(2,1)S(1)} %round_grad.1.refs_4_), channel_id=1, source_target_pairs={{0,4},{2,6},{4,0},{6,2},{8,12},{10,14},{12,8},{14,10},{16,20},{18,... | collective-permute-start | bytes 393224 | tf_op jit(solution)/shard_map/ppermute | solution.py:335
  28.8 1.2 %collective-permute-done.3.refs_3_ = bf16[256,1024]{1,0:T(8,128)(2,1)S(1)} collective-permute-done((bf16[256,1024]{1,0:T(8,128)(2,1)S(1)}, bf16[256,1024]{1,0:T(8,128)(2,1)S(1)}, u32[]{:S(2)}, u32[]{:S(2)}) %collective-permute-start.3) | collective-permute-done | bytes 524320 | tf_op jit(solution)/shard_map/ppermute | solution.py:335
  30.0 2.5 %collective-permute-done.9.refs_7_ = bf16[256,256]{1,0:T(8,128)(2,1)S(1)} collective-permute-done((bf16[256,256]{1,0:T(8,128)(2,1)S(1)}, bf16[256,256]{1,0:T(8,128)(2,1)S(1)}, u32[]{:S(2)}, u32[]{:S(2)}) %collective-permute-start.9) | collective-permute-done | bytes 131104 | tf_op jit(solution)/shard_map/ppermute | solution.py:335
  32.4 1.4 %collective-permute-done.8.refs_6_ = bf16[256,256]{1,0:T(8,128)(2,1)S(1)} collective-permute-done((bf16[256,256]{1,0:T(8,128)(2,1)S(1)}, bf16[256,256]{1,0:T(8,128)(2,1)S(1)}, u32[]{:S(2)}, u32[]{:S(2)}) %collective-permute-start.8) | collective-permute-done | bytes 131104 | tf_op jit(solution)/shard_map/ppermute | solution.py:335
  34.6 1.5 %collective-permute-start.1 = (bf16[256,512]{1,0:T(8,128)(2,1)S(1)}, bf16[256,512]{1,0:T(8,128)(2,1)S(1)}, u32[]{:S(2)}, u32[]{:S(2)}) collective-permute-start(bf16[256,512]{1,0:T(8,128)(2,1)S(1)} %get-tuple-element.27), channel_id=1, source_target_pairs={{0,4},{2,6},{4,0},{6,2},{8,12},{10,14},{12,8},{14,10},{16,20},{18,... | collective-permute-start | bytes 786440 | tf_op jit(solution)/shard_map/ppermute | solution.py:335
  36.1 1.6 %collective-permute-start.2 = (bf16[256,512]{1,0:T(8,128)(2,1)S(1)}, bf16[256,512]{1,0:T(8,128)(2,1)S(1)}, u32[]{:S(2)}, u32[]{:S(2)}) collective-permute-start(bf16[256,512]{1,0:T(8,128)(2,1)S(1)} %get-tuple-element.28), channel_id=1, source_target_pairs={{0,8},{2,10},{4,12},{6,14},{8,0},{10,2},{12,4},{14,6},{16,24},{18,... | collective-permute-start | bytes 786440 | tf_op jit(solution)/shard_map/ppermute | solution.py:335
  37.7 2.7 %collective-permute-start.11 = (f32[256,256]{1,0:T(8,128)S(1)}, f32[256,256]{1,0:T(8,128)S(1)}, u32[]{:S(2)}, u32[]{:S(2)}) collective-permute-start(f32[256,256]{1,0:T(8,128)S(1)} %weight_fold.2), channel_id=1, source_target_pairs={{0,16},{2,18},{4,20},{6,22},{8,24},{10,26},{12,28},{14,30},{16,0},... | collective-permute-start | bytes 786440 | tf_op jit(solution)/shard_map/ppermute | solution.py:335
  40.4 3.0 %collective-permute-done.1.refs_1_ = bf16[256,512]{1,0:T(8,128)(2,1)S(1)} collective-permute-done((bf16[256,512]{1,0:T(8,128)(2,1)S(1)}, bf16[256,512]{1,0:T(8,128)(2,1)S(1)}, u32[]{:S(2)}, u32[]{:S(2)}) %collective-permute-start.1) | collective-permute-done | bytes 262176 | tf_op jit(solution)/shard_map/ppermute | solution.py:335
  43.4 6.5 %collective-permute-done.2.refs_2_ = bf16[256,512]{1,0:T(8,128)(2,1)S(1)} collective-permute-done((bf16[256,512]{1,0:T(8,128)(2,1)S(1)}, bf16[256,512]{1,0:T(8,128)(2,1)S(1)}, u32[]{:S(2)}, u32[]{:S(2)}) %collective-permute-start.2) | collective-permute-done | bytes 262176 | tf_op jit(solution)/shard_map/ppermute | solution.py:335
  50.4 2.0 %collective-permute-done.11.b_ref = f32[256,256]{1,0:T(8,128)S(1)} collective-permute-done((f32[256,256]{1,0:T(8,128)S(1)}, f32[256,256]{1,0:T(8,128)S(1)}, u32[]{:S(2)}, u32[]{:S(2)}) %collective-permute-start.11) | collective-permute-done | bytes 262176 | tf_op jit(solution)/shard_map/ppermute | solution.py:335
  53.5 3.2 %collective-permute-start.13 = (bf16[256,256]{1,0:T(8,128)(2,1)S(1)}, bf16[256,256]{1,0:T(8,128)(2,1)S(1)}, u32[]{:S(2)}, u32[]{:S(2)}) collective-permute-start(bf16[256,256]{1,0:T(8,128)(2,1)S(1)} %weight_finish.1.refs_0_), channel_id=1, source_target_pairs={{0,8},{2,10},{4,12},{6,14},{8,0},{10,2},{12,4},{14,6},{16,24},{18,... | collective-permute-start | bytes 393224 | tf_op jit(solution)/shard_map/ppermute | solution.py:335
  56.7 4.6 %collective-permute-done.14.refs_1_.refs_2_ = bf16[256,256]{1,0:T(8,128)(2,1)S(1)} collective-permute-done((bf16[256,256]{1,0:T(8,128)(2,1)S(1)}, bf16[256,256]{1,0:T(8,128)(2,1)S(1)}, u32[]{:S(2)}, u32[]{:S(2)}) %collective-permute-start.14) | collective-permute-done | bytes 131104 | tf_op jit(solution)/shard_map/ppermute | solution.py:335
  61.3 0.7 collective-permute-done.13.refs_0_.refs_1_
  62.0 1.2 %collective-permute-start.16 = (bf16[512,256]{1,0:T(8,128)(2,1)S(1)}, bf16[512,256]{1,0:T(8,128)(2,1)S(1)}, u32[]{:S(2)}, u32[]{:S(2)}) collective-permute-start(bf16[512,256]{1,0:T(8,128)(2,1)S(1)} %stack.3), channel_id=1, source_target_pairs={{0,4},{2,6},{4,0},{6,2},{8,12},{10,14},{12,8},{14,10},{16,20},{18,... | collective-permute-start | bytes 786440 | tf_op jit(solution)/shard_map/ppermute | solution.py:335
  63.2 3.4 %collective-permute-done.17.refs_1_.refs_5_ = bf16[256,256]{1,0:T(8,128)(2,1)S(1)} collective-permute-done((bf16[256,256]{1,0:T(8,128)(2,1)S(1)}, bf16[256,256]{1,0:T(8,128)(2,1)S(1)}, u32[]{:S(2)}, u32[]{:S(2)}) %collective-permute-start.17) | collective-permute-done | bytes 131104 | tf_op jit(solution)/shard_map/ppermute | solution.py:335
  66.7 0.7 collective-permute-start.18
  67.5 4.9 %collective-permute-done.18.refs_2_.refs_6_ = bf16[256,256]{1,0:T(8,128)(2,1)S(1)} collective-permute-done((bf16[256,256]{1,0:T(8,128)(2,1)S(1)}, bf16[256,256]{1,0:T(8,128)(2,1)S(1)}, u32[]{:S(2)}, u32[]{:S(2)}) %collective-permute-start.18) | collective-permute-done | bytes 131104 | tf_op jit(solution)/shard_map/ppermute | solution.py:335
  72.5 1.3 %weight_assemble.1.refs_1_ = bf16[4096,256]{1,0:T(8,128)(2,1)} custom-call(bf16[256,256]{1,0:T(8,128)(2,1)S(1)} %weight_finish.1.refs_0_, bf16[256,256]{1,0:T(8,128)(2,1)S(1)} %collective-permute-done.13.refs_0_.refs_1_, bf16[256,256]{1,0:T(8,128)(2,1)S(1)} %collective-permute-done.14.refs_1_.refs_2_, ...), custom_call_target="tpu_custom_call" | custom-call | tf_op jit(solution)/shard_map/weight_assemble/pallas_call | solution.py:321
  73.8 0.6 collective-permute-done.19.refs_0_
  74.4 0.8 %weight_complete.1 = bf16[4096,256]{1,0:T(8,128)(2,1)} custom-call(bf16[1024,256]{1,0:T(8,128)(2,1)S(1)} %collective-permute-done.19.refs_0_, bf16[4096,256]{1,0:T(8,128)(2,1)} %weight_assemble.1.refs_1_), custom_call_target="tpu_custom_call", output_to_operand_aliasing={{}: (1, {})} | custom-call | tf_op jit(solution)/shard_map/weight_complete/pallas_call | solution.py:321
  (41 shorter events, 4.5 us)
Async XLA Ops:
  0.6 1.6 %copy-start = (bf16[1,256,4096]{2,1,0:T(8,128)(2,1)S(1)}, bf16[1,256,4096]{2,1,0:T(8,128)(2,1)}, u32[]{:S(2)}) copy-start(bf16[1,256,4096]{2,1,0:T(8,128)(2,1)} %param.6) | copy-start | bytes 6291460
  2.2 1.6 %copy-start.2 = (bf16[4096,256]{1,0:T(8,128)(2,1)S(1)}, bf16[4096,256]{1,0:T(8,128)(2,1)}, u32[]{:S(2)}) copy-start(bf16[4096,256]{1,0:T(8,128)(2,1)} %w_ref.1) | copy-start | bytes 6291460
  4.5 9.4 %copy-start.3 = (bf16[1,128,1024]{2,1,0:T(8,128)(2,1)S(1)}, bf16[1,128,1024]{2,1,0:T(8,128)(2,1)}, u32[]{:S(2)}) copy-start(bf16[1,128,1024]{2,1,0:T(8,128)(2,1)} %param.7) | copy-start | bytes 786436
  4.5 9.4 %copy-start.4 = (bf16[1,128,1024]{2,1,0:T(8,128)(2,1)S(1)}, bf16[1,128,1024]{2,1,0:T(8,128)(2,1)}, u32[]{:S(2)}) copy-start(bf16[1,128,1024]{2,1,0:T(8,128)(2,1)} %param.8) | copy-start | bytes 786436
  4.6 9.3 %copy-start.5 = (s32[1,256]{1,0:T(1,128)S(1)}, s32[1,256]{1,0:T(1,128)}, u32[]{:S(2)}) copy-start(s32[1,256]{1,0:T(1,128)} %param.10) | copy-start | bytes 3076
  4.6 9.3 %copy-start.6 = (s32[2]{0:T(128)S(1)}, s32[2]{0:T(128)}, u32[]{:S(2)}) copy-start(s32[2]{0:T(128)} %order_ref.1) | copy-start | bytes 28
  4.6 9.3 %collective-permute-start = (f32[256,256]{1,0:T(8,128)S(1)}, f32[256,256]{1,0:T(8,128)S(1)}, u32[]{:S(2)}, u32[]{:S(2)}) collective-permute-start(f32[256,256]{1,0:T(8,128)S(1)} %project.1.refs_0_), channel_id=1, source_target_pairs={{0,1},{1,0},{2,3},{3,2},{4,5},{5,4},{6,7},{7,6},{8,9},{9,8},{10,11... | collective-permute-start | bytes 786440 | tf_op jit(solution)/shard_map/ppermute | solution.py:349
  7.9 8.4 %collective-permute-start.4 = (bf16[256,512]{1,0:T(8,128)(2,1)S(1)}, bf16[256,512]{1,0:T(8,128)(2,1)S(1)}, u32[]{:S(2)}, u32[]{:S(2)}) collective-permute-start(bf16[256,512]{1,0:T(8,128)(2,1)S(1)} %get-tuple-element.31), channel_id=1, source_target_pairs={{0,4},{2,6},{4,0},{6,2},{8,12},{10,14},{12,8},{14,10},{16,20},{18,... | collective-permute-start | bytes 786440 | tf_op jit(solution)/shard_map/ppermute | solution.py:335
  9.5 9.2 %collective-permute-start.5 = (bf16[256,512]{1,0:T(8,128)(2,1)S(1)}, bf16[256,512]{1,0:T(8,128)(2,1)S(1)}, u32[]{:S(2)}, u32[]{:S(2)}) collective-permute-start(bf16[256,512]{1,0:T(8,128)(2,1)S(1)} %get-tuple-element.32), channel_id=1, source_target_pairs={{0,8},{2,10},{4,12},{6,14},{8,0},{10,2},{12,4},{14,6},{16,24},{18,... | collective-permute-start | bytes 786440 | tf_op jit(solution)/shard_map/ppermute | solution.py:335
  11.1 18.9 %collective-permute-start.3 = (bf16[256,1024]{1,0:T(8,128)(2,1)S(1)}, bf16[256,1024]{1,0:T(8,128)(2,1)S(1)}, u32[]{:S(2)}, u32[]{:S(2)}) collective-permute-start(bf16[256,1024]{1,0:T(8,128)(2,1)S(1)} %get-tuple-element.29), channel_id=1, source_target_pairs={{0,12},{2,14},{4,8},{6,10},{8,4},{10,6},{12,0},{14,2},{16,28},{18,... | collective-permute-start | bytes 1572872 | tf_op jit(solution)/shard_map/ppermute | solution.py:335
  18.7 15.6 %copy-start.1 = (bf16[1,256,4096]{2,1,0:T(8,128)(2,1)S(1)}, bf16[1,256,4096]{2,1,0:T(8,128)(2,1)}, u32[]{:S(2)}) copy-start(bf16[1,256,4096]{2,1,0:T(8,128)(2,1)} %param.6) | copy-start | bytes 6291460
  18.8 6.4 %collective-permute-start.6 = (f32[256,256]{1,0:T(8,128)S(1)}, f32[256,256]{1,0:T(8,128)S(1)}, u32[]{:S(2)}, u32[]{:S(2)}) collective-permute-start(f32[256,256]{1,0:T(8,128)S(1)} %after.1.a_ref), channel_id=1, source_target_pairs={{0,1},{1,0},{2,3},{3,2},{4,5},{5,4},{6,7},{7,6},{8,9},{9,8},{10,11... | collective-permute-start | bytes 786440 | tf_op jit(solution)/shard_map/ppermute | solution.py:355
  25.2 7.2 %collective-permute-start.9 = (bf16[256,256]{1,0:T(8,128)(2,1)S(1)}, bf16[256,256]{1,0:T(8,128)(2,1)S(1)}, u32[]{:S(2)}, u32[]{:S(2)}) collective-permute-start(bf16[256,256]{1,0:T(8,128)(2,1)S(1)} %round_grad.1.refs_4_), channel_id=1, source_target_pairs={{0,12},{2,14},{4,8},{6,10},{8,4},{10,6},{12,0},{14,2},{16,28},{18,... | collective-permute-start | bytes 393224 | tf_op jit(solution)/shard_map/ppermute | solution.py:335
  26.8 7.1 %collective-permute-start.8 = (bf16[256,256]{1,0:T(8,128)(2,1)S(1)}, bf16[256,256]{1,0:T(8,128)(2,1)S(1)}, u32[]{:S(2)}, u32[]{:S(2)}) collective-permute-start(bf16[256,256]{1,0:T(8,128)(2,1)S(1)} %round_grad.1.refs_4_), channel_id=1, source_target_pairs={{0,8},{2,10},{4,12},{6,14},{8,0},{10,2},{12,4},{14,6},{16,24},{18,... | collective-permute-start | bytes 393224 | tf_op jit(solution)/shard_map/ppermute | solution.py:335
  27.3 6.6 %collective-permute-start.7 = (bf16[256,256]{1,0:T(8,128)(2,1)S(1)}, bf16[256,256]{1,0:T(8,128)(2,1)S(1)}, u32[]{:S(2)}, u32[]{:S(2)}) collective-permute-start(bf16[256,256]{1,0:T(8,128)(2,1)S(1)} %round_grad.1.refs_4_), channel_id=1, source_target_pairs={{0,4},{2,6},{4,0},{6,2},{8,12},{10,14},{12,8},{14,10},{16,20},{18,... | collective-permute-start | bytes 393224 | tf_op jit(solution)/shard_map/ppermute | solution.py:335
  34.3 3.4 %collective-permute-start.10 = (f32[256,256]{1,0:T(8,128)S(1)}, f32[256,256]{1,0:T(8,128)S(1)}, u32[]{:S(2)}, u32[]{:S(2)}) collective-permute-start(f32[256,256]{1,0:T(8,128)S(1)} %get-tuple-element.37), channel_id=1, source_target_pairs={{0,2},{2,0},{4,6},{6,4},{8,10},{10,8},{12,14},{14,12},{16,18},{18,... | collective-permute-start | bytes 786440 | tf_op jit(solution)/shard_map/ppermute | solution.py:335
  34.6 8.7 %collective-permute-start.1 = (bf16[256,512]{1,0:T(8,128)(2,1)S(1)}, bf16[256,512]{1,0:T(8,128)(2,1)S(1)}, u32[]{:S(2)}, u32[]{:S(2)}) collective-permute-start(bf16[256,512]{1,0:T(8,128)(2,1)S(1)} %get-tuple-element.27), channel_id=1, source_target_pairs={{0,4},{2,6},{4,0},{6,2},{8,12},{10,14},{12,8},{14,10},{16,20},{18,... | collective-permute-start | bytes 786440 | tf_op jit(solution)/shard_map/ppermute | solution.py:335
  36.1 13.8 %collective-permute-start.2 = (bf16[256,512]{1,0:T(8,128)(2,1)S(1)}, bf16[256,512]{1,0:T(8,128)(2,1)S(1)}, u32[]{:S(2)}, u32[]{:S(2)}) collective-permute-start(bf16[256,512]{1,0:T(8,128)(2,1)S(1)} %get-tuple-element.28), channel_id=1, source_target_pairs={{0,8},{2,10},{4,12},{6,14},{8,0},{10,2},{12,4},{14,6},{16,24},{18,... | collective-permute-start | bytes 786440 | tf_op jit(solution)/shard_map/ppermute | solution.py:335
  37.7 14.7 %collective-permute-start.11 = (f32[256,256]{1,0:T(8,128)S(1)}, f32[256,256]{1,0:T(8,128)S(1)}, u32[]{:S(2)}, u32[]{:S(2)}) collective-permute-start(f32[256,256]{1,0:T(8,128)S(1)} %weight_fold.2), channel_id=1, source_target_pairs={{0,16},{2,18},{4,20},{6,22},{8,24},{10,26},{12,28},{14,30},{16,0},... | collective-permute-start | bytes 786440 | tf_op jit(solution)/shard_map/ppermute | solution.py:335
  50.4 2.1 %collective-permute-start.12 = (f32[256,256]{1,0:T(8,128)S(1)}, f32[256,256]{1,0:T(8,128)S(1)}, u32[]{:S(2)}, u32[]{:S(2)}) collective-permute-start(f32[256,256]{1,0:T(8,128)S(1)} %get-tuple-element.38), channel_id=1, source_target_pairs={{0,2},{2,0},{4,6},{6,4},{8,10},{10,8},{12,14},{14,12},{16,18},{18,... | collective-permute-start | bytes 786440 | tf_op jit(solution)/shard_map/ppermute | solution.py:335
  52.6 8.7 %collective-permute-start.14 = (bf16[256,256]{1,0:T(8,128)(2,1)S(1)}, bf16[256,256]{1,0:T(8,128)(2,1)S(1)}, u32[]{:S(2)}, u32[]{:S(2)}) collective-permute-start(bf16[256,256]{1,0:T(8,128)(2,1)S(1)} %weight_finish.1.refs_0_), channel_id=1, source_target_pairs={{0,16},{2,18},{4,20},{6,22},{8,24},{10,26},{12,28},{14,30},{16,0},... | collective-permute-start | bytes 393224 | tf_op jit(solution)/shard_map/ppermute | solution.py:335
  52.9 8.4 %collective-permute-start.15 = (bf16[256,256]{1,0:T(8,128)(2,1)S(1)}, bf16[256,256]{1,0:T(8,128)(2,1)S(1)}, u32[]{:S(2)}, u32[]{:S(2)}) collective-permute-start(bf16[256,256]{1,0:T(8,128)(2,1)S(1)} %weight_finish.1.refs_0_), channel_id=1, source_target_pairs={{0,4},{2,6},{4,0},{6,2},{8,12},{10,14},{12,8},{14,10},{16,20},{18,... | collective-permute-start | bytes 393224 | tf_op jit(solution)/shard_map/ppermute | solution.py:335
  53.5 8.5 %collective-permute-start.13 = (bf16[256,256]{1,0:T(8,128)(2,1)S(1)}, bf16[256,256]{1,0:T(8,128)(2,1)S(1)}, u32[]{:S(2)}, u32[]{:S(2)}) collective-permute-start(bf16[256,256]{1,0:T(8,128)(2,1)S(1)} %weight_finish.1.refs_0_), channel_id=1, source_target_pairs={{0,8},{2,10},{4,12},{6,14},{8,0},{10,2},{12,4},{14,6},{16,24},{18,... | collective-permute-start | bytes 393224 | tf_op jit(solution)/shard_map/ppermute | solution.py:335
  61.3 5.4 %collective-permute-start.17 = (bf16[256,256]{1,0:T(8,128)(2,1)S(1)}, bf16[256,256]{1,0:T(8,128)(2,1)S(1)}, u32[]{:S(2)}, u32[]{:S(2)}) collective-permute-start(bf16[256,256]{1,0:T(8,128)(2,1)S(1)} %collective-permute-done.14.refs_1_.refs_2_), channel_id=1, source_target_pairs={{0,8},{2,10},{4,12},{6,14},{8,0},{10,2},{12,4},{14,6},{16,24},{18,... | collective-permute-start | bytes 393224 | tf_op jit(solution)/shard_map/ppermute | solution.py:335
  62.0 10.4 %collective-permute-start.16 = (bf16[512,256]{1,0:T(8,128)(2,1)S(1)}, bf16[512,256]{1,0:T(8,128)(2,1)S(1)}, u32[]{:S(2)}, u32[]{:S(2)}) collective-permute-start(bf16[512,256]{1,0:T(8,128)(2,1)S(1)} %stack.3), channel_id=1, source_target_pairs={{0,4},{2,6},{4,0},{6,2},{8,12},{10,14},{12,8},{14,10},{16,20},{18,... | collective-permute-start | bytes 786440 | tf_op jit(solution)/shard_map/ppermute | solution.py:335
  66.7 5.7 %collective-permute-start.18 = (bf16[256,256]{1,0:T(8,128)(2,1)S(1)}, bf16[256,256]{1,0:T(8,128)(2,1)S(1)}, u32[]{:S(2)}, u32[]{:S(2)}) collective-permute-start(bf16[256,256]{1,0:T(8,128)(2,1)S(1)} %collective-permute-done.17.refs_1_.refs_5_), channel_id=1, source_target_pairs={{0,4},{2,6},{4,0},{6,2},{8,12},{10,14},{12,8},{14,10},{16,20},{18,... | collective-permute-start | bytes 393224 | tf_op jit(solution)/shard_map/ppermute | solution.py:335
  67.4 5.1 %collective-permute-start.20 = (bf16[1024,256]{1,0:T(8,128)(2,1)S(1)}, bf16[1024,256]{1,0:T(8,128)(2,1)S(1)}, u32[]{:S(2)}, u32[]{:S(2)}) collective-permute-start(bf16[1024,256]{1,0:T(8,128)(2,1)S(1)} %stack.5), channel_id=1, source_target_pairs={{0,2},{2,0},{4,6},{6,4},{8,10},{10,8},{12,14},{14,12},{16,18},{18,... | collective-permute-start | bytes 1572872 | tf_op jit(solution)/shard_map/ppermute | solution.py:335
  72.4 2.0 %collective-permute-start.19 = (bf16[1024,256]{1,0:T(8,128)(2,1)S(1)}, bf16[1024,256]{1,0:T(8,128)(2,1)S(1)}, u32[]{:S(2)}, u32[]{:S(2)}) collective-permute-start(bf16[1024,256]{1,0:T(8,128)(2,1)S(1)} %stack.4), channel_id=1, source_target_pairs={{0,2},{2,0},{4,6},{6,4},{8,10},{10,8},{12,14},{14,12},{16,18},{18,... | collective-permute-start | bytes 1572872 | tf_op jit(solution)/shard_map/ppermute | solution.py:335
where the time goes:
time: 75.4 us; the launch traced here: 75.2 us
  waiting for transfers between devices  40.4 us (54%)
  starting transfers between devices  22.8 us (30%)
  Pallas kernels  7.95 us (11%)
  local copies, waits for them, and re-layouts  3.21 us (4%)
  between operations  0.85 us (1%)
    ppermute x19, waiting for transfers between devices, hop(): return lax.ppermute(value, 'dp', [(i, i ^ bits) for i in range(count)])  33.3 us
    ppermute x19, starting transfers between devices, hop(): return lax.ppermute(value, 'dp', [(i, i ^ bits) for i in range(count)])  19.2 us
    ppermute x1, waiting for transfers between devices, per_device_16x2(): grad = round_grad(terms, lax.ppermute(terms, 'seq', swap), [done])  4.63 us
    unnamed x14, local copies, waits for them, and re-layouts  3.21 us
    ppermute x1, starting transfers between devices, per_device_16x2(): other = lax.ppermute(partial, 'seq', swap)  3 us
    ppermute x1, waiting for transfers between devices, per_device_16x2(): other = lax.ppermute(partial, 'seq', swap)  2.43 us
    pallas_call x1, Pallas kernels, attend(): pl.pallas_call(functools.partial(terms_kernel, len(kvs), 'seq'), out_shap...  2.28 us
    pallas_call x2, Pallas kernels, assemble(): pl.pallas_call(functools.partial(assemble_kernel, held, rows), out_shape=...  2.08 us
  transfers between devices with their start and end apart: 21, of which 15 were waited for; matrix products, arithmetic and copies ran while one was open for 0% of the time, Pallas kernels for 8%

commit v1 on v0

--- a/solution.py
+++ b/solution.py
@@ -121,6 +121,7 @@
 
 
 CORE, Y, Z1, Z2 = 1, 2, 4, 8
+CHUNKS = 4
 CORES = 2
 BLOCK = 4
 
@@ -163,39 +164,48 @@
         in_specs=[ANY] * (1 + len(after)),
         out_specs=[VMEM] * len(wanted),
         scratch_shapes=[pltpu.SemaphoreType.DMA((sum(2 * len(halves) for _, halves in wanted),))],
-        compiler_params=LIMIT,
+        compiler_params=pltpu.CompilerParams(vmem_limit_bytes=48 * 1024 * 1024),
         name=name,
     )(tokens, *after)
 
 
-def project_kernel(tok_ref, w_ref, out_ref):
-    out_ref[...] = _mm(tok_ref[...], w_ref[...], NN)
+def project_kernel(tok_ref, w_ref, out_ref, tok_v, w_v, tok_sems, w_sems):
+    chunks, width = w_v.shape[0], w_v.shape[1]
+    reads = []
+    for k in range(chunks):
+        cut = pl.ds(k * width, width)
+        tok = pltpu.make_async_copy(tok_ref.at[:, cut], tok_v.at[k], tok_sems.at[k])
+        w = pltpu.make_async_copy(w_ref.at[cut, :], w_v.at[k], w_sems.at[k])
+        tok.start()
+        w.start()
+        reads.append((tok, w))
+    total = None
+    for k, (tok, w) in enumerate(reads):
+        tok.wait()
+        w.wait()
+        term = _mm(tok_v[k], w_v[k], NN)
+        total = term if total is None else total + term
+    out_ref[...] = total
 
 
 def project(tokens, w_kv):
+    rows, features = tokens.shape
+    cols = w_kv.shape[1]
+    width = features // CHUNKS
     return pl.pallas_call(
         project_kernel,
-        out_shape=jax.ShapeDtypeStruct((tokens.shape[0], w_kv.shape[1]), F32),
-        in_specs=[VMEM, VMEM],
+        out_shape=jax.ShapeDtypeStruct((rows, cols), F32),
+        in_specs=[ANY, ANY],
         out_specs=VMEM,
-        compiler_params=LIMIT,
+        scratch_shapes=[
+            pltpu.VMEM((CHUNKS, rows, width), BF16),
+            pltpu.VMEM((CHUNKS, width, cols), BF16),
+            pltpu.SemaphoreType.DMA((CHUNKS,)),
+            pltpu.SemaphoreType.DMA((CHUNKS,)),
+        ],
+        compiler_params=pltpu.CompilerParams(vmem_limit_bytes=62 * 1024 * 1024),
         name="project",
     )(tokens, w_kv)
-
-
-def after_kernel(in_ref, *refs):
-    refs[-1][...] = in_ref[...]
-
-
-def after(value, arrived):
-    return pl.pallas_call(
-        after_kernel,
-        out_shape=jax.ShapeDtypeStruct(value.shape, value.dtype),
-        in_specs=[VMEM] + [ANY] * len(arrived),
-        out_specs=VMEM,
-        compiler_params=LIMIT,
-        name="after",
-    )(value, *arrived)
 
 
 def round_kernel(a_ref, b_ref, *refs):
@@ -229,7 +239,7 @@
 
 
 def weight_part(toks, grads, packs, starts):
-    part = jax.ShapeDtypeStruct((grads[0].shape[0], toks[0].shape[1] // CORES), F32)
+    part = jax.ShapeDtypeStruct((grads[0].shape[0], toks[-1].shape[1] // CORES), F32)
     return pl.pallas_call(
         functools.partial(weight_kernel, packs, starts),
         out_shape=[part, part],
@@ -341,27 +351,25 @@
     swap = [(0, 1), (1, 0)]
     near = (Y, Z1, Y | Z1)
     flat = tokens[0]
-    far_own, far_y, far_z, diagonal = slice_tokens(
-        flat, [(0, (True,)), (1, (True,)), (2, (True,)), (3, (True, False))], "slice_far"
+    both = (True, False)
+    own, tok_y, tok_z, far_d = slice_tokens(
+        flat, [(0, both), (1, both), (2, both), (3, (True,))], "slice_first"
     )
-    far_y, far_z, diagonal = hop(far_y, Y), hop(far_z, Z1), hop(diagonal, Y | Z1)
+    tok_y, tok_z, far_d = hop(tok_y, Y), hop(tok_z, Z1), hop(far_d, Y | Z1)
     partial = project(flat, w_kv)
     other = lax.ppermute(partial, "seq", swap)
     docs = doc_ids.reshape(-1, rows_dev)
     attention, query_grad, terms, done = attend(
         span_order, docs, queries[0], grad_out[0], [partial, other]
     )
-    terms = after(terms, [far_y, far_z])
-    grad = round_grad(terms, lax.ppermute(terms, "seq", swap), [done])
+    grad = round_grad(terms, lax.ppermute(terms, "seq", swap), [done, tok_y, tok_z])
     grads = [grad] + [hop(grad, bits) for bits in near]
-    keep, send = weight_part([far_own, far_y, far_z, diagonal], grads, dp_size, [0, 0, 0, 0])
+    keep, send = weight_part([own, tok_y, tok_z, far_d], grads, dp_size, [0, 0, 0, 0])
     part = fold(keep, hop(send, CORE))
     far = hop(part, Z2)
-    near_own, near_y, near_z = slice_tokens(
-        flat, [(0, (False,)), (1, (False,)), (2, (False,))], "slice_near", []
-    )
-    near_y, near_z = hop(near_y, Y), hop(near_z, Z1)
-    keep, send = weight_part([near_own, near_y, near_z, diagonal], grads, dp_size, [0, 0, 0, 2])
+    (near_d,) = slice_tokens(flat, [(3, (False,))], "slice_near_diagonal")
+    near_d = hop(near_d, Y | Z1)
+    keep, send = weight_part([own, tok_y, tok_z, near_d], grads, dp_size, [2, 2, 2, 0])
     own = finish(fold(keep, far), hop(send, CORE))
     z1, z2, y = hop(own, Z1), hop(own, Z2), hop(own, Y)
     z12 = hop(z2, Z1)

time: 75.4 us -> 76.5 us (1.015)
  waiting for transfers between devices: 40.4 us -> 36.6 us
  starting transfers between devices: 22.8 us -> 26.3 us
  Pallas kernels: 7.95 us -> 11 us
  local copies, waits for them, and re-layouts: 3.21 us -> 1.62 us
    pallas_call x2 -> x1, Pallas kernels: 0.72 us -> 3.71 us  [project(): pl.pallas_call(project_kernel, out_shape=jax.ShapeDtypeStruct((rows, cols...]
    ppermute x1, waiting for transfers between devices: 4.63 us -> 2.01 us  [per_device_16x2(): lax.ppermute(terms, 'seq', swap)]
    ppermute x19 -> x18, starting transfers between devices: 19.2 us -> 21.5 us  [hop(): return lax.ppermute(value, 'dp', [(i, i ^ bits) for i in range(count)])]
    unnamed x14, local copies, waits for them, and re-layouts: 3.21 us -> 1.62 us
    ppermute x1, starting transfers between devices: 0.6 us -> 1.82 us  [per_device_16x2(): lax.ppermute(terms, 'seq', swap)]
    ppermute x1, waiting for transfers between devices: 2.43 us -> 1.27 us  [per_device_16x2(): other = lax.ppermute(partial, 'seq', swap)]
    ppermute x19 -> x18, waiting for transfers between devices: 33.3 us -> 33.4 us  [hop(): return lax.ppermute(value, 'dp', [(i, i ^ bits) for i in range(count)])]
  transfers between devices with their start and end apart: 21 -> 20, of which waited for: 15 -> 13; matrix products, arithmetic and copies ran while one was open for 0% -> 0% of each run, Pallas kernels for 8% -> 8%
where the time goes in v1:
time: 76.5 us; the launch traced here: 76.4 us
  waiting for transfers between devices  36.6 us (48%)
  starting transfers between devices  26.3 us (34%)
  Pallas kernels  11 us (14%)
  local copies, waits for them, and re-layouts  1.62 us (2%)
  between operations  0.82 us (1%)
    ppermute x18, waiting for transfers between devices, hop(): return lax.ppermute(value, 'dp', [(i, i ^ bits) for i in range(count)])  33.4 us
    ppermute x18, starting transfers between devices, hop(): return lax.ppermute(value, 'dp', [(i, i ^ bits) for i in range(count)])  21.5 us
    pallas_call x1, Pallas kernels, project(): pl.pallas_call(project_kernel, out_shape=jax.ShapeDtypeStruct((rows, cols...  3.71 us
    ppermute x1, starting transfers between devices, per_device_16x2(): other = lax.ppermute(partial, 'seq', swap)  3 us
    pallas_call x1, Pallas kernels, attend(): pl.pallas_call(functools.partial(terms_kernel, len(kvs), 'seq'), out_shap...  2.28 us
    pallas_call x2, Pallas kernels, assemble(): pl.pallas_call(functools.partial(assemble_kernel, held, rows), out_shape=...  2.08 us
    ppermute x1, waiting for transfers between devices, per_device_16x2(): lax.ppermute(terms, 'seq', swap)  2.01 us
    ppermute x1, starting transfers between devices, per_device_16x2(): lax.ppermute(terms, 'seq', swap)  1.82 us
  transfers between devices with their start and end apart: 20, of which 13 were waited for; matrix products, arithmetic and copies ran while one was open for 0% of the time, Pallas kernels for 8%

profile of v1, /device:TPU:0, one launch (start us, length us, event | category | flops | bytes accessed | tf_op | source)
XLA Modules:
  0.0 76.4 jit_solution(17013255073096806882)
XLA Ops:
  0.6 3.7 %project.1.refs_0_ = f32[256,256]{1,0:T(8,128)} custom-call(bf16[256,4096]{1,0:T(8,128)(2,1)} %bitcast.6, bf16[4096,256]{1,0:T(8,128)(2,1)} %w_ref.1), custom_call_target="tpu_custom_call" | custom-call | tf_op jit(solution)/shard_map/project/pallas_call | solution.py:195
  4.3 3.0 %collective-permute-start = (f32[256,256]{1,0:T(8,128)}, f32[256,256]{1,0:T(8,128)S(1)}, u32[]{:S(2)}, u32[]{:S(2)}) collective-permute-start(f32[256,256]{1,0:T(8,128)} %project.1.refs_0_), channel_id=1, source_target_pairs={{0,1},{1,0},{2,3},{3,2},{4,5},{5,4},{6,7},{7,6},{8,9},{9,8},{10,11... | collective-permute-start | bytes 786440 | tf_op jit(solution)/shard_map/ppermute | solution.py:360
  7.4 1.6 %copy-done = bf16[1,256,4096]{2,1,0:T(8,128)(2,1)S(1)} copy-done((bf16[1,256,4096]{2,1,0:T(8,128)(2,1)S(1)}, bf16[1,256,4096]{2,1,0:T(8,128)(2,1)}, u32[]{:S(2)}) %copy-start) | copy-done | bytes 2097176
  9.4 1.6 %collective-permute-start.1 = (bf16[256,1024]{1,0:T(8,128)(2,1)S(1)}, bf16[256,1024]{1,0:T(8,128)(2,1)S(1)}, u32[]{:S(2)}, u32[]{:S(2)}) collective-permute-start(bf16[256,1024]{1,0:T(8,128)(2,1)S(1)} %get-tuple-element.24), channel_id=1, source_target_pairs={{0,4},{2,6},{4,0},{6,2},{8,12},{10,14},{12,8},{14,10},{16,20},{18,... | collective-permute-start | bytes 1572872 | tf_op jit(solution)/shard_map/ppermute | solution.py:345
  11.0 1.6 %collective-permute-start.2 = (bf16[256,1024]{1,0:T(8,128)(2,1)S(1)}, bf16[256,1024]{1,0:T(8,128)(2,1)S(1)}, u32[]{:S(2)}, u32[]{:S(2)}) collective-permute-start(bf16[256,1024]{1,0:T(8,128)(2,1)S(1)} %get-tuple-element.25), channel_id=1, source_target_pairs={{0,8},{2,10},{4,12},{6,14},{8,0},{10,2},{12,4},{14,6},{16,24},{18,... | collective-permute-start | bytes 1572872 | tf_op jit(solution)/shard_map/ppermute | solution.py:345
  12.6 1.3 %collective-permute-done.refs_1_ = f32[256,256]{1,0:T(8,128)S(1)} collective-permute-done((f32[256,256]{1,0:T(8,128)}, f32[256,256]{1,0:T(8,128)S(1)}, u32[]{:S(2)}, u32[]{:S(2)}) %collective-permute-start) | collective-permute-done | bytes 262176 | tf_op jit(solution)/shard_map/ppermute | solution.py:360
  13.9 2.3 %attention_terms.1 = (bf16[256,256]{1,0:T(8,128)(2,1)S(1)}, bf16[256,1024]{1,0:T(8,128)(2,1)S(1)}, bf16[256,1024]{1,0:T(8,128)(2,1)S(1)}, f32[256,256]{1,0:T(8,128)S(1)}) custom-call(s32[2]{0:T(128)S(1)} %copy-done.6, s32[2,128]{1,0:T(2,128)S(1)} %bitcast.11, bf16[128,1024]{1,0:T(8,128)(2,1)S(1)} %bitcast.9, bf16[128,1024]{1,0:T(8,128)(2,1)S(1)} %bitcast.10, ...), custom_call_target="tpu_custom_call" | custom-call | tf_op jit(solution)/shard_map/attention_terms/pallas_call | solution.py:99
  16.2 1.8 %collective-permute-start.4 = (f32[256,256]{1,0:T(8,128)S(1)}, f32[256,256]{1,0:T(8,128)S(1)}, u32[]{:S(2)}, u32[]{:S(2)}) collective-permute-start(f32[256,256]{1,0:T(8,128)S(1)} %get-tuple-element.26.a_ref), channel_id=1, source_target_pairs={{0,1},{1,0},{2,3},{3,2},{4,5},{5,4},{6,7},{7,6},{8,9},{9,8},{10,11... | collective-permute-start | bytes 786440 | tf_op jit(solution)/shard_map/ppermute | solution.py:365
  18.0 2.5 %collective-permute-start.8 = (bf16[256,512]{1,0:T(8,128)(2,1)S(1)}, bf16[256,512]{1,0:T(8,128)(2,1)S(1)}, u32[]{:S(2)}, u32[]{:S(2)}) collective-permute-start(bf16[256,512]{1,0:T(8,128)(2,1)S(1)} %get-tuple-element.29), channel_id=1, source_target_pairs={{0,12},{2,14},{4,8},{6,10},{8,4},{10,6},{12,0},{14,2},{16,28},{18,... | collective-permute-start | bytes 786440 | tf_op jit(solution)/shard_map/ppermute | solution.py:345
  20.5 1.2 %attention_outputs.1 = (bf16[128,1024]{1,0:T(8,128)(2,1)}, bf16[128,1024]{1,0:T(8,128)(2,1)}, f32[8,128]{1,0:T(8,128)S(1)}) custom-call(bf16[256,256]{1,0:T(8,128)(2,1)S(1)} %get-tuple-element.18.kv_ref, bf16[256,1024]{1,0:T(8,128)(2,1)S(1)} %get-tuple-element.19.low_ref, bf16[256,1024]{1,0:T(8,128)(2,1)S(1)} %get-tuple-element.20.ds_ref), custom_call_target="tpu_custom_call" | custom-call | tf_op jit(solution)/shard_map/attention_outputs/pallas_call | solution.py:112
  21.7 2.0 %collective-permute-done.4.b_ref = f32[256,256]{1,0:T(8,128)S(1)} collective-permute-done((f32[256,256]{1,0:T(8,128)S(1)}, f32[256,256]{1,0:T(8,128)S(1)}, u32[]{:S(2)}, u32[]{:S(2)}) %collective-permute-start.4) | collective-permute-done | bytes 262176 | tf_op jit(solution)/shard_map/ppermute | solution.py:365
  23.7 2.1 %collective-permute-done.2.refs_2_ = bf16[256,1024]{1,0:T(8,128)(2,1)S(1)} collective-permute-done((bf16[256,1024]{1,0:T(8,128)(2,1)S(1)}, bf16[256,1024]{1,0:T(8,128)(2,1)S(1)}, u32[]{:S(2)}, u32[]{:S(2)}) %collective-permute-start.2) | collective-permute-done | bytes 524320 | tf_op jit(solution)/shard_map/ppermute | solution.py:345
  25.9 1.6 %collective-permute-start.7 = (bf16[256,256]{1,0:T(8,128)(2,1)S(1)}, bf16[256,256]{1,0:T(8,128)(2,1)S(1)}, u32[]{:S(2)}, u32[]{:S(2)}) collective-permute-start(bf16[256,256]{1,0:T(8,128)(2,1)S(1)} %round_grad.1.refs_4_), channel_id=1, source_target_pairs={{0,12},{2,14},{4,8},{6,10},{8,4},{10,6},{12,0},{14,2},{16,28},{18,... | collective-permute-start | bytes 393224 | tf_op jit(solution)/shard_map/ppermute | solution.py:345
  27.9 1.5 %collective-permute-start.5 = (bf16[256,256]{1,0:T(8,128)(2,1)S(1)}, bf16[256,256]{1,0:T(8,128)(2,1)S(1)}, u32[]{:S(2)}, u32[]{:S(2)}) collective-permute-start(bf16[256,256]{1,0:T(8,128)(2,1)S(1)} %round_grad.1.refs_4_), channel_id=1, source_target_pairs={{0,4},{2,6},{4,0},{6,2},{8,12},{10,14},{12,8},{14,10},{16,20},{18,... | collective-permute-start | bytes 393224 | tf_op jit(solution)/shard_map/ppermute | solution.py:345
  29.5 2.0 %collective-permute-done.8.refs_3_ = bf16[256,512]{1,0:T(8,128)(2,1)S(1)} collective-permute-done((bf16[256,512]{1,0:T(8,128)(2,1)S(1)}, bf16[256,512]{1,0:T(8,128)(2,1)S(1)}, u32[]{:S(2)}, u32[]{:S(2)}) %collective-permute-start.8) | collective-permute-done | bytes 262176 | tf_op jit(solution)/shard_map/ppermute | solution.py:345
  31.5 2.5 %collective-permute-done.7.refs_7_ = bf16[256,256]{1,0:T(8,128)(2,1)S(1)} collective-permute-done((bf16[256,256]{1,0:T(8,128)(2,1)S(1)}, bf16[256,256]{1,0:T(8,128)(2,1)S(1)}, u32[]{:S(2)}, u32[]{:S(2)}) %collective-permute-start.7) | collective-permute-done | bytes 131104 | tf_op jit(solution)/shard_map/ppermute | solution.py:345
  34.0 1.4 %collective-permute-done.6.refs_6_ = bf16[256,256]{1,0:T(8,128)(2,1)S(1)} collective-permute-done((bf16[256,256]{1,0:T(8,128)(2,1)S(1)}, bf16[256,256]{1,0:T(8,128)(2,1)S(1)}, u32[]{:S(2)}, u32[]{:S(2)}) %collective-permute-start.6) | collective-permute-done | bytes 131104 | tf_op jit(solution)/shard_map/ppermute | solution.py:345
  36.0 2.5 %collective-permute-start.3 = (bf16[256,512]{1,0:T(8,128)(2,1)S(1)}, bf16[256,512]{1,0:T(8,128)(2,1)S(1)}, u32[]{:S(2)}, u32[]{:S(2)}) collective-permute-start(bf16[256,512]{1,0:T(8,128)(2,1)S(1)} %slice_near_diagonal.1), channel_id=1, source_target_pairs={{0,12},{2,14},{4,8},{6,10},{8,4},{10,6},{12,0},{14,2},{16,28},{18,... | collective-permute-start | bytes 786440 | tf_op jit(solution)/shard_map/ppermute | solution.py:345
  38.6 2.7 %collective-permute-start.10 = (f32[256,256]{1,0:T(8,128)S(1)}, f32[256,256]{1,0:T(8,128)S(1)}, u32[]{:S(2)}, u32[]{:S(2)}) collective-permute-start(f32[256,256]{1,0:T(8,128)S(1)} %weight_fold.2), channel_id=1, source_target_pairs={{0,16},{2,18},{4,20},{6,22},{8,24},{10,26},{12,28},{14,30},{16,0},... | collective-permute-start | bytes 786440 | tf_op jit(solution)/shard_map/ppermute | solution.py:345
  41.2 9.8 %collective-permute-done.3.refs_3_ = bf16[256,512]{1,0:T(8,128)(2,1)S(1)} collective-permute-done((bf16[256,512]{1,0:T(8,128)(2,1)S(1)}, bf16[256,512]{1,0:T(8,128)(2,1)S(1)}, u32[]{:S(2)}, u32[]{:S(2)}) %collective-permute-start.3) | collective-permute-done | bytes 262176 | tf_op jit(solution)/shard_map/ppermute | solution.py:345
  51.6 2.0 %collective-permute-done.10.b_ref = f32[256,256]{1,0:T(8,128)S(1)} collective-permute-done((f32[256,256]{1,0:T(8,128)S(1)}, f32[256,256]{1,0:T(8,128)S(1)}, u32[]{:S(2)}, u32[]{:S(2)}) %collective-permute-start.10) | collective-permute-done | bytes 262176 | tf_op jit(solution)/shard_map/ppermute | solution.py:345
  54.1 0.8 %collective-permute-start.14 = (bf16[256,256]{1,0:T(8,128)(2,1)S(1)}, bf16[256,256]{1,0:T(8,128)(2,1)S(1)}, u32[]{:S(2)}, u32[]{:S(2)}) collective-permute-start(bf16[256,256]{1,0:T(8,128)(2,1)S(1)} %weight_finish.1.refs_0_), channel_id=1, source_target_pairs={{0,4},{2,6},{4,0},{6,2},{8,12},{10,14},{12,8},{14,10},{16,20},{18,... | collective-permute-start | bytes 393224 | tf_op jit(solution)/shard_map/ppermute | solution.py:345
  54.8 3.5 %collective-permute-start.12 = (bf16[256,256]{1,0:T(8,128)(2,1)S(1)}, bf16[256,256]{1,0:T(8,128)(2,1)S(1)}, u32[]{:S(2)}, u32[]{:S(2)}) collective-permute-start(bf16[256,256]{1,0:T(8,128)(2,1)S(1)} %weight_finish.1.refs_0_), channel_id=1, source_target_pairs={{0,8},{2,10},{4,12},{6,14},{8,0},{10,2},{12,4},{14,6},{16,24},{18,... | collective-permute-start | bytes 393224 | tf_op jit(solution)/shard_map/ppermute | solution.py:345
  58.3 4.2 %collective-permute-done.13.refs_1_.refs_2_ = bf16[256,256]{1,0:T(8,128)(2,1)S(1)} collective-permute-done((bf16[256,256]{1,0:T(8,128)(2,1)S(1)}, bf16[256,256]{1,0:T(8,128)(2,1)S(1)}, u32[]{:S(2)}, u32[]{:S(2)}) %collective-permute-start.13) | collective-permute-done | bytes 131104 | tf_op jit(solution)/shard_map/ppermute | solution.py:345
  62.4 1.3 %collective-permute-done.12.refs_0_.refs_1_ = bf16[256,256]{1,0:T(8,128)(2,1)S(1)} collective-permute-done((bf16[256,256]{1,0:T(8,128)(2,1)S(1)}, bf16[256,256]{1,0:T(8,128)(2,1)S(1)}, u32[]{:S(2)}, u32[]{:S(2)}) %collective-permute-start.12) | collective-permute-done | bytes 131104 | tf_op jit(solution)/shard_map/ppermute | solution.py:345
  63.8 0.7 collective-permute-start.15
  64.5 3.3 %collective-permute-done.16.refs_1_.refs_5_ = bf16[256,256]{1,0:T(8,128)(2,1)S(1)} collective-permute-done((bf16[256,256]{1,0:T(8,128)(2,1)S(1)}, bf16[256,256]{1,0:T(8,128)(2,1)S(1)}, u32[]{:S(2)}, u32[]{:S(2)}) %collective-permute-start.16) | collective-permute-done | bytes 131104 | tf_op jit(solution)/shard_map/ppermute | solution.py:345
  67.8 1.5 %collective-permute-start.17 = (bf16[256,256]{1,0:T(8,128)(2,1)S(1)}, bf16[256,256]{1,0:T(8,128)(2,1)S(1)}, u32[]{:S(2)}, u32[]{:S(2)}) collective-permute-start(bf16[256,256]{1,0:T(8,128)(2,1)S(1)} %collective-permute-done.16.refs_1_.refs_5_), channel_id=1, source_target_pairs={{0,4},{2,6},{4,0},{6,2},{8,12},{10,14},{12,8},{14,10},{16,20},{18,... | collective-permute-start | bytes 393224 | tf_op jit(solution)/shard_map/ppermute | solution.py:345
  69.4 4.1 %collective-permute-done.17.refs_2_.refs_6_ = bf16[256,256]{1,0:T(8,128)(2,1)S(1)} collective-permute-done((bf16[256,256]{1,0:T(8,128)(2,1)S(1)}, bf16[256,256]{1,0:T(8,128)(2,1)S(1)}, u32[]{:S(2)}, u32[]{:S(2)}) %collective-permute-start.17) | collective-permute-done | bytes 131104 | tf_op jit(solution)/shard_map/ppermute | solution.py:345
  73.7 1.3 %weight_assemble.1.refs_1_ = bf16[4096,256]{1,0:T(8,128)(2,1)} custom-call(bf16[256,256]{1,0:T(8,128)(2,1)S(1)} %weight_finish.1.refs_0_, bf16[256,256]{1,0:T(8,128)(2,1)S(1)} %collective-permute-done.12.refs_0_.refs_1_, bf16[256,256]{1,0:T(8,128)(2,1)S(1)} %collective-permute-done.13.refs_1_.refs_2_, ...), custom_call_target="tpu_custom_call" | custom-call | tf_op jit(solution)/shard_map/weight_assemble/pallas_call | solution.py:331
  74.9 0.6 collective-permute-done.18.refs_0_
  75.5 0.8 %weight_complete.1 = bf16[4096,256]{1,0:T(8,128)(2,1)} custom-call(bf16[1024,256]{1,0:T(8,128)(2,1)S(1)} %collective-permute-done.18.refs_0_, bf16[4096,256]{1,0:T(8,128)(2,1)} %weight_assemble.1.refs_1_), custom_call_target="tpu_custom_call", output_to_operand_aliasing={{}: (1, {})} | custom-call | tf_op jit(solution)/shard_map/weight_complete/pallas_call | solution.py:331
  (38 shorter events, 2.8 us)
Async XLA Ops:
  4.3 9.5 %collective-permute-start = (f32[256,256]{1,0:T(8,128)}, f32[256,256]{1,0:T(8,128)S(1)}, u32[]{:S(2)}, u32[]{:S(2)}) collective-permute-start(f32[256,256]{1,0:T(8,128)} %project.1.refs_0_), channel_id=1, source_target_pairs={{0,1},{1,0},{2,3},{3,2},{4,5},{5,4},{6,7},{7,6},{8,9},{9,8},{10,11... | collective-permute-start | bytes 786440 | tf_op jit(solution)/shard_map/ppermute | solution.py:360
  7.4 1.6 %copy-start = (bf16[1,256,4096]{2,1,0:T(8,128)(2,1)S(1)}, bf16[1,256,4096]{2,1,0:T(8,128)(2,1)}, u32[]{:S(2)}) copy-start(bf16[1,256,4096]{2,1,0:T(8,128)(2,1)} %param.6) | copy-start | bytes 6291460
  8.9 4.9 %copy-start.2 = (f32[256,256]{1,0:T(8,128)S(1)}, f32[256,256]{1,0:T(8,128)}, u32[]{:S(2)}) copy-start(f32[256,256]{1,0:T(8,128)} %project.1.refs_0_) | copy-start | bytes 786436
  8.9 4.9 %copy-start.3 = (bf16[1,128,1024]{2,1,0:T(8,128)(2,1)S(1)}, bf16[1,128,1024]{2,1,0:T(8,128)(2,1)}, u32[]{:S(2)}) copy-start(bf16[1,128,1024]{2,1,0:T(8,128)(2,1)} %param.7) | copy-start | bytes 786436
  8.9 4.9 %copy-start.4 = (bf16[1,128,1024]{2,1,0:T(8,128)(2,1)S(1)}, bf16[1,128,1024]{2,1,0:T(8,128)(2,1)}, u32[]{:S(2)}) copy-start(bf16[1,128,1024]{2,1,0:T(8,128)(2,1)} %param.8) | copy-start | bytes 786436
  8.9 4.9 %copy-start.5 = (s32[1,256]{1,0:T(1,128)S(1)}, s32[1,256]{1,0:T(1,128)}, u32[]{:S(2)}) copy-start(s32[1,256]{1,0:T(1,128)} %param.10) | copy-start | bytes 3076
  9.0 4.9 %copy-start.6 = (s32[2]{0:T(128)S(1)}, s32[2]{0:T(128)}, u32[]{:S(2)}) copy-start(s32[2]{0:T(128)} %order_ref.1) | copy-start | bytes 28
  9.4 14.3 %collective-permute-start.1 = (bf16[256,1024]{1,0:T(8,128)(2,1)S(1)}, bf16[256,1024]{1,0:T(8,128)(2,1)S(1)}, u32[]{:S(2)}, u32[]{:S(2)}) collective-permute-start(bf16[256,1024]{1,0:T(8,128)(2,1)S(1)} %get-tuple-element.24), channel_id=1, source_target_pairs={{0,4},{2,6},{4,0},{6,2},{8,12},{10,14},{12,8},{14,10},{16,20},{18,... | collective-permute-start | bytes 1572872 | tf_op jit(solution)/shard_map/ppermute | solution.py:345
  11.0 14.9 %collective-permute-start.2 = (bf16[256,1024]{1,0:T(8,128)(2,1)S(1)}, bf16[256,1024]{1,0:T(8,128)(2,1)S(1)}, u32[]{:S(2)}, u32[]{:S(2)}) collective-permute-start(bf16[256,1024]{1,0:T(8,128)(2,1)S(1)} %get-tuple-element.25), channel_id=1, source_target_pairs={{0,8},{2,10},{4,12},{6,14},{8,0},{10,2},{12,4},{14,6},{16,24},{18,... | collective-permute-start | bytes 1572872 | tf_op jit(solution)/shard_map/ppermute | solution.py:345
  16.2 7.6 %collective-permute-start.4 = (f32[256,256]{1,0:T(8,128)S(1)}, f32[256,256]{1,0:T(8,128)S(1)}, u32[]{:S(2)}, u32[]{:S(2)}) collective-permute-start(f32[256,256]{1,0:T(8,128)S(1)} %get-tuple-element.26.a_ref), channel_id=1, source_target_pairs={{0,1},{1,0},{2,3},{3,2},{4,5},{5,4},{6,7},{7,6},{8,9},{9,8},{10,11... | collective-permute-start | bytes 786440 | tf_op jit(solution)/shard_map/ppermute | solution.py:365
  18.0 13.5 %collective-permute-start.8 = (bf16[256,512]{1,0:T(8,128)(2,1)S(1)}, bf16[256,512]{1,0:T(8,128)(2,1)S(1)}, u32[]{:S(2)}, u32[]{:S(2)}) collective-permute-start(bf16[256,512]{1,0:T(8,128)(2,1)S(1)} %get-tuple-element.29), channel_id=1, source_target_pairs={{0,12},{2,14},{4,8},{6,10},{8,4},{10,6},{12,0},{14,2},{16,28},{18,... | collective-permute-start | bytes 786440 | tf_op jit(solution)/shard_map/ppermute | solution.py:345
  21.7 14.2 %copy-start.1 = (bf16[1,256,4096]{2,1,0:T(8,128)(2,1)S(1)}, bf16[1,256,4096]{2,1,0:T(8,128)(2,1)}, u32[]{:S(2)}) copy-start(bf16[1,256,4096]{2,1,0:T(8,128)(2,1)} %param.6) | copy-start | bytes 6291460
  25.9 8.1 %collective-permute-start.7 = (bf16[256,256]{1,0:T(8,128)(2,1)S(1)}, bf16[256,256]{1,0:T(8,128)(2,1)S(1)}, u32[]{:S(2)}, u32[]{:S(2)}) collective-permute-start(bf16[256,256]{1,0:T(8,128)(2,1)S(1)} %round_grad.1.refs_4_), channel_id=1, source_target_pairs={{0,12},{2,14},{4,8},{6,10},{8,4},{10,6},{12,0},{14,2},{16,28},{18,... | collective-permute-start | bytes 393224 | tf_op jit(solution)/shard_map/ppermute | solution.py:345
  27.5 7.9 %collective-permute-start.6 = (bf16[256,256]{1,0:T(8,128)(2,1)S(1)}, bf16[256,256]{1,0:T(8,128)(2,1)S(1)}, u32[]{:S(2)}, u32[]{:S(2)}) collective-permute-start(bf16[256,256]{1,0:T(8,128)(2,1)S(1)} %round_grad.1.refs_4_), channel_id=1, source_target_pairs={{0,8},{2,10},{4,12},{6,14},{8,0},{10,2},{12,4},{14,6},{16,24},{18,... | collective-permute-start | bytes 393224 | tf_op jit(solution)/shard_map/ppermute | solution.py:345
  27.9 7.5 %collective-permute-start.5 = (bf16[256,256]{1,0:T(8,128)(2,1)S(1)}, bf16[256,256]{1,0:T(8,128)(2,1)S(1)}, u32[]{:S(2)}, u32[]{:S(2)}) collective-permute-start(bf16[256,256]{1,0:T(8,128)(2,1)S(1)} %round_grad.1.refs_4_), channel_id=1, source_target_pairs={{0,4},{2,6},{4,0},{6,2},{8,12},{10,14},{12,8},{14,10},{16,20},{18,... | collective-permute-start | bytes 393224 | tf_op jit(solution)/shard_map/ppermute | solution.py:345
  35.9 2.7 %collective-permute-start.9 = (f32[256,256]{1,0:T(8,128)S(1)}, f32[256,256]{1,0:T(8,128)S(1)}, u32[]{:S(2)}, u32[]{:S(2)}) collective-permute-start(f32[256,256]{1,0:T(8,128)S(1)} %get-tuple-element.31), channel_id=1, source_target_pairs={{0,2},{2,0},{4,6},{6,4},{8,10},{10,8},{12,14},{14,12},{16,18},{18,... | collective-permute-start | bytes 786440 | tf_op jit(solution)/shard_map/ppermute | solution.py:345
  36.0 15.0 %collective-permute-start.3 = (bf16[256,512]{1,0:T(8,128)(2,1)S(1)}, bf16[256,512]{1,0:T(8,128)(2,1)S(1)}, u32[]{:S(2)}, u32[]{:S(2)}) collective-permute-start(bf16[256,512]{1,0:T(8,128)(2,1)S(1)} %slice_near_diagonal.1), channel_id=1, source_target_pairs={{0,12},{2,14},{4,8},{6,10},{8,4},{10,6},{12,0},{14,2},{16,28},{18,... | collective-permute-start | bytes 786440 | tf_op jit(solution)/shard_map/ppermute | solution.py:345
  38.6 15.0 %collective-permute-start.10 = (f32[256,256]{1,0:T(8,128)S(1)}, f32[256,256]{1,0:T(8,128)S(1)}, u32[]{:S(2)}, u32[]{:S(2)}) collective-permute-start(f32[256,256]{1,0:T(8,128)S(1)} %weight_fold.2), channel_id=1, source_target_pairs={{0,16},{2,18},{4,20},{6,22},{8,24},{10,26},{12,28},{14,30},{16,0},... | collective-permute-start | bytes 786440 | tf_op jit(solution)/shard_map/ppermute | solution.py:345
  51.5 2.1 %collective-permute-start.11 = (f32[256,256]{1,0:T(8,128)S(1)}, f32[256,256]{1,0:T(8,128)S(1)}, u32[]{:S(2)}, u32[]{:S(2)}) collective-permute-start(f32[256,256]{1,0:T(8,128)S(1)} %get-tuple-element.32), channel_id=1, source_target_pairs={{0,2},{2,0},{4,6},{6,4},{8,10},{10,8},{12,14},{14,12},{16,18},{18,... | collective-permute-start | bytes 786440 | tf_op jit(solution)/shard_map/ppermute | solution.py:345
  53.8 8.7 %collective-permute-start.13 = (bf16[256,256]{1,0:T(8,128)(2,1)S(1)}, bf16[256,256]{1,0:T(8,128)(2,1)S(1)}, u32[]{:S(2)}, u32[]{:S(2)}) collective-permute-start(bf16[256,256]{1,0:T(8,128)(2,1)S(1)} %weight_finish.1.refs_0_), channel_id=1, source_target_pairs={{0,16},{2,18},{4,20},{6,22},{8,24},{10,26},{12,28},{14,30},{16,0},... | collective-permute-start | bytes 393224 | tf_op jit(solution)/shard_map/ppermute | solution.py:345
  54.1 8.4 %collective-permute-start.14 = (bf16[256,256]{1,0:T(8,128)(2,1)S(1)}, bf16[256,256]{1,0:T(8,128)(2,1)S(1)}, u32[]{:S(2)}, u32[]{:S(2)}) collective-permute-start(bf16[256,256]{1,0:T(8,128)(2,1)S(1)} %weight_finish.1.refs_0_), channel_id=1, source_target_pairs={{0,4},{2,6},{4,0},{6,2},{8,12},{10,14},{12,8},{14,10},{16,20},{18,... | collective-permute-start | bytes 393224 | tf_op jit(solution)/shard_map/ppermute | solution.py:345
  54.8 8.9 %collective-permute-start.12 = (bf16[256,256]{1,0:T(8,128)(2,1)S(1)}, bf16[256,256]{1,0:T(8,128)(2,1)S(1)}, u32[]{:S(2)}, u32[]{:S(2)}) collective-permute-start(bf16[256,256]{1,0:T(8,128)(2,1)S(1)} %weight_finish.1.refs_0_), channel_id=1, source_target_pairs={{0,8},{2,10},{4,12},{6,14},{8,0},{10,2},{12,4},{14,6},{16,24},{18,... | collective-permute-start | bytes 393224 | tf_op jit(solution)/shard_map/ppermute | solution.py:345
  62.4 5.4 %collective-permute-start.16 = (bf16[256,256]{1,0:T(8,128)(2,1)S(1)}, bf16[256,256]{1,0:T(8,128)(2,1)S(1)}, u32[]{:S(2)}, u32[]{:S(2)}) collective-permute-start(bf16[256,256]{1,0:T(8,128)(2,1)S(1)} %collective-permute-done.13.refs_1_.refs_2_), channel_id=1, source_target_pairs={{0,8},{2,10},{4,12},{6,14},{8,0},{10,2},{12,4},{14,6},{16,24},{18,... | collective-permute-start | bytes 393224 | tf_op jit(solution)/shard_map/ppermute | solution.py:345
  63.8 9.8 %collective-permute-start.15 = (bf16[512,256]{1,0:T(8,128)(2,1)S(1)}, bf16[512,256]{1,0:T(8,128)(2,1)S(1)}, u32[]{:S(2)}, u32[]{:S(2)}) collective-permute-start(bf16[512,256]{1,0:T(8,128)(2,1)S(1)} %stack.3), channel_id=1, source_target_pairs={{0,4},{2,6},{4,0},{6,2},{8,12},{10,14},{12,8},{14,10},{16,20},{18,... | collective-permute-start | bytes 786440 | tf_op jit(solution)/shard_map/ppermute | solution.py:345
  67.8 5.7 %collective-permute-start.17 = (bf16[256,256]{1,0:T(8,128)(2,1)S(1)}, bf16[256,256]{1,0:T(8,128)(2,1)S(1)}, u32[]{:S(2)}, u32[]{:S(2)}) collective-permute-start(bf16[256,256]{1,0:T(8,128)(2,1)S(1)} %collective-permute-done.16.refs_1_.refs_5_), channel_id=1, source_target_pairs={{0,4},{2,6},{4,0},{6,2},{8,12},{10,14},{12,8},{14,10},{16,20},{18,... | collective-permute-start | bytes 393224 | tf_op jit(solution)/shard_map/ppermute | solution.py:345
  69.3 4.3 %collective-permute-start.19 = (bf16[1024,256]{1,0:T(8,128)(2,1)S(1)}, bf16[1024,256]{1,0:T(8,128)(2,1)S(1)}, u32[]{:S(2)}, u32[]{:S(2)}) collective-permute-start(bf16[1024,256]{1,0:T(8,128)(2,1)S(1)} %stack.5), channel_id=1, source_target_pairs={{0,2},{2,0},{4,6},{6,4},{8,10},{10,8},{12,14},{14,12},{16,18},{18,... | collective-permute-start | bytes 1572872 | tf_op jit(solution)/shard_map/ppermute | solution.py:345
  73.6 2.0 %collective-permute-start.18 = (bf16[1024,256]{1,0:T(8,128)(2,1)S(1)}, bf16[1024,256]{1,0:T(8,128)(2,1)S(1)}, u32[]{:S(2)}, u32[]{:S(2)}) collective-permute-start(bf16[1024,256]{1,0:T(8,128)(2,1)S(1)} %stack.4), channel_id=1, source_target_pairs={{0,2},{2,0},{4,6},{6,4},{8,10},{10,8},{12,14},{14,12},{16,18},{18,... | collective-permute-start | bytes 1572872 | tf_op jit(solution)/shard_map/ppermute | solution.py:345

commit v2 on v0

--- a/solution.py
+++ b/solution.py
@@ -183,21 +183,6 @@
     )(tokens, w_kv)
 
 
-def after_kernel(in_ref, *refs):
-    refs[-1][...] = in_ref[...]
-
-
-def after(value, arrived):
-    return pl.pallas_call(
-        after_kernel,
-        out_shape=jax.ShapeDtypeStruct(value.shape, value.dtype),
-        in_specs=[VMEM] + [ANY] * len(arrived),
-        out_specs=VMEM,
-        compiler_params=LIMIT,
-        name="after",
-    )(value, *arrived)
-
-
 def round_kernel(a_ref, b_ref, *refs):
     refs[-1][...] = (a_ref[...] + b_ref[...]).astype(BF16)
 
@@ -229,7 +214,7 @@
 
 
 def weight_part(toks, grads, packs, starts):
-    part = jax.ShapeDtypeStruct((grads[0].shape[0], toks[0].shape[1] // CORES), F32)
+    part = jax.ShapeDtypeStruct((grads[0].shape[0], toks[-1].shape[1] // CORES), F32)
     return pl.pallas_call(
         functools.partial(weight_kernel, packs, starts),
         out_shape=[part, part],
@@ -341,42 +326,39 @@
     swap = [(0, 1), (1, 0)]
     near = (Y, Z1, Y | Z1)
     flat = tokens[0]
-    far_own, far_y, far_z, diagonal = slice_tokens(
-        flat, [(0, (True,)), (1, (True,)), (2, (True,)), (3, (True, False))], "slice_far"
+    both = (True, False)
+    own, tok_y, tok_z, far_d = slice_tokens(
+        flat, [(0, both), (1, both), (2, both), (3, (True,))], "slice_first"
     )
-    far_y, far_z, diagonal = hop(far_y, Y), hop(far_z, Z1), hop(diagonal, Y | Z1)
+    tok_y, tok_z, far_d = hop(tok_y, Y), hop(tok_z, Z1), hop(far_d, Y | Z1)
     partial = project(flat, w_kv)
     other = lax.ppermute(partial, "seq", swap)
     docs = doc_ids.reshape(-1, rows_dev)
     attention, query_grad, terms, done = attend(
         span_order, docs, queries[0], grad_out[0], [partial, other]
     )
-    terms = after(terms, [far_y, far_z])
-    grad = round_grad(terms, lax.ppermute(terms, "seq", swap), [done])
+    grad = round_grad(terms, lax.ppermute(terms, "seq", swap), [done, tok_y, tok_z])
     grads = [grad] + [hop(grad, bits) for bits in near]
-    keep, send = weight_part([far_own, far_y, far_z, diagonal], grads, dp_size, [0, 0, 0, 0])
+    keep, send = weight_part([own, tok_y, tok_z, far_d], grads, dp_size, [0, 0, 0, 0])
     part = fold(keep, hop(send, CORE))
     far = hop(part, Z2)
-    near_own, near_y, near_z = slice_tokens(
-        flat, [(0, (False,)), (1, (False,)), (2, (False,))], "slice_near", []
-    )
-    near_y, near_z = hop(near_y, Y), hop(near_z, Z1)
-    keep, send = weight_part([near_own, near_y, near_z, diagonal], grads, dp_size, [0, 0, 0, 2])
+    (near_d,) = slice_tokens(flat, [(3, (False,))], "slice_near_diagonal")
+    near_d = hop(near_d, Y | Z1)
+    keep, send = weight_part([own, tok_y, tok_z, near_d], grads, dp_size, [2, 2, 2, 0])
     own = finish(fold(keep, far), hop(send, CORE))
-    z1, z2, y = hop(own, Z1), hop(own, Z2), hop(own, Y)
-    z12 = hop(z2, Z1)
-    zy = hop(stack([z1, z2], [y]), Y)
-    z12y = hop(z12, Y)
-    first = hop(stack([own, z1, z2, y]), CORE)
-    last = hop(stack([zy, z12, z12y]), CORE)
+    z1, y, d, z2 = hop(own, Z1), hop(own, Y), hop(own, Y | Z1), hop(own, Z2)
+    z21, z2y, z2d = hop(z2, Z1), hop(z2, Y), hop(z2, Y | Z1)
+    first = hop(stack([own, z1, y, d]), CORE)
+    last = hop(stack([z2, z21, z2y, z2d]), CORE)
     pieces = [
         (own, [0]),
         (z1, [Z1]),
+        (y, [Y]),
+        (d, [Y | Z1]),
         (z2, [Z2]),
-        (y, [Y]),
-        (zy, [Z1 | Y, Z2 | Y]),
-        (z12, [Z1 | Z2]),
-        (z12y, [Z1 | Z2 | Y]),
+        (z21, [Z2 | Z1]),
+        (z2y, [Z2 | Y]),
+        (z2d, [Z2 | Y | Z1]),
     ]
     held = [[bit | CORE for _, bits in part for bit in bits] for part in (pieces[:4], pieces[4:])]
     weight_grad = assemble(pieces + [(first, held[0])], dp_size)

time: 75.4 us -> 73.2 us (0.971)
  waiting for transfers between devices: 40.4 us -> 33.8 us
  starting transfers between devices: 22.8 us -> 27.3 us
    ppermute x19, waiting for transfers between devices: 33.3 us -> 29 us  [hop(): return lax.ppermute(value, 'dp', [(i, i ^ bits) for i in range(count)])]
    ppermute x19, starting transfers between devices: 19.2 us -> 22.5 us  [hop(): return lax.ppermute(value, 'dp', [(i, i ^ bits) for i in range(count)])]
    ppermute x1, waiting for transfers between devices: 4.63 us -> 2.01 us  [per_device_16x2(): lax.ppermute(terms, 'seq', swap)]
    ppermute x1, starting transfers between devices: 0.6 us -> 1.82 us  [per_device_16x2(): lax.ppermute(terms, 'seq', swap)]
  transfers between devices with their start and end apart: 21 -> 21, of which waited for: 15 -> 14; matrix products, arithmetic and copies ran while one was open for 0% -> 0% of each run, Pallas kernels for 8% -> 8%
where the time goes in v2:
time: 73.2 us; the launch traced here: 73 us
  waiting for transfers between devices  33.8 us (46%)
  starting transfers between devices  27.3 us (37%)
  Pallas kernels  7.95 us (11%)
  local copies, waits for them, and re-layouts  3.21 us (4%)
  between operations  0.84 us (1%)
    ppermute x19, waiting for transfers between devices, hop(): return lax.ppermute(value, 'dp', [(i, i ^ bits) for i in range(count)])  29 us
    ppermute x19, starting transfers between devices, hop(): return lax.ppermute(value, 'dp', [(i, i ^ bits) for i in range(count)])  22.5 us
    unnamed x14, local copies, waits for them, and re-layouts  3.21 us
    ppermute x1, starting transfers between devices, per_device_16x2(): other = lax.ppermute(partial, 'seq', swap)  3 us
    ppermute x1, waiting for transfers between devices, per_device_16x2(): other = lax.ppermute(partial, 'seq', swap)  2.7 us
    pallas_call x1, Pallas kernels, attend(): pl.pallas_call(functools.partial(terms_kernel, len(kvs), 'seq'), out_shap...  2.28 us
    pallas_call x2, Pallas kernels, assemble(): pl.pallas_call(functools.partial(assemble_kernel, held, rows), out_shape=...  2.08 us
    ppermute x1, waiting for transfers between devices, per_device_16x2(): lax.ppermute(terms, 'seq', swap)  2.01 us
  transfers between devices with their start and end apart: 21, of which 14 were waited for; matrix products, arithmetic and copies ran while one was open for 0% of the time, Pallas kernels for 8%

profile of v2, /device:TPU:0, one launch (start us, length us, event | category | flops | bytes accessed | tf_op | source)
XLA Modules:
  0.0 73.0 jit_solution(13405988189945976125)
XLA Ops:
  0.6 1.6 %copy-done = bf16[1,256,4096]{2,1,0:T(8,128)(2,1)S(1)} copy-done((bf16[1,256,4096]{2,1,0:T(8,128)(2,1)S(1)}, bf16[1,256,4096]{2,1,0:T(8,128)(2,1)}, u32[]{:S(2)}) %copy-start) | copy-done | bytes 2097176
  2.2 1.6 %copy-done.2 = bf16[4096,256]{1,0:T(8,128)(2,1)S(1)} copy-done((bf16[4096,256]{1,0:T(8,128)(2,1)S(1)}, bf16[4096,256]{1,0:T(8,128)(2,1)}, u32[]{:S(2)}) %copy-start.2) | copy-done | bytes 2097176
  3.8 0.7 project.1.refs_0_
  4.6 3.0 %collective-permute-start = (f32[256,256]{1,0:T(8,128)S(1)}, f32[256,256]{1,0:T(8,128)S(1)}, u32[]{:S(2)}, u32[]{:S(2)}) collective-permute-start(f32[256,256]{1,0:T(8,128)S(1)} %project.1.refs_0_), channel_id=1, source_target_pairs={{0,1},{1,0},{2,3},{3,2},{4,5},{5,4},{6,7},{7,6},{8,9},{9,8},{10,11... | collective-permute-start | bytes 786440 | tf_op jit(solution)/shard_map/ppermute | solution.py:335
  8.0 1.6 %collective-permute-start.1 = (bf16[256,1024]{1,0:T(8,128)(2,1)S(1)}, bf16[256,1024]{1,0:T(8,128)(2,1)S(1)}, u32[]{:S(2)}, u32[]{:S(2)}) collective-permute-start(bf16[256,1024]{1,0:T(8,128)(2,1)S(1)} %get-tuple-element.24), channel_id=1, source_target_pairs={{0,4},{2,6},{4,0},{6,2},{8,12},{10,14},{12,8},{14,10},{16,20},{18,... | collective-permute-start | bytes 1572872 | tf_op jit(solution)/shard_map/ppermute | solution.py:320
  9.6 1.6 %collective-permute-start.2 = (bf16[256,1024]{1,0:T(8,128)(2,1)S(1)}, bf16[256,1024]{1,0:T(8,128)(2,1)S(1)}, u32[]{:S(2)}, u32[]{:S(2)}) collective-permute-start(bf16[256,1024]{1,0:T(8,128)(2,1)S(1)} %get-tuple-element.25), channel_id=1, source_target_pairs={{0,8},{2,10},{4,12},{6,14},{8,0},{10,2},{12,4},{14,6},{16,24},{18,... | collective-permute-start | bytes 1572872 | tf_op jit(solution)/shard_map/ppermute | solution.py:320
  11.2 2.7 %collective-permute-done.refs_1_ = f32[256,256]{1,0:T(8,128)S(1)} collective-permute-done((f32[256,256]{1,0:T(8,128)S(1)}, f32[256,256]{1,0:T(8,128)S(1)}, u32[]{:S(2)}, u32[]{:S(2)}) %collective-permute-start) | collective-permute-done | bytes 262176 | tf_op jit(solution)/shard_map/ppermute | solution.py:335
  13.9 2.3 %attention_terms.1 = (bf16[256,256]{1,0:T(8,128)(2,1)S(1)}, bf16[256,1024]{1,0:T(8,128)(2,1)S(1)}, bf16[256,1024]{1,0:T(8,128)(2,1)S(1)}, f32[256,256]{1,0:T(8,128)S(1)}) custom-call(s32[2]{0:T(128)S(1)} %copy-done.6, s32[2,128]{1,0:T(2,128)S(1)} %bitcast.11, bf16[128,1024]{1,0:T(8,128)(2,1)S(1)} %bitcast.9, bf16[128,1024]{1,0:T(8,128)(2,1)S(1)} %bitcast.10, ...), custom_call_target="tpu_custom_call" | custom-call | tf_op jit(solution)/shard_map/attention_terms/pallas_call | solution.py:99
  16.2 1.8 %collective-permute-start.4 = (f32[256,256]{1,0:T(8,128)S(1)}, f32[256,256]{1,0:T(8,128)S(1)}, u32[]{:S(2)}, u32[]{:S(2)}) collective-permute-start(f32[256,256]{1,0:T(8,128)S(1)} %get-tuple-element.26.a_ref), channel_id=1, source_target_pairs={{0,1},{1,0},{2,3},{3,2},{4,5},{5,4},{6,7},{7,6},{8,9},{9,8},{10,11... | collective-permute-start | bytes 786440 | tf_op jit(solution)/shard_map/ppermute | solution.py:340
  18.0 2.5 %collective-permute-start.8 = (bf16[256,512]{1,0:T(8,128)(2,1)S(1)}, bf16[256,512]{1,0:T(8,128)(2,1)S(1)}, u32[]{:S(2)}, u32[]{:S(2)}) collective-permute-start(bf16[256,512]{1,0:T(8,128)(2,1)S(1)} %get-tuple-element.29), channel_id=1, source_target_pairs={{0,12},{2,14},{4,8},{6,10},{8,4},{10,6},{12,0},{14,2},{16,28},{18,... | collective-permute-start | bytes 786440 | tf_op jit(solution)/shard_map/ppermute | solution.py:320
  20.5 1.2 %attention_outputs.1 = (bf16[128,1024]{1,0:T(8,128)(2,1)}, bf16[128,1024]{1,0:T(8,128)(2,1)}, f32[8,128]{1,0:T(8,128)S(1)}) custom-call(bf16[256,256]{1,0:T(8,128)(2,1)S(1)} %get-tuple-element.18.kv_ref, bf16[256,1024]{1,0:T(8,128)(2,1)S(1)} %get-tuple-element.19.low_ref, bf16[256,1024]{1,0:T(8,128)(2,1)S(1)} %get-tuple-element.20.ds_ref), custom_call_target="tpu_custom_call" | custom-call | tf_op jit(solution)/shard_map/attention_outputs/pallas_call | solution.py:112
  21.7 2.0 %collective-permute-done.4.b_ref = f32[256,256]{1,0:T(8,128)S(1)} collective-permute-done((f32[256,256]{1,0:T(8,128)S(1)}, f32[256,256]{1,0:T(8,128)S(1)}, u32[]{:S(2)}, u32[]{:S(2)}) %collective-permute-start.4) | collective-permute-done | bytes 262176 | tf_op jit(solution)/shard_map/ppermute | solution.py:340
  23.8 0.7 collective-permute-done.2.refs_2_
  24.5 1.8 %collective-permute-start.7 = (bf16[256,256]{1,0:T(8,128)(2,1)S(1)}, bf16[256,256]{1,0:T(8,128)(2,1)S(1)}, u32[]{:S(2)}, u32[]{:S(2)}) collective-permute-start(bf16[256,256]{1,0:T(8,128)(2,1)S(1)} %round_grad.1.refs_4_), channel_id=1, source_target_pairs={{0,12},{2,14},{4,8},{6,10},{8,4},{10,6},{12,0},{14,2},{16,28},{18,... | collective-permute-start | bytes 393224 | tf_op jit(solution)/shard_map/ppermute | solution.py:320
  26.8 1.3 %collective-permute-start.5 = (bf16[256,256]{1,0:T(8,128)(2,1)S(1)}, bf16[256,256]{1,0:T(8,128)(2,1)S(1)}, u32[]{:S(2)}, u32[]{:S(2)}) collective-permute-start(bf16[256,256]{1,0:T(8,128)(2,1)S(1)} %round_grad.1.refs_4_), channel_id=1, source_target_pairs={{0,4},{2,6},{4,0},{6,2},{8,12},{10,14},{12,8},{14,10},{16,20},{18,... | collective-permute-start | bytes 393224 | tf_op jit(solution)/shard_map/ppermute | solution.py:320
  28.1 2.0 %collective-permute-done.8.refs_3_ = bf16[256,512]{1,0:T(8,128)(2,1)S(1)} collective-permute-done((bf16[256,512]{1,0:T(8,128)(2,1)S(1)}, bf16[256,512]{1,0:T(8,128)(2,1)S(1)}, u32[]{:S(2)}, u32[]{:S(2)}) %collective-permute-start.8) | collective-permute-done | bytes 262176 | tf_op jit(solution)/shard_map/ppermute | solution.py:320
  30.1 2.5 %collective-permute-done.7.refs_7_ = bf16[256,256]{1,0:T(8,128)(2,1)S(1)} collective-permute-done((bf16[256,256]{1,0:T(8,128)(2,1)S(1)}, bf16[256,256]{1,0:T(8,128)(2,1)S(1)}, u32[]{:S(2)}, u32[]{:S(2)}) %collective-permute-start.7) | collective-permute-done | bytes 131104 | tf_op jit(solution)/shard_map/ppermute | solution.py:320
  32.6 1.4 %collective-permute-done.6.refs_6_ = bf16[256,256]{1,0:T(8,128)(2,1)S(1)} collective-permute-done((bf16[256,256]{1,0:T(8,128)(2,1)S(1)}, bf16[256,256]{1,0:T(8,128)(2,1)S(1)}, u32[]{:S(2)}, u32[]{:S(2)}) %collective-permute-start.6) | collective-permute-done | bytes 131104 | tf_op jit(solution)/shard_map/ppermute | solution.py:320
  34.6 2.5 %collective-permute-start.3 = (bf16[256,512]{1,0:T(8,128)(2,1)S(1)}, bf16[256,512]{1,0:T(8,128)(2,1)S(1)}, u32[]{:S(2)}, u32[]{:S(2)}) collective-permute-start(bf16[256,512]{1,0:T(8,128)(2,1)S(1)} %slice_near_diagonal.1), channel_id=1, source_target_pairs={{0,12},{2,14},{4,8},{6,10},{8,4},{10,6},{12,0},{14,2},{16,28},{18,... | collective-permute-start | bytes 786440 | tf_op jit(solution)/shard_map/ppermute | solution.py:320
  37.2 2.7 %collective-permute-start.10 = (f32[256,256]{1,0:T(8,128)S(1)}, f32[256,256]{1,0:T(8,128)S(1)}, u32[]{:S(2)}, u32[]{:S(2)}) collective-permute-start(f32[256,256]{1,0:T(8,128)S(1)} %weight_fold.2), channel_id=1, source_target_pairs={{0,16},{2,18},{4,20},{6,22},{8,24},{10,26},{12,28},{14,30},{16,0},... | collective-permute-start | bytes 786440 | tf_op jit(solution)/shard_map/ppermute | solution.py:320
  39.8 9.8 %collective-permute-done.3.refs_3_ = bf16[256,512]{1,0:T(8,128)(2,1)S(1)} collective-permute-done((bf16[256,512]{1,0:T(8,128)(2,1)S(1)}, bf16[256,512]{1,0:T(8,128)(2,1)S(1)}, u32[]{:S(2)}, u32[]{:S(2)}) %collective-permute-start.3) | collective-permute-done | bytes 262176 | tf_op jit(solution)/shard_map/ppermute | solution.py:320
  50.2 2.0 %collective-permute-done.10.b_ref = f32[256,256]{1,0:T(8,128)S(1)} collective-permute-done((f32[256,256]{1,0:T(8,128)S(1)}, f32[256,256]{1,0:T(8,128)S(1)}, u32[]{:S(2)}, u32[]{:S(2)}) %collective-permute-start.10) | collective-permute-done | bytes 262176 | tf_op jit(solution)/shard_map/ppermute | solution.py:320
  52.6 3.7 %collective-permute-start.19 = (bf16[256,256]{1,0:T(8,128)(2,1)S(1)}, bf16[256,256]{1,0:T(8,128)(2,1)S(1)}, u32[]{:S(2)}, u32[]{:S(2)}) collective-permute-start(bf16[256,256]{1,0:T(8,128)(2,1)S(1)} %weight_finish.1.refs_0_), channel_id=1, source_target_pairs={{0,12},{2,14},{4,8},{6,10},{8,4},{10,6},{12,0},{14,2},{16,28},{18,... | collective-permute-start | bytes 393224 | tf_op jit(solution)/shard_map/ppermute | solution.py:320
  56.9 4.1 %collective-permute-done.12.refs_0_.refs_4_ = bf16[256,256]{1,0:T(8,128)(2,1)S(1)} collective-permute-done((bf16[256,256]{1,0:T(8,128)(2,1)S(1)}, bf16[256,256]{1,0:T(8,128)(2,1)S(1)}, u32[]{:S(2)}, u32[]{:S(2)}) %collective-permute-start.12) | collective-permute-done | bytes 131104 | tf_op jit(solution)/shard_map/ppermute | solution.py:320
  61.0 1.5 %collective-permute-start.14 = (bf16[256,256]{1,0:T(8,128)(2,1)S(1)}, bf16[256,256]{1,0:T(8,128)(2,1)S(1)}, u32[]{:S(2)}, u32[]{:S(2)}) collective-permute-start(bf16[256,256]{1,0:T(8,128)(2,1)S(1)} %collective-permute-done.12.refs_0_.refs_4_), channel_id=1, source_target_pairs={{0,4},{2,6},{4,0},{6,2},{8,12},{10,14},{12,8},{14,10},{16,20},{18,... | collective-permute-start | bytes 393224 | tf_op jit(solution)/shard_map/ppermute | solution.py:320
  62.8 1.7 %collective-permute-start.13 = (bf16[256,256]{1,0:T(8,128)(2,1)S(1)}, bf16[256,256]{1,0:T(8,128)(2,1)S(1)}, u32[]{:S(2)}, u32[]{:S(2)}) collective-permute-start(bf16[256,256]{1,0:T(8,128)(2,1)S(1)} %collective-permute-done.12.refs_0_.refs_4_), channel_id=1, source_target_pairs={{0,8},{2,10},{4,12},{6,14},{8,0},{10,2},{12,4},{14,6},{16,24},{18,... | collective-permute-start | bytes 393224 | tf_op jit(solution)/shard_map/ppermute | solution.py:320
  64.6 3.7 %collective-permute-done.15.refs_3_.refs_7_ = bf16[256,256]{1,0:T(8,128)(2,1)S(1)} collective-permute-done((bf16[256,256]{1,0:T(8,128)(2,1)S(1)}, bf16[256,256]{1,0:T(8,128)(2,1)S(1)}, u32[]{:S(2)}, u32[]{:S(2)}) %collective-permute-start.15) | collective-permute-done | bytes 131104 | tf_op jit(solution)/shard_map/ppermute | solution.py:320
  68.3 0.9 %collective-permute-done.14.refs_2_.refs_6_ = bf16[256,256]{1,0:T(8,128)(2,1)S(1)} collective-permute-done((bf16[256,256]{1,0:T(8,128)(2,1)S(1)}, bf16[256,256]{1,0:T(8,128)(2,1)S(1)}, u32[]{:S(2)}, u32[]{:S(2)}) %collective-permute-start.14) | collective-permute-done | bytes 131104 | tf_op jit(solution)/shard_map/ppermute | solution.py:320
  69.2 1.0 %collective-permute-done.13.refs_1_.refs_5_ = bf16[256,256]{1,0:T(8,128)(2,1)S(1)} collective-permute-done((bf16[256,256]{1,0:T(8,128)(2,1)S(1)}, bf16[256,256]{1,0:T(8,128)(2,1)S(1)}, u32[]{:S(2)}, u32[]{:S(2)}) %collective-permute-start.13) | collective-permute-done | bytes 131104 | tf_op jit(solution)/shard_map/ppermute | solution.py:320
  70.3 1.3 %weight_assemble.1.refs_1_ = bf16[4096,256]{1,0:T(8,128)(2,1)} custom-call(bf16[256,256]{1,0:T(8,128)(2,1)S(1)} %weight_finish.1.refs_0_, bf16[256,256]{1,0:T(8,128)(2,1)S(1)} %collective-permute-done.17.refs_1_, bf16[256,256]{1,0:T(8,128)(2,1)S(1)} %collective-permute-done.18.refs_2_, bf16[256,256]{1,0:T(8,128)(2,1)S(1)} %collective-permute-done.19.refs_3_, ...), custom_call_target="tpu_custom_call" | custom-call | tf_op jit(solution)/shard_map/weight_assemble/pallas_call | solution.py:306
  71.6 0.6 collective-permute-done.16.refs_0_
  72.2 0.8 %weight_complete.1 = bf16[4096,256]{1,0:T(8,128)(2,1)} custom-call(bf16[1024,256]{1,0:T(8,128)(2,1)S(1)} %collective-permute-done.16.refs_0_, bf16[4096,256]{1,0:T(8,128)(2,1)} %weight_assemble.1.refs_1_), custom_call_target="tpu_custom_call", output_to_operand_aliasing={{}: (1, {})} | custom-call | tf_op jit(solution)/shard_map/weight_complete/pallas_call | solution.py:306
  (39 shorter events, 3.7 us)
Async XLA Ops:
  0.6 1.6 %copy-start = (bf16[1,256,4096]{2,1,0:T(8,128)(2,1)S(1)}, bf16[1,256,4096]{2,1,0:T(8,128)(2,1)}, u32[]{:S(2)}) copy-start(bf16[1,256,4096]{2,1,0:T(8,128)(2,1)} %param.6) | copy-start | bytes 6291460
  2.2 1.6 %copy-start.2 = (bf16[4096,256]{1,0:T(8,128)(2,1)S(1)}, bf16[4096,256]{1,0:T(8,128)(2,1)}, u32[]{:S(2)}) copy-start(bf16[4096,256]{1,0:T(8,128)(2,1)} %w_ref.1) | copy-start | bytes 6291460
  4.5 9.4 %copy-start.3 = (bf16[1,128,1024]{2,1,0:T(8,128)(2,1)S(1)}, bf16[1,128,1024]{2,1,0:T(8,128)(2,1)}, u32[]{:S(2)}) copy-start(bf16[1,128,1024]{2,1,0:T(8,128)(2,1)} %param.7) | copy-start | bytes 786436
  4.5 9.4 %copy-start.4 = (bf16[1,128,1024]{2,1,0:T(8,128)(2,1)S(1)}, bf16[1,128,1024]{2,1,0:T(8,128)(2,1)}, u32[]{:S(2)}) copy-start(bf16[1,128,1024]{2,1,0:T(8,128)(2,1)} %param.8) | copy-start | bytes 786436
  4.6 9.3 %copy-start.5 = (s32[1,256]{1,0:T(1,128)S(1)}, s32[1,256]{1,0:T(1,128)}, u32[]{:S(2)}) copy-start(s32[1,256]{1,0:T(1,128)} %param.10) | copy-start | bytes 3076
  4.6 9.3 %copy-start.6 = (s32[2]{0:T(128)S(1)}, s32[2]{0:T(128)}, u32[]{:S(2)}) copy-start(s32[2]{0:T(128)} %order_ref.1) | copy-start | bytes 28
  4.6 9.3 %collective-permute-start = (f32[256,256]{1,0:T(8,128)S(1)}, f32[256,256]{1,0:T(8,128)S(1)}, u32[]{:S(2)}, u32[]{:S(2)}) collective-permute-start(f32[256,256]{1,0:T(8,128)S(1)} %project.1.refs_0_), channel_id=1, source_target_pairs={{0,1},{1,0},{2,3},{3,2},{4,5},{5,4},{6,7},{7,6},{8,9},{9,8},{10,11... | collective-permute-start | bytes 786440 | tf_op jit(solution)/shard_map/ppermute | solution.py:335
  8.0 15.7 %collective-permute-start.1 = (bf16[256,1024]{1,0:T(8,128)(2,1)S(1)}, bf16[256,1024]{1,0:T(8,128)(2,1)S(1)}, u32[]{:S(2)}, u32[]{:S(2)}) collective-permute-start(bf16[256,1024]{1,0:T(8,128)(2,1)S(1)} %get-tuple-element.24), channel_id=1, source_target_pairs={{0,4},{2,6},{4,0},{6,2},{8,12},{10,14},{12,8},{14,10},{16,20},{18,... | collective-permute-start | bytes 1572872 | tf_op jit(solution)/shard_map/ppermute | solution.py:320
  9.6 14.9 %collective-permute-start.2 = (bf16[256,1024]{1,0:T(8,128)(2,1)S(1)}, bf16[256,1024]{1,0:T(8,128)(2,1)S(1)}, u32[]{:S(2)}, u32[]{:S(2)}) collective-permute-start(bf16[256,1024]{1,0:T(8,128)(2,1)S(1)} %get-tuple-element.25), channel_id=1, source_target_pairs={{0,8},{2,10},{4,12},{6,14},{8,0},{10,2},{12,4},{14,6},{16,24},{18,... | collective-permute-start | bytes 1572872 | tf_op jit(solution)/shard_map/ppermute | solution.py:320
  16.2 7.6 %collective-permute-start.4 = (f32[256,256]{1,0:T(8,128)S(1)}, f32[256,256]{1,0:T(8,128)S(1)}, u32[]{:S(2)}, u32[]{:S(2)}) collective-permute-start(f32[256,256]{1,0:T(8,128)S(1)} %get-tuple-element.26.a_ref), channel_id=1, source_target_pairs={{0,1},{1,0},{2,3},{3,2},{4,5},{5,4},{6,7},{7,6},{8,9},{9,8},{10,11... | collective-permute-start | bytes 786440 | tf_op jit(solution)/shard_map/ppermute | solution.py:340
  18.0 12.1 %collective-permute-start.8 = (bf16[256,512]{1,0:T(8,128)(2,1)S(1)}, bf16[256,512]{1,0:T(8,128)(2,1)S(1)}, u32[]{:S(2)}, u32[]{:S(2)}) collective-permute-start(bf16[256,512]{1,0:T(8,128)(2,1)S(1)} %get-tuple-element.29), channel_id=1, source_target_pairs={{0,12},{2,14},{4,8},{6,10},{8,4},{10,6},{12,0},{14,2},{16,28},{18,... | collective-permute-start | bytes 786440 | tf_op jit(solution)/shard_map/ppermute | solution.py:320
  21.7 12.8 %copy-start.1 = (bf16[1,256,4096]{2,1,0:T(8,128)(2,1)S(1)}, bf16[1,256,4096]{2,1,0:T(8,128)(2,1)}, u32[]{:S(2)}) copy-start(bf16[1,256,4096]{2,1,0:T(8,128)(2,1)} %param.6) | copy-start | bytes 6291460
  24.5 8.1 %collective-permute-start.7 = (bf16[256,256]{1,0:T(8,128)(2,1)S(1)}, bf16[256,256]{1,0:T(8,128)(2,1)S(1)}, u32[]{:S(2)}, u32[]{:S(2)}) collective-permute-start(bf16[256,256]{1,0:T(8,128)(2,1)S(1)} %round_grad.1.refs_4_), channel_id=1, source_target_pairs={{0,12},{2,14},{4,8},{6,10},{8,4},{10,6},{12,0},{14,2},{16,28},{18,... | collective-permute-start | bytes 393224 | tf_op jit(solution)/shard_map/ppermute | solution.py:320
  26.3 7.7 %collective-permute-start.6 = (bf16[256,256]{1,0:T(8,128)(2,1)S(1)}, bf16[256,256]{1,0:T(8,128)(2,1)S(1)}, u32[]{:S(2)}, u32[]{:S(2)}) collective-permute-start(bf16[256,256]{1,0:T(8,128)(2,1)S(1)} %round_grad.1.refs_4_), channel_id=1, source_target_pairs={{0,8},{2,10},{4,12},{6,14},{8,0},{10,2},{12,4},{14,6},{16,24},{18,... | collective-permute-start | bytes 393224 | tf_op jit(solution)/shard_map/ppermute | solution.py:320
  26.8 7.2 %collective-permute-start.5 = (bf16[256,256]{1,0:T(8,128)(2,1)S(1)}, bf16[256,256]{1,0:T(8,128)(2,1)S(1)}, u32[]{:S(2)}, u32[]{:S(2)}) collective-permute-start(bf16[256,256]{1,0:T(8,128)(2,1)S(1)} %round_grad.1.refs_4_), channel_id=1, source_target_pairs={{0,4},{2,6},{4,0},{6,2},{8,12},{10,14},{12,8},{14,10},{16,20},{18,... | collective-permute-start | bytes 393224 | tf_op jit(solution)/shard_map/ppermute | solution.py:320
  34.4 2.7 %collective-permute-start.9 = (f32[256,256]{1,0:T(8,128)S(1)}, f32[256,256]{1,0:T(8,128)S(1)}, u32[]{:S(2)}, u32[]{:S(2)}) collective-permute-start(f32[256,256]{1,0:T(8,128)S(1)} %get-tuple-element.31), channel_id=1, source_target_pairs={{0,2},{2,0},{4,6},{6,4},{8,10},{10,8},{12,14},{14,12},{16,18},{18,... | collective-permute-start | bytes 786440 | tf_op jit(solution)/shard_map/ppermute | solution.py:320
  34.6 15.0 %collective-permute-start.3 = (bf16[256,512]{1,0:T(8,128)(2,1)S(1)}, bf16[256,512]{1,0:T(8,128)(2,1)S(1)}, u32[]{:S(2)}, u32[]{:S(2)}) collective-permute-start(bf16[256,512]{1,0:T(8,128)(2,1)S(1)} %slice_near_diagonal.1), channel_id=1, source_target_pairs={{0,12},{2,14},{4,8},{6,10},{8,4},{10,6},{12,0},{14,2},{16,28},{18,... | collective-permute-start | bytes 786440 | tf_op jit(solution)/shard_map/ppermute | solution.py:320
  37.2 15.0 %collective-permute-start.10 = (f32[256,256]{1,0:T(8,128)S(1)}, f32[256,256]{1,0:T(8,128)S(1)}, u32[]{:S(2)}, u32[]{:S(2)}) collective-permute-start(f32[256,256]{1,0:T(8,128)S(1)} %weight_fold.2), channel_id=1, source_target_pairs={{0,16},{2,18},{4,20},{6,22},{8,24},{10,26},{12,28},{14,30},{16,0},... | collective-permute-start | bytes 786440 | tf_op jit(solution)/shard_map/ppermute | solution.py:320
  50.1 2.1 %collective-permute-start.11 = (f32[256,256]{1,0:T(8,128)S(1)}, f32[256,256]{1,0:T(8,128)S(1)}, u32[]{:S(2)}, u32[]{:S(2)}) collective-permute-start(f32[256,256]{1,0:T(8,128)S(1)} %get-tuple-element.32), channel_id=1, source_target_pairs={{0,2},{2,0},{4,6},{6,4},{8,10},{10,8},{12,14},{14,12},{16,18},{18,... | collective-permute-start | bytes 786440 | tf_op jit(solution)/shard_map/ppermute | solution.py:320
  52.3 8.7 %collective-permute-start.12 = (bf16[256,256]{1,0:T(8,128)(2,1)S(1)}, bf16[256,256]{1,0:T(8,128)(2,1)S(1)}, u32[]{:S(2)}, u32[]{:S(2)}) collective-permute-start(bf16[256,256]{1,0:T(8,128)(2,1)S(1)} %weight_finish.1.refs_0_), channel_id=1, source_target_pairs={{0,16},{2,18},{4,20},{6,22},{8,24},{10,26},{12,28},{14,30},{16,0},... | collective-permute-start | bytes 393224 | tf_op jit(solution)/shard_map/ppermute | solution.py:320
  52.6 10.2 %collective-permute-start.19 = (bf16[256,256]{1,0:T(8,128)(2,1)S(1)}, bf16[256,256]{1,0:T(8,128)(2,1)S(1)}, u32[]{:S(2)}, u32[]{:S(2)}) collective-permute-start(bf16[256,256]{1,0:T(8,128)(2,1)S(1)} %weight_finish.1.refs_0_), channel_id=1, source_target_pairs={{0,12},{2,14},{4,8},{6,10},{8,4},{10,6},{12,0},{14,2},{16,28},{18,... | collective-permute-start | bytes 393224 | tf_op jit(solution)/shard_map/ppermute | solution.py:320
  56.3 8.2 %collective-permute-start.18 = (bf16[256,256]{1,0:T(8,128)(2,1)S(1)}, bf16[256,256]{1,0:T(8,128)(2,1)S(1)}, u32[]{:S(2)}, u32[]{:S(2)}) collective-permute-start(bf16[256,256]{1,0:T(8,128)(2,1)S(1)} %weight_finish.1.refs_0_), channel_id=1, source_target_pairs={{0,4},{2,6},{4,0},{6,2},{8,12},{10,14},{12,8},{14,10},{16,20},{18,... | collective-permute-start | bytes 393224 | tf_op jit(solution)/shard_map/ppermute | solution.py:320
  56.9 7.6 %collective-permute-start.17 = (bf16[256,256]{1,0:T(8,128)(2,1)S(1)}, bf16[256,256]{1,0:T(8,128)(2,1)S(1)}, u32[]{:S(2)}, u32[]{:S(2)}) collective-permute-start(bf16[256,256]{1,0:T(8,128)(2,1)S(1)} %weight_finish.1.refs_0_), channel_id=1, source_target_pairs={{0,8},{2,10},{4,12},{6,14},{8,0},{10,2},{12,4},{14,6},{16,24},{18,... | collective-permute-start | bytes 393224 | tf_op jit(solution)/shard_map/ppermute | solution.py:320
  61.0 7.3 %collective-permute-start.15 = (bf16[256,256]{1,0:T(8,128)(2,1)S(1)}, bf16[256,256]{1,0:T(8,128)(2,1)S(1)}, u32[]{:S(2)}, u32[]{:S(2)}) collective-permute-start(bf16[256,256]{1,0:T(8,128)(2,1)S(1)} %collective-permute-done.12.refs_0_.refs_4_), channel_id=1, source_target_pairs={{0,12},{2,14},{4,8},{6,10},{8,4},{10,6},{12,0},{14,2},{16,28},{18,... | collective-permute-start | bytes 393224 | tf_op jit(solution)/shard_map/ppermute | solution.py:320
  61.0 8.2 %collective-permute-start.14 = (bf16[256,256]{1,0:T(8,128)(2,1)S(1)}, bf16[256,256]{1,0:T(8,128)(2,1)S(1)}, u32[]{:S(2)}, u32[]{:S(2)}) collective-permute-start(bf16[256,256]{1,0:T(8,128)(2,1)S(1)} %collective-permute-done.12.refs_0_.refs_4_), channel_id=1, source_target_pairs={{0,4},{2,6},{4,0},{6,2},{8,12},{10,14},{12,8},{14,10},{16,20},{18,... | collective-permute-start | bytes 393224 | tf_op jit(solution)/shard_map/ppermute | solution.py:320
  62.8 7.4 %collective-permute-start.13 = (bf16[256,256]{1,0:T(8,128)(2,1)S(1)}, bf16[256,256]{1,0:T(8,128)(2,1)S(1)}, u32[]{:S(2)}, u32[]{:S(2)}) collective-permute-start(bf16[256,256]{1,0:T(8,128)(2,1)S(1)} %collective-permute-done.12.refs_0_.refs_4_), channel_id=1, source_target_pairs={{0,8},{2,10},{4,12},{6,14},{8,0},{10,2},{12,4},{14,6},{16,24},{18,... | collective-permute-start | bytes 393224 | tf_op jit(solution)/shard_map/ppermute | solution.py:320
  64.6 5.7 %collective-permute-start.20 = (bf16[1024,256]{1,0:T(8,128)(2,1)S(1)}, bf16[1024,256]{1,0:T(8,128)(2,1)S(1)}, u32[]{:S(2)}, u32[]{:S(2)}) collective-permute-start(bf16[1024,256]{1,0:T(8,128)(2,1)S(1)} %stack.3), channel_id=1, source_target_pairs={{0,2},{2,0},{4,6},{6,4},{8,10},{10,8},{12,14},{14,12},{16,18},{18,... | collective-permute-start | bytes 1572872 | tf_op jit(solution)/shard_map/ppermute | solution.py:320
  70.2 2.0 %collective-permute-start.16 = (bf16[1024,256]{1,0:T(8,128)(2,1)S(1)}, bf16[1024,256]{1,0:T(8,128)(2,1)S(1)}, u32[]{:S(2)}, u32[]{:S(2)}) collective-permute-start(bf16[1024,256]{1,0:T(8,128)(2,1)S(1)} %stack.2), channel_id=1, source_target_pairs={{0,2},{2,0},{4,6},{6,4},{8,10},{10,8},{12,14},{14,12},{16,18},{18,... | collective-permute-start | bytes 1572872 | tf_op jit(solution)/shard_map/ppermute | solution.py:320

commit v3 on v2

--- a/solution.py
+++ b/solution.py
@@ -199,8 +199,12 @@
 
 
 def weight_kernel(packs, starts, *refs):
-    toks, grads = refs[:BLOCK], refs[BLOCK : 2 * BLOCK]
-    keep_ref, send_ref = refs[2 * BLOCK :]
+    toks, grads_ref, (keep_ref, send_ref) = refs[:BLOCK], refs[BLOCK], refs[BLOCK + 1 :]
+    rows = grads_ref.shape[0] // BLOCK
+    mine = block_of(lax.axis_index("dp"))
+    grads = []
+    for k in range(BLOCK):
+        grads.append(grads_ref[pl.ds(pl.multiple_of((mine ^ k) * rows, rows), rows), :])
     width = keep_ref.shape[1]
     starts = [start * width for start in starts]
     core = lax.rem(lax.axis_index("dp"), CORES)
@@ -208,21 +212,21 @@
         acc = None
         for k in range(BLOCK):
             first = pl.multiple_of(starts[k] + which * width, width)
-            term = _mm(grads[k][...], toks[k][:, pl.ds(first, width)], NN)
+            term = _mm(grads[k], toks[k][:, pl.ds(first, width)], NN)
             acc = term if acc is None else acc + term
         ref[...] = acc * (1.0 / packs)
 
 
 def weight_part(toks, grads, packs, starts):
-    part = jax.ShapeDtypeStruct((grads[0].shape[0], toks[-1].shape[1] // CORES), F32)
+    part = jax.ShapeDtypeStruct((grads.shape[1], toks[-1].shape[1] // CORES), F32)
     return pl.pallas_call(
         functools.partial(weight_kernel, packs, starts),
         out_shape=[part, part],
-        in_specs=[VMEM] * (2 * BLOCK),
+        in_specs=[VMEM] * (BLOCK + 1),
         out_specs=[VMEM, VMEM],
         compiler_params=LIMIT,
         name="weight_part",
-    )(*toks, *grads)
+    )(*toks, grads)
 
 
 def fold_kernel(a_ref, b_ref, out_ref):
@@ -320,6 +324,32 @@
     return lax.ppermute(value, "dp", [(i, i ^ bits) for i in range(count)])
 
 
+def copies_kernel(in_ref, out_ref):
+    rows = in_ref.shape[0]
+    for k in range(BLOCK):
+        out_ref[k * rows : (k + 1) * rows, :] = in_ref[...]
+
+
+def spread(value):
+    copies = pl.pallas_call(
+        copies_kernel,
+        out_shape=jax.ShapeDtypeStruct((BLOCK * value.shape[0], value.shape[1]), value.dtype),
+        in_specs=[VMEM],
+        out_specs=VMEM,
+        compiler_params=LIMIT,
+        name="copies",
+    )(value)
+    count = lax.axis_size("dp")
+    groups = [
+        [high + block * CORES + core for block in range(BLOCK)]
+        for high in range(0, count, CORES * BLOCK)
+        for core in range(CORES)
+    ]
+    return lax.all_to_all(
+        copies, "dp", split_axis=0, concat_axis=0, axis_index_groups=groups, tiled=True
+    )
+
+
 def per_device_16x2(tokens, queries, grad_out, w_kv, doc_ids, span_order):
     dp_size = lax.axis_size("dp")
     rows_dev = queries.shape[1]
@@ -338,7 +368,7 @@
         span_order, docs, queries[0], grad_out[0], [partial, other]
     )
     grad = round_grad(terms, lax.ppermute(terms, "seq", swap), [done, tok_y, tok_z])
-    grads = [grad] + [hop(grad, bits) for bits in near]
+    grads = spread(grad)
     keep, send = weight_part([own, tok_y, tok_z, far_d], grads, dp_size, [0, 0, 0, 0])
     part = fold(keep, hop(send, CORE))
     far = hop(part, Z2)

time: 73.2 us -> 83.9 us (1.15)
  waiting for transfers between devices: 33.8 us -> 41.9 us
  local copies, waits for them, and re-layouts: 3.21 us -> 6.55 us
  starting transfers between devices: 27.3 us -> 24.2 us
  Pallas kernels: 7.95 us -> 10.1 us
    ppermute x19 -> x16, starting transfers between devices: 22.5 us -> 15.2 us  [hop(): return lax.ppermute(value, 'dp', [(i, i ^ bits) for i in range(count)])]
    ppermute x19 -> x16, waiting for transfers between devices: 29 us -> 36.1 us  [hop(): return lax.ppermute(value, 'dp', [(i, i ^ bits) for i in range(count)])]
    all_to_all x0 -> x1, starting transfers between devices: none -> 4.14 us  [spread(): lax.all_to_all(copies, 'dp', split_axis=0, concat_axis=0, axis_index_grou...]
    unnamed x14 -> x24, local copies, waits for them, and re-layouts: 3.21 us -> 6.55 us
    ppermute x1, waiting for transfers between devices: 2.01 us -> 4.54 us  [per_device_16x2(): lax.ppermute(terms, 'seq', swap)]
    pallas_call x2, Pallas kernels: 0.9 us -> 2.99 us  [weight_part(): pl.pallas_call(functools.partial(weight_kernel, packs, starts), out_shape...]
    ppermute x1, waiting for transfers between devices: 2.7 us -> 1.26 us  [per_device_16x2(): other = lax.ppermute(partial, 'seq', swap)]
  transfers between devices with their start and end apart: 21 -> 19, of which waited for: 14 -> 13; matrix products, arithmetic and copies ran while one was open for 0% -> 0% of each run, Pallas kernels for 8% -> 8%
where the time goes in v3:
time: 83.9 us; the launch traced here: 83.5 us
  waiting for transfers between devices  41.9 us (50%)
  starting transfers between devices  24.2 us (29%)
  Pallas kernels  10.1 us (12%)
  local copies, waits for them, and re-layouts  6.55 us (8%)
  between operations  0.9 us (1%)
    ppermute x16, waiting for transfers between devices, hop(): return lax.ppermute(value, 'dp', [(i, i ^ bits) for i in range(count)])  36.1 us
    ppermute x16, starting transfers between devices, hop(): return lax.ppermute(value, 'dp', [(i, i ^ bits) for i in range(count)])  15.2 us
    unnamed x24, local copies, waits for them, and re-layouts  6.55 us
    ppermute x1, waiting for transfers between devices, per_device_16x2(): lax.ppermute(terms, 'seq', swap)  4.54 us
    all_to_all x1, starting transfers between devices, spread(): lax.all_to_all(copies, 'dp', split_axis=0, concat_axis=0, axis_index_grou...  4.14 us
    ppermute x1, starting transfers between devices, per_device_16x2(): other = lax.ppermute(partial, 'seq', swap)  3 us
    pallas_call x2, Pallas kernels, weight_part(): pl.pallas_call(functools.partial(weight_kernel, packs, starts), out_shape...  2.99 us
    pallas_call x1, Pallas kernels, attend(): pl.pallas_call(functools.partial(terms_kernel, len(kvs), 'seq'), out_shap...  2.28 us
  transfers between devices with their start and end apart: 19, of which 13 were waited for; matrix products, arithmetic and copies ran while one was open for 0% of the time, Pallas kernels for 8%

profile of v3, /device:TPU:0, one launch (start us, length us, event | category | flops | bytes accessed | tf_op | source)
XLA Modules:
  0.0 83.5 jit_solution(7800785547293703219)
XLA Ops:
  0.6 1.6 %copy-done = bf16[1,256,4096]{2,1,0:T(8,128)(2,1)S(1)} copy-done((bf16[1,256,4096]{2,1,0:T(8,128)(2,1)S(1)}, bf16[1,256,4096]{2,1,0:T(8,128)(2,1)}, u32[]{:S(2)}) %copy-start) | copy-done | bytes 2097176
  2.2 1.6 %copy-done.3 = bf16[4096,256]{1,0:T(8,128)(2,1)S(1)} copy-done((bf16[4096,256]{1,0:T(8,128)(2,1)S(1)}, bf16[4096,256]{1,0:T(8,128)(2,1)}, u32[]{:S(2)}) %copy-start.3) | copy-done | bytes 2097176
  3.8 0.7 project.1.refs_0_
  4.6 3.0 %collective-permute-start = (f32[256,256]{1,0:T(8,128)S(1)}, f32[256,256]{1,0:T(8,128)S(1)}, u32[]{:S(2)}, u32[]{:S(2)}) collective-permute-start(f32[256,256]{1,0:T(8,128)S(1)} %project.1.refs_0_), channel_id=1, source_target_pairs={{0,1},{1,0},{2,3},{3,2},{4,5},{5,4},{6,7},{7,6},{8,9},{9,8},{10,11... | collective-permute-start | bytes 786440 | tf_op jit(solution)/shard_map/ppermute | solution.py:365
  8.0 0.8 copy-done.4
  9.5 1.5 %collective-permute-start.1 = (bf16[256,1024]{1,0:T(8,128)(2,1)S(1)}, bf16[256,1024]{1,0:T(8,128)(2,1)S(1)}, u32[]{:S(2)}, u32[]{:S(2)}) collective-permute-start(bf16[256,1024]{1,0:T(8,128)(2,1)S(1)} %get-tuple-element.24), channel_id=1, source_target_pairs={{0,4},{2,6},{4,0},{6,2},{8,12},{10,14},{12,8},{14,10},{16,20},{18,... | collective-permute-start | bytes 1572872 | tf_op jit(solution)/shard_map/ppermute | solution.py:324
  11.0 1.6 %collective-permute-start.2 = (bf16[256,1024]{1,0:T(8,128)(2,1)S(1)}, bf16[256,1024]{1,0:T(8,128)(2,1)S(1)}, u32[]{:S(2)}, u32[]{:S(2)}) collective-permute-start(bf16[256,1024]{1,0:T(8,128)(2,1)S(1)} %get-tuple-element.25), channel_id=1, source_target_pairs={{0,8},{2,10},{4,12},{6,14},{8,0},{10,2},{12,4},{14,6},{16,24},{18,... | collective-permute-start | bytes 1572872 | tf_op jit(solution)/shard_map/ppermute | solution.py:324
  12.6 1.3 %collective-permute-done.refs_1_ = f32[256,256]{1,0:T(8,128)S(1)} collective-permute-done((f32[256,256]{1,0:T(8,128)S(1)}, f32[256,256]{1,0:T(8,128)S(1)}, u32[]{:S(2)}, u32[]{:S(2)}) %collective-permute-start) | collective-permute-done | bytes 262176 | tf_op jit(solution)/shard_map/ppermute | solution.py:365
  13.9 2.3 %attention_terms.1 = (bf16[256,256]{1,0:T(8,128)(2,1)S(1)}, bf16[256,1024]{1,0:T(8,128)(2,1)S(1)}, bf16[256,1024]{1,0:T(8,128)(2,1)S(1)}, f32[256,256]{1,0:T(8,128)S(1)}) custom-call(s32[2]{0:T(128)S(1)} %copy-done.10, s32[2,128]{1,0:T(2,128)S(1)} %bitcast.14, bf16[128,1024]{1,0:T(8,128)(2,1)S(1)} %bitcast.12, bf16[128,1024]{1,0:T(8,128)(2,1)S(1)} %bitcast.13, ...), custom_call_target="tpu_custom_call" | custom-call | tf_op jit(solution)/shard_map/attention_terms/pallas_call | solution.py:99
  16.2 1.8 %collective-permute-start.4 = (f32[256,256]{1,0:T(8,128)S(1)}, f32[256,256]{1,0:T(8,128)S(1)}, u32[]{:S(2)}, u32[]{:S(2)}) collective-permute-start(f32[256,256]{1,0:T(8,128)S(1)} %get-tuple-element.26.a_ref), channel_id=1, source_target_pairs={{0,1},{1,0},{2,3},{3,2},{4,5},{5,4},{6,7},{7,6},{8,9},{9,8},{10,11... | collective-permute-start | bytes 786440 | tf_op jit(solution)/shard_map/ppermute | solution.py:370
  18.0 1.2 %attention_outputs.1 = (bf16[128,1024]{1,0:T(8,128)(2,1)}, bf16[128,1024]{1,0:T(8,128)(2,1)}, f32[8,128]{1,0:T(8,128)S(1)}) custom-call(bf16[256,256]{1,0:T(8,128)(2,1)S(1)} %get-tuple-element.18.kv_ref, bf16[256,1024]{1,0:T(8,128)(2,1)S(1)} %get-tuple-element.19.low_ref, bf16[256,1024]{1,0:T(8,128)(2,1)S(1)} %get-tuple-element.20.ds_ref), custom_call_target="tpu_custom_call" | custom-call | tf_op jit(solution)/shard_map/attention_outputs/pallas_call | solution.py:112
  19.2 4.5 %collective-permute-done.4.b_ref = f32[256,256]{1,0:T(8,128)S(1)} collective-permute-done((f32[256,256]{1,0:T(8,128)S(1)}, f32[256,256]{1,0:T(8,128)S(1)}, u32[]{:S(2)}, u32[]{:S(2)}) %collective-permute-start.4) | collective-permute-done | bytes 262176 | tf_op jit(solution)/shard_map/ppermute | solution.py:370
  24.2 0.8 copy-done.2
  25.0 4.1 %all-to-all-start = ((bf16[4,256,256]{2,1,0:T(8,128)(2,1)}), bf16[4,256,256]{2,1,0:T(8,128)(2,1)}, u32[]{:S(2)}, u32[]{:S(2)}) async-start(bf16[4,256,256]{2,1,0:T(8,128)(2,1)} %bitcast.11), calls=%async_computation | async-start | bytes 1048576 | tf_op jit(solution)/shard_map/all_to_all | solution.py:348
  29.2 2.9 %collective-permute-start.5 = (bf16[256,512]{1,0:T(8,128)(2,1)}, bf16[256,512]{1,0:T(8,128)(2,1)S(1)}, u32[]{:S(2)}, u32[]{:S(2)}) collective-permute-start(bf16[256,512]{1,0:T(8,128)(2,1)} %copy-done.11), channel_id=1, source_target_pairs={{0,12},{2,14},{4,8},{6,10},{8,4},{10,6},{12,0},{14,2},{16,28},{18,... | collective-permute-start | bytes 786440 | tf_op jit(solution)/shard_map/ppermute | solution.py:324
  32.1 10.5 %collective-permute-done.5.refs_3_ = bf16[256,512]{1,0:T(8,128)(2,1)S(1)} collective-permute-done((bf16[256,512]{1,0:T(8,128)(2,1)}, bf16[256,512]{1,0:T(8,128)(2,1)S(1)}, u32[]{:S(2)}, u32[]{:S(2)}) %collective-permute-start.5) | collective-permute-done | bytes 262176 | tf_op jit(solution)/shard_map/ppermute | solution.py:324
  42.5 1.0 %copy-done.5 = bf16[256,1024]{1,0:T(8,128)(2,1)S(1)} copy-done((bf16[256,1024]{1,0:T(8,128)(2,1)S(1)}, bf16[256,1024]{1,0:T(8,128)(2,1)}, u32[]{:S(2)}) %copy-start.5) | copy-done | bytes 524312
  43.6 1.5 %weight_part.3 = (f32[256,256]{1,0:T(8,128)S(1)}, f32[256,256]{1,0:T(8,128)S(1)}) custom-call(bf16[256,1024]{1,0:T(8,128)(2,1)S(1)} %copy-done.5, bf16[256,1024]{1,0:T(8,128)(2,1)S(1)} %collective-permute-done.1.refs_1_, bf16[256,1024]{1,0:T(8,128)(2,1)S(1)} %collective-permute-done.2.refs_2_, bf16[256,512]{1,0:T(8,128)(2,1)S(1)} %collective-permute-done.5.refs_3_, ...), custom_call_target="tpu_custom_call" | custom-call | tf_op jit(solution)/shard_map/weight_part/pallas_call | solution.py:222
  45.6 1.1 %collective-permute-done.6.b_ref = f32[256,256]{1,0:T(8,128)S(1)} collective-permute-done((f32[256,256]{1,0:T(8,128)S(1)}, f32[256,256]{1,0:T(8,128)S(1)}, u32[]{:S(2)}, u32[]{:S(2)}) %collective-permute-start.6) | collective-permute-done | bytes 262176 | tf_op jit(solution)/shard_map/ppermute | solution.py:324
  46.7 2.7 %collective-permute-start.7 = (f32[256,256]{1,0:T(8,128)S(1)}, f32[256,256]{1,0:T(8,128)S(1)}, u32[]{:S(2)}, u32[]{:S(2)}) collective-permute-start(f32[256,256]{1,0:T(8,128)S(1)} %weight_fold.2), channel_id=1, source_target_pairs={{0,16},{2,18},{4,20},{6,22},{8,24},{10,26},{12,28},{14,30},{16,0},... | collective-permute-start | bytes 786440 | tf_op jit(solution)/shard_map/ppermute | solution.py:324
  49.4 11.2 %collective-permute-done.3.refs_3_ = bf16[256,512]{1,0:T(8,128)(2,1)S(1)} collective-permute-done((bf16[256,512]{1,0:T(8,128)(2,1)S(1)}, bf16[256,512]{1,0:T(8,128)(2,1)S(1)}, u32[]{:S(2)}, u32[]{:S(2)}) %collective-permute-start.3) | collective-permute-done | bytes 262176 | tf_op jit(solution)/shard_map/ppermute | solution.py:324
  60.5 1.5 %weight_part.2 = (f32[256,256]{1,0:T(8,128)S(1)}, f32[256,256]{1,0:T(8,128)S(1)}) custom-call(bf16[256,1024]{1,0:T(8,128)(2,1)S(1)} %copy-done.6, bf16[256,1024]{1,0:T(8,128)(2,1)S(1)} %collective-permute-done.1.refs_1_, bf16[256,1024]{1,0:T(8,128)(2,1)S(1)} %collective-permute-done.2.refs_2_, bf16[256,512]{1,0:T(8,128)(2,1)S(1)} %collective-permute-done.3.refs_3_, ...), custom_call_target="tpu_custom_call" | custom-call | tf_op jit(solution)/shard_map/weight_part/pallas_call | solution.py:222
  62.2 1.5 %collective-permute-done.8.b_ref = f32[256,256]{1,0:T(8,128)S(1)} collective-permute-done((f32[256,256]{1,0:T(8,128)S(1)}, f32[256,256]{1,0:T(8,128)S(1)}, u32[]{:S(2)}, u32[]{:S(2)}) %collective-permute-start.8) | collective-permute-done | bytes 262176 | tf_op jit(solution)/shard_map/ppermute | solution.py:324
  63.8 2.3 %collective-permute-start.16 = (bf16[256,256]{1,0:T(8,128)(2,1)S(1)}, bf16[256,256]{1,0:T(8,128)(2,1)S(1)}, u32[]{:S(2)}, u32[]{:S(2)}) collective-permute-start(bf16[256,256]{1,0:T(8,128)(2,1)S(1)} %weight_finish.1.refs_0_), channel_id=1, source_target_pairs={{0,12},{2,14},{4,8},{6,10},{8,4},{10,6},{12,0},{14,2},{16,28},{18,... | collective-permute-start | bytes 393224 | tf_op jit(solution)/shard_map/ppermute | solution.py:324
  67.4 3.9 %collective-permute-done.9.refs_0_.refs_4_ = bf16[256,256]{1,0:T(8,128)(2,1)S(1)} collective-permute-done((bf16[256,256]{1,0:T(8,128)(2,1)S(1)}, bf16[256,256]{1,0:T(8,128)(2,1)S(1)}, u32[]{:S(2)}, u32[]{:S(2)}) %collective-permute-start.9) | collective-permute-done | bytes 131104 | tf_op jit(solution)/shard_map/ppermute | solution.py:324
  71.3 1.4 %collective-permute-start.11 = (bf16[256,256]{1,0:T(8,128)(2,1)S(1)}, bf16[256,256]{1,0:T(8,128)(2,1)S(1)}, u32[]{:S(2)}, u32[]{:S(2)}) collective-permute-start(bf16[256,256]{1,0:T(8,128)(2,1)S(1)} %collective-permute-done.9.refs_0_.refs_4_), channel_id=1, source_target_pairs={{0,4},{2,6},{4,0},{6,2},{8,12},{10,14},{12,8},{14,10},{16,20},{18,... | collective-permute-start | bytes 393224 | tf_op jit(solution)/shard_map/ppermute | solution.py:324
  72.7 1.1 %collective-permute-done.16.refs_3_ = bf16[256,256]{1,0:T(8,128)(2,1)S(1)} collective-permute-done((bf16[256,256]{1,0:T(8,128)(2,1)S(1)}, bf16[256,256]{1,0:T(8,128)(2,1)S(1)}, u32[]{:S(2)}, u32[]{:S(2)}) %collective-permute-start.16) | collective-permute-done | bytes 131104 | tf_op jit(solution)/shard_map/ppermute | solution.py:324
  73.8 0.9 %collective-permute-start.10 = (bf16[256,256]{1,0:T(8,128)(2,1)S(1)}, bf16[256,256]{1,0:T(8,128)(2,1)S(1)}, u32[]{:S(2)}, u32[]{:S(2)}) collective-permute-start(bf16[256,256]{1,0:T(8,128)(2,1)S(1)} %collective-permute-done.9.refs_0_.refs_4_), channel_id=1, source_target_pairs={{0,8},{2,10},{4,12},{6,14},{8,0},{10,2},{12,4},{14,6},{16,24},{18,... | collective-permute-start | bytes 393224 | tf_op jit(solution)/shard_map/ppermute | solution.py:324
  75.4 4.1 %collective-permute-done.12.refs_3_.refs_7_ = bf16[256,256]{1,0:T(8,128)(2,1)S(1)} collective-permute-done((bf16[256,256]{1,0:T(8,128)(2,1)S(1)}, bf16[256,256]{1,0:T(8,128)(2,1)S(1)}, u32[]{:S(2)}, u32[]{:S(2)}) %collective-permute-start.12) | collective-permute-done | bytes 131104 | tf_op jit(solution)/shard_map/ppermute | solution.py:324
  79.5 1.2 %collective-permute-done.10.refs_1_.refs_5_ = bf16[256,256]{1,0:T(8,128)(2,1)S(1)} collective-permute-done((bf16[256,256]{1,0:T(8,128)(2,1)S(1)}, bf16[256,256]{1,0:T(8,128)(2,1)S(1)}, u32[]{:S(2)}, u32[]{:S(2)}) %collective-permute-start.10) | collective-permute-done | bytes 131104 | tf_op jit(solution)/shard_map/ppermute | solution.py:324
  80.8 1.3 %weight_assemble.1.refs_1_ = bf16[4096,256]{1,0:T(8,128)(2,1)} custom-call(bf16[256,256]{1,0:T(8,128)(2,1)S(1)} %weight_finish.1.refs_0_, bf16[256,256]{1,0:T(8,128)(2,1)S(1)} %collective-permute-done.14.refs_1_, bf16[256,256]{1,0:T(8,128)(2,1)S(1)} %collective-permute-done.15.refs_2_, bf16[256,256]{1,0:T(8,128)(2,1)S(1)} %collective-permute-done.16.refs_3_, ...), custom_call_target="tpu_custom_call" | custom-call | tf_op jit(solution)/shard_map/weight_assemble/pallas_call | solution.py:310
  82.7 0.8 weight_complete.1
  (46 shorter events, 5.2 us)
Async XLA Ops:
  0.6 1.6 %copy-start = (bf16[1,256,4096]{2,1,0:T(8,128)(2,1)S(1)}, bf16[1,256,4096]{2,1,0:T(8,128)(2,1)}, u32[]{:S(2)}) copy-start(bf16[1,256,4096]{2,1,0:T(8,128)(2,1)} %param.6) | copy-start | bytes 6291460
  2.2 1.6 %copy-start.3 = (bf16[4096,256]{1,0:T(8,128)(2,1)S(1)}, bf16[4096,256]{1,0:T(8,128)(2,1)}, u32[]{:S(2)}) copy-start(bf16[4096,256]{1,0:T(8,128)(2,1)} %w_ref.1) | copy-start | bytes 6291460
  4.5 9.4 %copy-start.7 = (bf16[1,128,1024]{2,1,0:T(8,128)(2,1)S(1)}, bf16[1,128,1024]{2,1,0:T(8,128)(2,1)}, u32[]{:S(2)}) copy-start(bf16[1,128,1024]{2,1,0:T(8,128)(2,1)} %param.7) | copy-start | bytes 786436
  4.5 9.4 %copy-start.8 = (bf16[1,128,1024]{2,1,0:T(8,128)(2,1)S(1)}, bf16[1,128,1024]{2,1,0:T(8,128)(2,1)}, u32[]{:S(2)}) copy-start(bf16[1,128,1024]{2,1,0:T(8,128)(2,1)} %param.8) | copy-start | bytes 786436
  4.6 9.3 %copy-start.9 = (s32[1,256]{1,0:T(1,128)S(1)}, s32[1,256]{1,0:T(1,128)}, u32[]{:S(2)}) copy-start(s32[1,256]{1,0:T(1,128)} %param.10) | copy-start | bytes 3076
  4.6 9.3 %copy-start.10 = (s32[2]{0:T(128)S(1)}, s32[2]{0:T(128)}, u32[]{:S(2)}) copy-start(s32[2]{0:T(128)} %order_ref.1) | copy-start | bytes 28
  4.6 9.3 %collective-permute-start = (f32[256,256]{1,0:T(8,128)S(1)}, f32[256,256]{1,0:T(8,128)S(1)}, u32[]{:S(2)}, u32[]{:S(2)}) collective-permute-start(f32[256,256]{1,0:T(8,128)S(1)} %project.1.refs_0_), channel_id=1, source_target_pairs={{0,1},{1,0},{2,3},{3,2},{4,5},{5,4},{6,7},{7,6},{8,9},{9,8},{10,11... | collective-permute-start | bytes 786440 | tf_op jit(solution)/shard_map/ppermute | solution.py:365
  8.0 0.8 copy-start.4
  8.8 0.7 copy-start.11
  9.5 14.2 %collective-permute-start.1 = (bf16[256,1024]{1,0:T(8,128)(2,1)S(1)}, bf16[256,1024]{1,0:T(8,128)(2,1)S(1)}, u32[]{:S(2)}, u32[]{:S(2)}) collective-permute-start(bf16[256,1024]{1,0:T(8,128)(2,1)S(1)} %get-tuple-element.24), channel_id=1, source_target_pairs={{0,4},{2,6},{4,0},{6,2},{8,12},{10,14},{12,8},{14,10},{16,20},{18,... | collective-permute-start | bytes 1572872 | tf_op jit(solution)/shard_map/ppermute | solution.py:324
  11.0 13.1 %collective-permute-start.2 = (bf16[256,1024]{1,0:T(8,128)(2,1)S(1)}, bf16[256,1024]{1,0:T(8,128)(2,1)S(1)}, u32[]{:S(2)}, u32[]{:S(2)}) collective-permute-start(bf16[256,1024]{1,0:T(8,128)(2,1)S(1)} %get-tuple-element.25), channel_id=1, source_target_pairs={{0,8},{2,10},{4,12},{6,14},{8,0},{10,2},{12,4},{14,6},{16,24},{18,... | collective-permute-start | bytes 1572872 | tf_op jit(solution)/shard_map/ppermute | solution.py:324
  16.2 7.6 %collective-permute-start.4 = (f32[256,256]{1,0:T(8,128)S(1)}, f32[256,256]{1,0:T(8,128)S(1)}, u32[]{:S(2)}, u32[]{:S(2)}) collective-permute-start(f32[256,256]{1,0:T(8,128)S(1)} %get-tuple-element.26.a_ref), channel_id=1, source_target_pairs={{0,1},{1,0},{2,3},{3,2},{4,5},{5,4},{6,7},{7,6},{8,9},{9,8},{10,11... | collective-permute-start | bytes 786440 | tf_op jit(solution)/shard_map/ppermute | solution.py:370
  24.2 21.0 %copy-start.1 = (bf16[1,256,4096]{2,1,0:T(8,128)(2,1)S(1)}, bf16[1,256,4096]{2,1,0:T(8,128)(2,1)}, u32[]{:S(2)}) copy-start(bf16[1,256,4096]{2,1,0:T(8,128)(2,1)} %param.6) | copy-start | bytes 6291460
  24.2 0.8 copy-start.2
  25.0 17.5 %all-to-all-start = ((bf16[4,256,256]{2,1,0:T(8,128)(2,1)}), bf16[4,256,256]{2,1,0:T(8,128)(2,1)}, u32[]{:S(2)}, u32[]{:S(2)}) async-start(bf16[4,256,256]{2,1,0:T(8,128)(2,1)} %bitcast.11), calls=%async_computation | async-start | bytes 1048576 | tf_op jit(solution)/shard_map/all_to_all | solution.py:348
  29.2 13.3 %collective-permute-start.5 = (bf16[256,512]{1,0:T(8,128)(2,1)}, bf16[256,512]{1,0:T(8,128)(2,1)S(1)}, u32[]{:S(2)}, u32[]{:S(2)}) collective-permute-start(bf16[256,512]{1,0:T(8,128)(2,1)} %copy-done.11), channel_id=1, source_target_pairs={{0,12},{2,14},{4,8},{6,10},{8,4},{10,6},{12,0},{14,2},{16,28},{18,... | collective-permute-start | bytes 786440 | tf_op jit(solution)/shard_map/ppermute | solution.py:324
  42.5 1.0 %copy-start.5 = (bf16[256,1024]{1,0:T(8,128)(2,1)S(1)}, bf16[256,1024]{1,0:T(8,128)(2,1)}, u32[]{:S(2)}) copy-start(bf16[256,1024]{1,0:T(8,128)(2,1)} %copy-done.4) | copy-start | bytes 1572868
  45.1 15.5 %copy-start.6 = (bf16[256,1024]{1,0:T(8,128)(2,1)S(1)}, bf16[256,1024]{1,0:T(8,128)(2,1)}, u32[]{:S(2)}) copy-start(bf16[256,1024]{1,0:T(8,128)(2,1)} %copy-done.4) | copy-start | bytes 1572868
  45.1 1.6 %collective-permute-start.6 = (f32[256,256]{1,0:T(8,128)S(1)}, f32[256,256]{1,0:T(8,128)S(1)}, u32[]{:S(2)}, u32[]{:S(2)}) collective-permute-start(f32[256,256]{1,0:T(8,128)S(1)} %get-tuple-element.31), channel_id=1, source_target_pairs={{0,2},{2,0},{4,6},{6,4},{8,10},{10,8},{12,14},{14,12},{16,18},{18,... | collective-permute-start | bytes 786440 | tf_op jit(solution)/shard_map/ppermute | solution.py:324
  45.3 15.3 %collective-permute-start.3 = (bf16[256,512]{1,0:T(8,128)(2,1)S(1)}, bf16[256,512]{1,0:T(8,128)(2,1)S(1)}, u32[]{:S(2)}, u32[]{:S(2)}) collective-permute-start(bf16[256,512]{1,0:T(8,128)(2,1)S(1)} %slice_near_diagonal.1), channel_id=1, source_target_pairs={{0,12},{2,14},{4,8},{6,10},{8,4},{10,6},{12,0},{14,2},{16,28},{18,... | collective-permute-start | bytes 786440 | tf_op jit(solution)/shard_map/ppermute | solution.py:324
  46.7 15.4 %collective-permute-start.7 = (f32[256,256]{1,0:T(8,128)S(1)}, f32[256,256]{1,0:T(8,128)S(1)}, u32[]{:S(2)}, u32[]{:S(2)}) collective-permute-start(f32[256,256]{1,0:T(8,128)S(1)} %weight_fold.2), channel_id=1, source_target_pairs={{0,16},{2,18},{4,20},{6,22},{8,24},{10,26},{12,28},{14,30},{16,0},... | collective-permute-start | bytes 786440 | tf_op jit(solution)/shard_map/ppermute | solution.py:324
  62.0 1.6 %collective-permute-start.8 = (f32[256,256]{1,0:T(8,128)S(1)}, f32[256,256]{1,0:T(8,128)S(1)}, u32[]{:S(2)}, u32[]{:S(2)}) collective-permute-start(f32[256,256]{1,0:T(8,128)S(1)} %get-tuple-element.32), channel_id=1, source_target_pairs={{0,2},{2,0},{4,6},{6,4},{8,10},{10,8},{12,14},{14,12},{16,18},{18,... | collective-permute-start | bytes 786440 | tf_op jit(solution)/shard_map/ppermute | solution.py:324
  63.7 7.5 %collective-permute-start.9 = (bf16[256,256]{1,0:T(8,128)(2,1)S(1)}, bf16[256,256]{1,0:T(8,128)(2,1)S(1)}, u32[]{:S(2)}, u32[]{:S(2)}) collective-permute-start(bf16[256,256]{1,0:T(8,128)(2,1)S(1)} %weight_finish.1.refs_0_), channel_id=1, source_target_pairs={{0,16},{2,18},{4,20},{6,22},{8,24},{10,26},{12,28},{14,30},{16,0},... | collective-permute-start | bytes 393224 | tf_op jit(solution)/shard_map/ppermute | solution.py:324
  63.8 10.0 %collective-permute-start.16 = (bf16[256,256]{1,0:T(8,128)(2,1)S(1)}, bf16[256,256]{1,0:T(8,128)(2,1)S(1)}, u32[]{:S(2)}, u32[]{:S(2)}) collective-permute-start(bf16[256,256]{1,0:T(8,128)(2,1)S(1)} %weight_finish.1.refs_0_), channel_id=1, source_target_pairs={{0,12},{2,14},{4,8},{6,10},{8,4},{10,6},{12,0},{14,2},{16,28},{18,... | collective-permute-start | bytes 393224 | tf_op jit(solution)/shard_map/ppermute | solution.py:324
  66.1 8.6 %collective-permute-start.15 = (bf16[256,256]{1,0:T(8,128)(2,1)S(1)}, bf16[256,256]{1,0:T(8,128)(2,1)S(1)}, u32[]{:S(2)}, u32[]{:S(2)}) collective-permute-start(bf16[256,256]{1,0:T(8,128)(2,1)S(1)} %weight_finish.1.refs_0_), channel_id=1, source_target_pairs={{0,4},{2,6},{4,0},{6,2},{8,12},{10,14},{12,8},{14,10},{16,20},{18,... | collective-permute-start | bytes 393224 | tf_op jit(solution)/shard_map/ppermute | solution.py:324
  66.7 8.6 %collective-permute-start.14 = (bf16[256,256]{1,0:T(8,128)(2,1)S(1)}, bf16[256,256]{1,0:T(8,128)(2,1)S(1)}, u32[]{:S(2)}, u32[]{:S(2)}) collective-permute-start(bf16[256,256]{1,0:T(8,128)(2,1)S(1)} %weight_finish.1.refs_0_), channel_id=1, source_target_pairs={{0,8},{2,10},{4,12},{6,14},{8,0},{10,2},{12,4},{14,6},{16,24},{18,... | collective-permute-start | bytes 393224 | tf_op jit(solution)/shard_map/ppermute | solution.py:324
  71.2 8.3 %collective-permute-start.12 = (bf16[256,256]{1,0:T(8,128)(2,1)S(1)}, bf16[256,256]{1,0:T(8,128)(2,1)S(1)}, u32[]{:S(2)}, u32[]{:S(2)}) collective-permute-start(bf16[256,256]{1,0:T(8,128)(2,1)S(1)} %collective-permute-done.9.refs_0_.refs_4_), channel_id=1, source_target_pairs={{0,12},{2,14},{4,8},{6,10},{8,4},{10,6},{12,0},{14,2},{16,28},{18,... | collective-permute-start | bytes 393224 | tf_op jit(solution)/shard_map/ppermute | solution.py:324
  71.3 8.3 %collective-permute-start.11 = (bf16[256,256]{1,0:T(8,128)(2,1)S(1)}, bf16[256,256]{1,0:T(8,128)(2,1)S(1)}, u32[]{:S(2)}, u32[]{:S(2)}) collective-permute-start(bf16[256,256]{1,0:T(8,128)(2,1)S(1)} %collective-permute-done.9.refs_0_.refs_4_), channel_id=1, source_target_pairs={{0,4},{2,6},{4,0},{6,2},{8,12},{10,14},{12,8},{14,10},{16,20},{18,... | collective-permute-start | bytes 393224 | tf_op jit(solution)/shard_map/ppermute | solution.py:324
  73.8 6.9 %collective-permute-start.10 = (bf16[256,256]{1,0:T(8,128)(2,1)S(1)}, bf16[256,256]{1,0:T(8,128)(2,1)S(1)}, u32[]{:S(2)}, u32[]{:S(2)}) collective-permute-start(bf16[256,256]{1,0:T(8,128)(2,1)S(1)} %collective-permute-done.9.refs_0_.refs_4_), channel_id=1, source_target_pairs={{0,8},{2,10},{4,12},{6,14},{8,0},{10,2},{12,4},{14,6},{16,24},{18,... | collective-permute-start | bytes 393224 | tf_op jit(solution)/shard_map/ppermute | solution.py:324
  75.4 5.5 %collective-permute-start.17 = (bf16[1024,256]{1,0:T(8,128)(2,1)S(1)}, bf16[1024,256]{1,0:T(8,128)(2,1)S(1)}, u32[]{:S(2)}, u32[]{:S(2)}) collective-permute-start(bf16[1024,256]{1,0:T(8,128)(2,1)S(1)} %stack.3), channel_id=1, source_target_pairs={{0,2},{2,0},{4,6},{6,4},{8,10},{10,8},{12,14},{14,12},{16,18},{18,... | collective-permute-start | bytes 1572872 | tf_op jit(solution)/shard_map/ppermute | solution.py:324
  80.8 2.0 %collective-permute-start.13 = (bf16[1024,256]{1,0:T(8,128)(2,1)S(1)}, bf16[1024,256]{1,0:T(8,128)(2,1)S(1)}, u32[]{:S(2)}, u32[]{:S(2)}) collective-permute-start(bf16[1024,256]{1,0:T(8,128)(2,1)S(1)} %stack.2), channel_id=1, source_target_pairs={{0,2},{2,0},{4,6},{6,4},{8,10},{10,8},{12,14},{14,12},{16,18},{18,... | collective-permute-start | bytes 1572872 | tf_op jit(solution)/shard_map/ppermute | solution.py:324

commit v4 on v2

--- a/solution.py
+++ b/solution.py
@@ -9,8 +9,9 @@
 from jax.sharding import PartitionSpec as P
 
 HEAD = 128
+LOG2E = math.log2(math.e)
 QH = 8
-GROUP = 2
+GROUP = 4
 F32 = jnp.float32
 BF16 = jnp.bfloat16
 NT = (((1,), (1,)), ((), ()))
@@ -64,8 +65,8 @@
         heads = range(first, first + GROUP)
         q = jnp.concatenate([q_ref[:, h * HEAD : (h + 1) * HEAD] for h in heads], axis=0)
         g = jnp.concatenate([g_ref[:, h * HEAD : (h + 1) * HEAD] for h in heads], axis=0)
-        scores = jnp.where(allowed, _mm(keys, q, NT) * scale, F32(-1e30))
-        expo = jnp.exp(scores - jnp.max(scores, axis=0, keepdims=True))
+        scores = jnp.where(allowed, _mm(keys, q, NT), F32(-1e30))
+        expo = jnp.exp2((scores - jnp.max(scores, axis=0, keepdims=True)) * (scale * LOG2E))
         probs = expo * (1.0 / jnp.sum(expo, axis=0, keepdims=True))
         low = probs.astype(BF16)
         grad_probs = _mm(values, g, NT)

time: 73.2 us -> 73.2 us (level)
  transfers between devices with their start and end apart: 21 -> 21, of which waited for: 14 -> 14; matrix products, arithmetic and copies ran while one was open for 0% -> 0% of each run, Pallas kernels for 8% -> 7%
where the time goes in v4:
time: 73.2 us; the launch traced here: 73 us
  waiting for transfers between devices  34.2 us (47%)
  starting transfers between devices  27.3 us (37%)
  Pallas kernels  7.54 us (10%)
  local copies, waits for them, and re-layouts  3.21 us (4%)
  between operations  0.83 us (1%)
    ppermute x19, waiting for transfers between devices, hop(): return lax.ppermute(value, 'dp', [(i, i ^ bits) for i in range(count)])  29.5 us
    ppermute x19, starting transfers between devices, hop(): return lax.ppermute(value, 'dp', [(i, i ^ bits) for i in range(count)])  22.5 us
    unnamed x14, local copies, waits for them, and re-layouts  3.21 us
    ppermute x1, starting transfers between devices, per_device_16x2(): other = lax.ppermute(partial, 'seq', swap)  3 us
    ppermute x1, waiting for transfers between devices, per_device_16x2(): other = lax.ppermute(partial, 'seq', swap)  2.7 us
    pallas_call x2, Pallas kernels, assemble(): pl.pallas_call(functools.partial(assemble_kernel, held, rows), out_shape=...  2.08 us
    ppermute x1, waiting for transfers between devices, per_device_16x2(): lax.ppermute(terms, 'seq', swap)  1.96 us
    pallas_call x1, Pallas kernels, attend(): pl.pallas_call(functools.partial(terms_kernel, len(kvs), 'seq'), out_shap...  1.81 us
  transfers between devices with their start and end apart: 21, of which 14 were waited for; matrix products, arithmetic and copies ran while one was open for 0% of the time, Pallas kernels for 7%

profile of v4, /device:TPU:0, one launch (start us, length us, event | category | flops | bytes accessed | tf_op | source)
XLA Modules:
  0.0 73.0 jit_solution(16438474909697553488)
XLA Ops:
  0.6 1.6 %copy-done = bf16[1,256,4096]{2,1,0:T(8,128)(2,1)S(1)} copy-done((bf16[1,256,4096]{2,1,0:T(8,128)(2,1)S(1)}, bf16[1,256,4096]{2,1,0:T(8,128)(2,1)}, u32[]{:S(2)}) %copy-start) | copy-done | bytes 2097176
  2.2 1.6 %copy-done.2 = bf16[4096,256]{1,0:T(8,128)(2,1)S(1)} copy-done((bf16[4096,256]{1,0:T(8,128)(2,1)S(1)}, bf16[4096,256]{1,0:T(8,128)(2,1)}, u32[]{:S(2)}) %copy-start.2) | copy-done | bytes 2097176
  3.8 0.7 project.1.refs_0_
  4.6 3.0 %collective-permute-start = (f32[256,256]{1,0:T(8,128)S(1)}, f32[256,256]{1,0:T(8,128)S(1)}, u32[]{:S(2)}, u32[]{:S(2)}) collective-permute-start(f32[256,256]{1,0:T(8,128)S(1)} %project.1.refs_0_), channel_id=1, source_target_pairs={{0,1},{1,0},{2,3},{3,2},{4,5},{5,4},{6,7},{7,6},{8,9},{9,8},{10,11... | collective-permute-start | bytes 786440 | tf_op jit(solution)/shard_map/ppermute | solution.py:336
  8.0 1.6 %collective-permute-start.1 = (bf16[256,1024]{1,0:T(8,128)(2,1)S(1)}, bf16[256,1024]{1,0:T(8,128)(2,1)S(1)}, u32[]{:S(2)}, u32[]{:S(2)}) collective-permute-start(bf16[256,1024]{1,0:T(8,128)(2,1)S(1)} %get-tuple-element.24), channel_id=1, source_target_pairs={{0,4},{2,6},{4,0},{6,2},{8,12},{10,14},{12,8},{14,10},{16,20},{18,... | collective-permute-start | bytes 1572872 | tf_op jit(solution)/shard_map/ppermute | solution.py:321
  9.6 1.6 %collective-permute-start.2 = (bf16[256,1024]{1,0:T(8,128)(2,1)S(1)}, bf16[256,1024]{1,0:T(8,128)(2,1)S(1)}, u32[]{:S(2)}, u32[]{:S(2)}) collective-permute-start(bf16[256,1024]{1,0:T(8,128)(2,1)S(1)} %get-tuple-element.25), channel_id=1, source_target_pairs={{0,8},{2,10},{4,12},{6,14},{8,0},{10,2},{12,4},{14,6},{16,24},{18,... | collective-permute-start | bytes 1572872 | tf_op jit(solution)/shard_map/ppermute | solution.py:321
  11.2 2.7 %collective-permute-done.refs_1_ = f32[256,256]{1,0:T(8,128)S(1)} collective-permute-done((f32[256,256]{1,0:T(8,128)S(1)}, f32[256,256]{1,0:T(8,128)S(1)}, u32[]{:S(2)}, u32[]{:S(2)}) %collective-permute-start) | collective-permute-done | bytes 262176 | tf_op jit(solution)/shard_map/ppermute | solution.py:336
  13.9 1.8 %attention_terms.1 = (bf16[256,256]{1,0:T(8,128)(2,1)S(1)}, bf16[256,1024]{1,0:T(8,128)(2,1)S(1)}, bf16[256,1024]{1,0:T(8,128)(2,1)S(1)}, f32[256,256]{1,0:T(8,128)S(1)}) custom-call(s32[2]{0:T(128)S(1)} %copy-done.6, s32[2,128]{1,0:T(2,128)S(1)} %bitcast.11, bf16[128,1024]{1,0:T(8,128)(2,1)S(1)} %bitcast.9, bf16[128,1024]{1,0:T(8,128)(2,1)S(1)} %bitcast.10, ...), custom_call_target="tpu_custom_call" | custom-call | tf_op jit(solution)/shard_map/attention_terms/pallas_call | solution.py:100
  15.7 1.8 %collective-permute-start.4 = (f32[256,256]{1,0:T(8,128)S(1)}, f32[256,256]{1,0:T(8,128)S(1)}, u32[]{:S(2)}, u32[]{:S(2)}) collective-permute-start(f32[256,256]{1,0:T(8,128)S(1)} %get-tuple-element.26.a_ref), channel_id=1, source_target_pairs={{0,1},{1,0},{2,3},{3,2},{4,5},{5,4},{6,7},{7,6},{8,9},{9,8},{10,11... | collective-permute-start | bytes 786440 | tf_op jit(solution)/shard_map/ppermute | solution.py:341
  17.5 2.5 %collective-permute-start.8 = (bf16[256,512]{1,0:T(8,128)(2,1)S(1)}, bf16[256,512]{1,0:T(8,128)(2,1)S(1)}, u32[]{:S(2)}, u32[]{:S(2)}) collective-permute-start(bf16[256,512]{1,0:T(8,128)(2,1)S(1)} %get-tuple-element.29), channel_id=1, source_target_pairs={{0,12},{2,14},{4,8},{6,10},{8,4},{10,6},{12,0},{14,2},{16,28},{18,... | collective-permute-start | bytes 786440 | tf_op jit(solution)/shard_map/ppermute | solution.py:321
  20.1 1.3 %attention_outputs.1 = (bf16[128,1024]{1,0:T(8,128)(2,1)}, bf16[128,1024]{1,0:T(8,128)(2,1)}, f32[8,128]{1,0:T(8,128)S(1)}) custom-call(bf16[256,256]{1,0:T(8,128)(2,1)S(1)} %get-tuple-element.18.kv_ref, bf16[256,1024]{1,0:T(8,128)(2,1)S(1)} %get-tuple-element.19.low_ref, bf16[256,1024]{1,0:T(8,128)(2,1)S(1)} %get-tuple-element.20.ds_ref), custom_call_target="tpu_custom_call" | custom-call | tf_op jit(solution)/shard_map/attention_outputs/pallas_call | solution.py:113
  21.3 2.0 %collective-permute-done.4.b_ref = f32[256,256]{1,0:T(8,128)S(1)} collective-permute-done((f32[256,256]{1,0:T(8,128)S(1)}, f32[256,256]{1,0:T(8,128)S(1)}, u32[]{:S(2)}, u32[]{:S(2)}) %collective-permute-start.4) | collective-permute-done | bytes 262176 | tf_op jit(solution)/shard_map/ppermute | solution.py:341
  23.3 1.2 %collective-permute-done.2.refs_2_ = bf16[256,1024]{1,0:T(8,128)(2,1)S(1)} collective-permute-done((bf16[256,1024]{1,0:T(8,128)(2,1)S(1)}, bf16[256,1024]{1,0:T(8,128)(2,1)S(1)}, u32[]{:S(2)}, u32[]{:S(2)}) %collective-permute-start.2) | collective-permute-done | bytes 524320 | tf_op jit(solution)/shard_map/ppermute | solution.py:321
  24.5 1.6 %collective-permute-start.7 = (bf16[256,256]{1,0:T(8,128)(2,1)S(1)}, bf16[256,256]{1,0:T(8,128)(2,1)S(1)}, u32[]{:S(2)}, u32[]{:S(2)}) collective-permute-start(bf16[256,256]{1,0:T(8,128)(2,1)S(1)} %round_grad.1.refs_4_), channel_id=1, source_target_pairs={{0,12},{2,14},{4,8},{6,10},{8,4},{10,6},{12,0},{14,2},{16,28},{18,... | collective-permute-start | bytes 393224 | tf_op jit(solution)/shard_map/ppermute | solution.py:321
  26.6 1.5 %collective-permute-start.5 = (bf16[256,256]{1,0:T(8,128)(2,1)S(1)}, bf16[256,256]{1,0:T(8,128)(2,1)S(1)}, u32[]{:S(2)}, u32[]{:S(2)}) collective-permute-start(bf16[256,256]{1,0:T(8,128)(2,1)S(1)} %round_grad.1.refs_4_), channel_id=1, source_target_pairs={{0,4},{2,6},{4,0},{6,2},{8,12},{10,14},{12,8},{14,10},{16,20},{18,... | collective-permute-start | bytes 393224 | tf_op jit(solution)/shard_map/ppermute | solution.py:321
  28.1 2.0 %collective-permute-done.8.refs_3_ = bf16[256,512]{1,0:T(8,128)(2,1)S(1)} collective-permute-done((bf16[256,512]{1,0:T(8,128)(2,1)S(1)}, bf16[256,512]{1,0:T(8,128)(2,1)S(1)}, u32[]{:S(2)}, u32[]{:S(2)}) %collective-permute-start.8) | collective-permute-done | bytes 262176 | tf_op jit(solution)/shard_map/ppermute | solution.py:321
  30.1 2.5 %collective-permute-done.7.refs_7_ = bf16[256,256]{1,0:T(8,128)(2,1)S(1)} collective-permute-done((bf16[256,256]{1,0:T(8,128)(2,1)S(1)}, bf16[256,256]{1,0:T(8,128)(2,1)S(1)}, u32[]{:S(2)}, u32[]{:S(2)}) %collective-permute-start.7) | collective-permute-done | bytes 131104 | tf_op jit(solution)/shard_map/ppermute | solution.py:321
  32.6 1.4 %collective-permute-done.6.refs_6_ = bf16[256,256]{1,0:T(8,128)(2,1)S(1)} collective-permute-done((bf16[256,256]{1,0:T(8,128)(2,1)S(1)}, bf16[256,256]{1,0:T(8,128)(2,1)S(1)}, u32[]{:S(2)}, u32[]{:S(2)}) %collective-permute-start.6) | collective-permute-done | bytes 131104 | tf_op jit(solution)/shard_map/ppermute | solution.py:321
  34.6 2.5 %collective-permute-start.3 = (bf16[256,512]{1,0:T(8,128)(2,1)S(1)}, bf16[256,512]{1,0:T(8,128)(2,1)S(1)}, u32[]{:S(2)}, u32[]{:S(2)}) collective-permute-start(bf16[256,512]{1,0:T(8,128)(2,1)S(1)} %slice_near_diagonal.1), channel_id=1, source_target_pairs={{0,12},{2,14},{4,8},{6,10},{8,4},{10,6},{12,0},{14,2},{16,28},{18,... | collective-permute-start | bytes 786440 | tf_op jit(solution)/shard_map/ppermute | solution.py:321
  37.2 2.7 %collective-permute-start.10 = (f32[256,256]{1,0:T(8,128)S(1)}, f32[256,256]{1,0:T(8,128)S(1)}, u32[]{:S(2)}, u32[]{:S(2)}) collective-permute-start(f32[256,256]{1,0:T(8,128)S(1)} %weight_fold.2), channel_id=1, source_target_pairs={{0,16},{2,18},{4,20},{6,22},{8,24},{10,26},{12,28},{14,30},{16,0},... | collective-permute-start | bytes 786440 | tf_op jit(solution)/shard_map/ppermute | solution.py:321
  39.8 9.8 %collective-permute-done.3.refs_3_ = bf16[256,512]{1,0:T(8,128)(2,1)S(1)} collective-permute-done((bf16[256,512]{1,0:T(8,128)(2,1)S(1)}, bf16[256,512]{1,0:T(8,128)(2,1)S(1)}, u32[]{:S(2)}, u32[]{:S(2)}) %collective-permute-start.3) | collective-permute-done | bytes 262176 | tf_op jit(solution)/shard_map/ppermute | solution.py:321
  50.2 2.0 %collective-permute-done.10.b_ref = f32[256,256]{1,0:T(8,128)S(1)} collective-permute-done((f32[256,256]{1,0:T(8,128)S(1)}, f32[256,256]{1,0:T(8,128)S(1)}, u32[]{:S(2)}, u32[]{:S(2)}) %collective-permute-start.10) | collective-permute-done | bytes 262176 | tf_op jit(solution)/shard_map/ppermute | solution.py:321
  52.6 3.7 %collective-permute-start.19 = (bf16[256,256]{1,0:T(8,128)(2,1)S(1)}, bf16[256,256]{1,0:T(8,128)(2,1)S(1)}, u32[]{:S(2)}, u32[]{:S(2)}) collective-permute-start(bf16[256,256]{1,0:T(8,128)(2,1)S(1)} %weight_finish.1.refs_0_), channel_id=1, source_target_pairs={{0,12},{2,14},{4,8},{6,10},{8,4},{10,6},{12,0},{14,2},{16,28},{18,... | collective-permute-start | bytes 393224 | tf_op jit(solution)/shard_map/ppermute | solution.py:321
  56.9 4.1 %collective-permute-done.12.refs_0_.refs_4_ = bf16[256,256]{1,0:T(8,128)(2,1)S(1)} collective-permute-done((bf16[256,256]{1,0:T(8,128)(2,1)S(1)}, bf16[256,256]{1,0:T(8,128)(2,1)S(1)}, u32[]{:S(2)}, u32[]{:S(2)}) %collective-permute-start.12) | collective-permute-done | bytes 131104 | tf_op jit(solution)/shard_map/ppermute | solution.py:321
  61.0 1.5 %collective-permute-start.14 = (bf16[256,256]{1,0:T(8,128)(2,1)S(1)}, bf16[256,256]{1,0:T(8,128)(2,1)S(1)}, u32[]{:S(2)}, u32[]{:S(2)}) collective-permute-start(bf16[256,256]{1,0:T(8,128)(2,1)S(1)} %collective-permute-done.12.refs_0_.refs_4_), channel_id=1, source_target_pairs={{0,4},{2,6},{4,0},{6,2},{8,12},{10,14},{12,8},{14,10},{16,20},{18,... | collective-permute-start | bytes 393224 | tf_op jit(solution)/shard_map/ppermute | solution.py:321
  62.8 1.7 %collective-permute-start.13 = (bf16[256,256]{1,0:T(8,128)(2,1)S(1)}, bf16[256,256]{1,0:T(8,128)(2,1)S(1)}, u32[]{:S(2)}, u32[]{:S(2)}) collective-permute-start(bf16[256,256]{1,0:T(8,128)(2,1)S(1)} %collective-permute-done.12.refs_0_.refs_4_), channel_id=1, source_target_pairs={{0,8},{2,10},{4,12},{6,14},{8,0},{10,2},{12,4},{14,6},{16,24},{18,... | collective-permute-start | bytes 393224 | tf_op jit(solution)/shard_map/ppermute | solution.py:321
  64.6 3.7 %collective-permute-done.15.refs_3_.refs_7_ = bf16[256,256]{1,0:T(8,128)(2,1)S(1)} collective-permute-done((bf16[256,256]{1,0:T(8,128)(2,1)S(1)}, bf16[256,256]{1,0:T(8,128)(2,1)S(1)}, u32[]{:S(2)}, u32[]{:S(2)}) %collective-permute-start.15) | collective-permute-done | bytes 131104 | tf_op jit(solution)/shard_map/ppermute | solution.py:321
  68.3 0.9 %collective-permute-done.14.refs_2_.refs_6_ = bf16[256,256]{1,0:T(8,128)(2,1)S(1)} collective-permute-done((bf16[256,256]{1,0:T(8,128)(2,1)S(1)}, bf16[256,256]{1,0:T(8,128)(2,1)S(1)}, u32[]{:S(2)}, u32[]{:S(2)}) %collective-permute-start.14) | collective-permute-done | bytes 131104 | tf_op jit(solution)/shard_map/ppermute | solution.py:321
  69.2 1.0 %collective-permute-done.13.refs_1_.refs_5_ = bf16[256,256]{1,0:T(8,128)(2,1)S(1)} collective-permute-done((bf16[256,256]{1,0:T(8,128)(2,1)S(1)}, bf16[256,256]{1,0:T(8,128)(2,1)S(1)}, u32[]{:S(2)}, u32[]{:S(2)}) %collective-permute-start.13) | collective-permute-done | bytes 131104 | tf_op jit(solution)/shard_map/ppermute | solution.py:321
  70.3 1.3 %weight_assemble.1.refs_1_ = bf16[4096,256]{1,0:T(8,128)(2,1)} custom-call(bf16[256,256]{1,0:T(8,128)(2,1)S(1)} %weight_finish.1.refs_0_, bf16[256,256]{1,0:T(8,128)(2,1)S(1)} %collective-permute-done.17.refs_1_, bf16[256,256]{1,0:T(8,128)(2,1)S(1)} %collective-permute-done.18.refs_2_, bf16[256,256]{1,0:T(8,128)(2,1)S(1)} %collective-permute-done.19.refs_3_, ...), custom_call_target="tpu_custom_call" | custom-call | tf_op jit(solution)/shard_map/weight_assemble/pallas_call | solution.py:307
  71.6 0.6 collective-permute-done.16.refs_0_
  72.2 0.8 %weight_complete.1 = bf16[4096,256]{1,0:T(8,128)(2,1)} custom-call(bf16[1024,256]{1,0:T(8,128)(2,1)S(1)} %collective-permute-done.16.refs_0_, bf16[4096,256]{1,0:T(8,128)(2,1)} %weight_assemble.1.refs_1_), custom_call_target="tpu_custom_call", output_to_operand_aliasing={{}: (1, {})} | custom-call | tf_op jit(solution)/shard_map/weight_complete/pallas_call | solution.py:307
  (39 shorter events, 3.7 us)
Async XLA Ops:
  0.6 1.6 %copy-start = (bf16[1,256,4096]{2,1,0:T(8,128)(2,1)S(1)}, bf16[1,256,4096]{2,1,0:T(8,128)(2,1)}, u32[]{:S(2)}) copy-start(bf16[1,256,4096]{2,1,0:T(8,128)(2,1)} %param.6) | copy-start | bytes 6291460
  2.2 1.6 %copy-start.2 = (bf16[4096,256]{1,0:T(8,128)(2,1)S(1)}, bf16[4096,256]{1,0:T(8,128)(2,1)}, u32[]{:S(2)}) copy-start(bf16[4096,256]{1,0:T(8,128)(2,1)} %w_ref.1) | copy-start | bytes 6291460
  4.5 9.4 %copy-start.3 = (bf16[1,128,1024]{2,1,0:T(8,128)(2,1)S(1)}, bf16[1,128,1024]{2,1,0:T(8,128)(2,1)}, u32[]{:S(2)}) copy-start(bf16[1,128,1024]{2,1,0:T(8,128)(2,1)} %param.7) | copy-start | bytes 786436
  4.5 9.4 %copy-start.4 = (bf16[1,128,1024]{2,1,0:T(8,128)(2,1)S(1)}, bf16[1,128,1024]{2,1,0:T(8,128)(2,1)}, u32[]{:S(2)}) copy-start(bf16[1,128,1024]{2,1,0:T(8,128)(2,1)} %param.8) | copy-start | bytes 786436
  4.6 9.3 %copy-start.5 = (s32[1,256]{1,0:T(1,128)S(1)}, s32[1,256]{1,0:T(1,128)}, u32[]{:S(2)}) copy-start(s32[1,256]{1,0:T(1,128)} %param.10) | copy-start | bytes 3076
  4.6 9.3 %copy-start.6 = (s32[2]{0:T(128)S(1)}, s32[2]{0:T(128)}, u32[]{:S(2)}) copy-start(s32[2]{0:T(128)} %order_ref.1) | copy-start | bytes 28
  4.6 9.3 %collective-permute-start = (f32[256,256]{1,0:T(8,128)S(1)}, f32[256,256]{1,0:T(8,128)S(1)}, u32[]{:S(2)}, u32[]{:S(2)}) collective-permute-start(f32[256,256]{1,0:T(8,128)S(1)} %project.1.refs_0_), channel_id=1, source_target_pairs={{0,1},{1,0},{2,3},{3,2},{4,5},{5,4},{6,7},{7,6},{8,9},{9,8},{10,11... | collective-permute-start | bytes 786440 | tf_op jit(solution)/shard_map/ppermute | solution.py:336
  8.0 15.3 %collective-permute-start.1 = (bf16[256,1024]{1,0:T(8,128)(2,1)S(1)}, bf16[256,1024]{1,0:T(8,128)(2,1)S(1)}, u32[]{:S(2)}, u32[]{:S(2)}) collective-permute-start(bf16[256,1024]{1,0:T(8,128)(2,1)S(1)} %get-tuple-element.24), channel_id=1, source_target_pairs={{0,4},{2,6},{4,0},{6,2},{8,12},{10,14},{12,8},{14,10},{16,20},{18,... | collective-permute-start | bytes 1572872 | tf_op jit(solution)/shard_map/ppermute | solution.py:321
  9.6 14.9 %collective-permute-start.2 = (bf16[256,1024]{1,0:T(8,128)(2,1)S(1)}, bf16[256,1024]{1,0:T(8,128)(2,1)S(1)}, u32[]{:S(2)}, u32[]{:S(2)}) collective-permute-start(bf16[256,1024]{1,0:T(8,128)(2,1)S(1)} %get-tuple-element.25), channel_id=1, source_target_pairs={{0,8},{2,10},{4,12},{6,14},{8,0},{10,2},{12,4},{14,6},{16,24},{18,... | collective-permute-start | bytes 1572872 | tf_op jit(solution)/shard_map/ppermute | solution.py:321
  15.7 7.6 %collective-permute-start.4 = (f32[256,256]{1,0:T(8,128)S(1)}, f32[256,256]{1,0:T(8,128)S(1)}, u32[]{:S(2)}, u32[]{:S(2)}) collective-permute-start(f32[256,256]{1,0:T(8,128)S(1)} %get-tuple-element.26.a_ref), channel_id=1, source_target_pairs={{0,1},{1,0},{2,3},{3,2},{4,5},{5,4},{6,7},{7,6},{8,9},{9,8},{10,11... | collective-permute-start | bytes 786440 | tf_op jit(solution)/shard_map/ppermute | solution.py:341
  17.5 12.6 %collective-permute-start.8 = (bf16[256,512]{1,0:T(8,128)(2,1)S(1)}, bf16[256,512]{1,0:T(8,128)(2,1)S(1)}, u32[]{:S(2)}, u32[]{:S(2)}) collective-permute-start(bf16[256,512]{1,0:T(8,128)(2,1)S(1)} %get-tuple-element.29), channel_id=1, source_target_pairs={{0,12},{2,14},{4,8},{6,10},{8,4},{10,6},{12,0},{14,2},{16,28},{18,... | collective-permute-start | bytes 786440 | tf_op jit(solution)/shard_map/ppermute | solution.py:321
  21.3 13.2 %copy-start.1 = (bf16[1,256,4096]{2,1,0:T(8,128)(2,1)S(1)}, bf16[1,256,4096]{2,1,0:T(8,128)(2,1)}, u32[]{:S(2)}) copy-start(bf16[1,256,4096]{2,1,0:T(8,128)(2,1)} %param.6) | copy-start | bytes 6291460
  24.5 8.1 %collective-permute-start.7 = (bf16[256,256]{1,0:T(8,128)(2,1)S(1)}, bf16[256,256]{1,0:T(8,128)(2,1)S(1)}, u32[]{:S(2)}, u32[]{:S(2)}) collective-permute-start(bf16[256,256]{1,0:T(8,128)(2,1)S(1)} %round_grad.1.refs_4_), channel_id=1, source_target_pairs={{0,12},{2,14},{4,8},{6,10},{8,4},{10,6},{12,0},{14,2},{16,28},{18,... | collective-permute-start | bytes 393224 | tf_op jit(solution)/shard_map/ppermute | solution.py:321
  26.1 7.9 %collective-permute-start.6 = (bf16[256,256]{1,0:T(8,128)(2,1)S(1)}, bf16[256,256]{1,0:T(8,128)(2,1)S(1)}, u32[]{:S(2)}, u32[]{:S(2)}) collective-permute-start(bf16[256,256]{1,0:T(8,128)(2,1)S(1)} %round_grad.1.refs_4_), channel_id=1, source_target_pairs={{0,8},{2,10},{4,12},{6,14},{8,0},{10,2},{12,4},{14,6},{16,24},{18,... | collective-permute-start | bytes 393224 | tf_op jit(solution)/shard_map/ppermute | solution.py:321
  26.6 7.4 %collective-permute-start.5 = (bf16[256,256]{1,0:T(8,128)(2,1)S(1)}, bf16[256,256]{1,0:T(8,128)(2,1)S(1)}, u32[]{:S(2)}, u32[]{:S(2)}) collective-permute-start(bf16[256,256]{1,0:T(8,128)(2,1)S(1)} %round_grad.1.refs_4_), channel_id=1, source_target_pairs={{0,4},{2,6},{4,0},{6,2},{8,12},{10,14},{12,8},{14,10},{16,20},{18,... | collective-permute-start | bytes 393224 | tf_op jit(solution)/shard_map/ppermute | solution.py:321
  34.4 2.7 %collective-permute-start.9 = (f32[256,256]{1,0:T(8,128)S(1)}, f32[256,256]{1,0:T(8,128)S(1)}, u32[]{:S(2)}, u32[]{:S(2)}) collective-permute-start(f32[256,256]{1,0:T(8,128)S(1)} %get-tuple-element.31), channel_id=1, source_target_pairs={{0,2},{2,0},{4,6},{6,4},{8,10},{10,8},{12,14},{14,12},{16,18},{18,... | collective-permute-start | bytes 786440 | tf_op jit(solution)/shard_map/ppermute | solution.py:321
  34.6 15.0 %collective-permute-start.3 = (bf16[256,512]{1,0:T(8,128)(2,1)S(1)}, bf16[256,512]{1,0:T(8,128)(2,1)S(1)}, u32[]{:S(2)}, u32[]{:S(2)}) collective-permute-start(bf16[256,512]{1,0:T(8,128)(2,1)S(1)} %slice_near_diagonal.1), channel_id=1, source_target_pairs={{0,12},{2,14},{4,8},{6,10},{8,4},{10,6},{12,0},{14,2},{16,28},{18,... | collective-permute-start | bytes 786440 | tf_op jit(solution)/shard_map/ppermute | solution.py:321
  37.2 15.0 %collective-permute-start.10 = (f32[256,256]{1,0:T(8,128)S(1)}, f32[256,256]{1,0:T(8,128)S(1)}, u32[]{:S(2)}, u32[]{:S(2)}) collective-permute-start(f32[256,256]{1,0:T(8,128)S(1)} %weight_fold.2), channel_id=1, source_target_pairs={{0,16},{2,18},{4,20},{6,22},{8,24},{10,26},{12,28},{14,30},{16,0},... | collective-permute-start | bytes 786440 | tf_op jit(solution)/shard_map/ppermute | solution.py:321
  50.1 2.1 %collective-permute-start.11 = (f32[256,256]{1,0:T(8,128)S(1)}, f32[256,256]{1,0:T(8,128)S(1)}, u32[]{:S(2)}, u32[]{:S(2)}) collective-permute-start(f32[256,256]{1,0:T(8,128)S(1)} %get-tuple-element.32), channel_id=1, source_target_pairs={{0,2},{2,0},{4,6},{6,4},{8,10},{10,8},{12,14},{14,12},{16,18},{18,... | collective-permute-start | bytes 786440 | tf_op jit(solution)/shard_map/ppermute | solution.py:321
  52.3 8.7 %collective-permute-start.12 = (bf16[256,256]{1,0:T(8,128)(2,1)S(1)}, bf16[256,256]{1,0:T(8,128)(2,1)S(1)}, u32[]{:S(2)}, u32[]{:S(2)}) collective-permute-start(bf16[256,256]{1,0:T(8,128)(2,1)S(1)} %weight_finish.1.refs_0_), channel_id=1, source_target_pairs={{0,16},{2,18},{4,20},{6,22},{8,24},{10,26},{12,28},{14,30},{16,0},... | collective-permute-start | bytes 393224 | tf_op jit(solution)/shard_map/ppermute | solution.py:321
  52.6 10.2 %collective-permute-start.19 = (bf16[256,256]{1,0:T(8,128)(2,1)S(1)}, bf16[256,256]{1,0:T(8,128)(2,1)S(1)}, u32[]{:S(2)}, u32[]{:S(2)}) collective-permute-start(bf16[256,256]{1,0:T(8,128)(2,1)S(1)} %weight_finish.1.refs_0_), channel_id=1, source_target_pairs={{0,12},{2,14},{4,8},{6,10},{8,4},{10,6},{12,0},{14,2},{16,28},{18,... | collective-permute-start | bytes 393224 | tf_op jit(solution)/shard_map/ppermute | solution.py:321
  56.3 8.2 %collective-permute-start.18 = (bf16[256,256]{1,0:T(8,128)(2,1)S(1)}, bf16[256,256]{1,0:T(8,128)(2,1)S(1)}, u32[]{:S(2)}, u32[]{:S(2)}) collective-permute-start(bf16[256,256]{1,0:T(8,128)(2,1)S(1)} %weight_finish.1.refs_0_), channel_id=1, source_target_pairs={{0,4},{2,6},{4,0},{6,2},{8,12},{10,14},{12,8},{14,10},{16,20},{18,... | collective-permute-start | bytes 393224 | tf_op jit(solution)/shard_map/ppermute | solution.py:321
  56.9 7.6 %collective-permute-start.17 = (bf16[256,256]{1,0:T(8,128)(2,1)S(1)}, bf16[256,256]{1,0:T(8,128)(2,1)S(1)}, u32[]{:S(2)}, u32[]{:S(2)}) collective-permute-start(bf16[256,256]{1,0:T(8,128)(2,1)S(1)} %weight_finish.1.refs_0_), channel_id=1, source_target_pairs={{0,8},{2,10},{4,12},{6,14},{8,0},{10,2},{12,4},{14,6},{16,24},{18,... | collective-permute-start | bytes 393224 | tf_op jit(solution)/shard_map/ppermute | solution.py:321
  61.0 7.3 %collective-permute-start.15 = (bf16[256,256]{1,0:T(8,128)(2,1)S(1)}, bf16[256,256]{1,0:T(8,128)(2,1)S(1)}, u32[]{:S(2)}, u32[]{:S(2)}) collective-permute-start(bf16[256,256]{1,0:T(8,128)(2,1)S(1)} %collective-permute-done.12.refs_0_.refs_4_), channel_id=1, source_target_pairs={{0,12},{2,14},{4,8},{6,10},{8,4},{10,6},{12,0},{14,2},{16,28},{18,... | collective-permute-start | bytes 393224 | tf_op jit(solution)/shard_map/ppermute | solution.py:321
  61.0 8.2 %collective-permute-start.14 = (bf16[256,256]{1,0:T(8,128)(2,1)S(1)}, bf16[256,256]{1,0:T(8,128)(2,1)S(1)}, u32[]{:S(2)}, u32[]{:S(2)}) collective-permute-start(bf16[256,256]{1,0:T(8,128)(2,1)S(1)} %collective-permute-done.12.refs_0_.refs_4_), channel_id=1, source_target_pairs={{0,4},{2,6},{4,0},{6,2},{8,12},{10,14},{12,8},{14,10},{16,20},{18,... | collective-permute-start | bytes 393224 | tf_op jit(solution)/shard_map/ppermute | solution.py:321
  62.8 7.4 %collective-permute-start.13 = (bf16[256,256]{1,0:T(8,128)(2,1)S(1)}, bf16[256,256]{1,0:T(8,128)(2,1)S(1)}, u32[]{:S(2)}, u32[]{:S(2)}) collective-permute-start(bf16[256,256]{1,0:T(8,128)(2,1)S(1)} %collective-permute-done.12.refs_0_.refs_4_), channel_id=1, source_target_pairs={{0,8},{2,10},{4,12},{6,14},{8,0},{10,2},{12,4},{14,6},{16,24},{18,... | collective-permute-start | bytes 393224 | tf_op jit(solution)/shard_map/ppermute | solution.py:321
  64.6 5.7 %collective-permute-start.20 = (bf16[1024,256]{1,0:T(8,128)(2,1)S(1)}, bf16[1024,256]{1,0:T(8,128)(2,1)S(1)}, u32[]{:S(2)}, u32[]{:S(2)}) collective-permute-start(bf16[1024,256]{1,0:T(8,128)(2,1)S(1)} %stack.3), channel_id=1, source_target_pairs={{0,2},{2,0},{4,6},{6,4},{8,10},{10,8},{12,14},{14,12},{16,18},{18,... | collective-permute-start | bytes 1572872 | tf_op jit(solution)/shard_map/ppermute | solution.py:321
  70.2 2.0 %collective-permute-start.16 = (bf16[1024,256]{1,0:T(8,128)(2,1)S(1)}, bf16[1024,256]{1,0:T(8,128)(2,1)S(1)}, u32[]{:S(2)}, u32[]{:S(2)}) collective-permute-start(bf16[1024,256]{1,0:T(8,128)(2,1)S(1)} %stack.2), channel_id=1, source_target_pairs={{0,2},{2,0},{4,6},{6,4},{8,10},{10,8},{12,14},{14,12},{16,18},{18,... | collective-permute-start | bytes 1572872 | tf_op jit(solution)/shard_map/ppermute | solution.py:321

commit v5 on v4

--- a/solution.py
+++ b/solution.py
@@ -122,6 +122,7 @@
 
 
 CORE, Y, Z1, Z2 = 1, 2, 4, 8
+CHUNKS = 8
 CORES = 2
 BLOCK = 4
 
@@ -136,8 +137,7 @@
     return pl.multiple_of((((block_of(device) ^ k) * CORES + core) * 2 + high) * width, width)
 
 
-def slice_kernel(wanted, tok_ref, *refs):
-    slices, sems = refs[-1 - len(wanted) : -1], refs[-1]
+def start_slices(wanted, tok_ref, slices, sems):
     me = lax.axis_index("dp")
     copies = []
     for (k, halves), ref in zip(wanted, slices):
@@ -151,7 +151,11 @@
                 )
                 copy.start()
                 copies.append(copy)
-    for copy in copies:
+    return copies
+
+
+def slice_kernel(wanted, tok_ref, *refs):
+    for copy in start_slices(wanted, tok_ref, refs[-1 - len(wanted) : -1], refs[-1]):
         copy.wait()
 
 
@@ -169,16 +173,41 @@
     )(tokens, *after)
 
 
-def project_kernel(tok_ref, w_ref, out_ref):
-    out_ref[...] = _mm(tok_ref[...], w_ref[...], NN)
-
-
-def project(tokens, w_kv):
-    return pl.pallas_call(
-        project_kernel,
-        out_shape=jax.ShapeDtypeStruct((tokens.shape[0], w_kv.shape[1]), F32),
-        in_specs=[VMEM, VMEM],
-        out_specs=VMEM,
+def project_kernel(wanted, tok_ref, w_ref, out_ref, *refs):
+    slices, (slice_sems, w_v, w_sems) = refs[:-3], refs[-3:]
+    chunk = w_ref.shape[0] // CHUNKS
+    loads = []
+    for k in range(CHUNKS):
+        cut = pl.ds(k * chunk, chunk)
+        load = pltpu.make_async_copy(w_ref.at[cut, :], w_v.at[cut, :], w_sems.at[k])
+        load.start()
+        loads.append(load)
+    copies = start_slices(wanted, tok_ref, slices, slice_sems)
+    total = None
+    for k, load in enumerate(loads):
+        load.wait()
+        cut = slice(k * chunk, (k + 1) * chunk)
+        term = _mm(tok_ref[:, cut], w_v[cut, :], NN)
+        total = term if total is None else total + term
+    out_ref[...] = total
+    for copy in copies:
+        copy.wait()
+
+
+def project(tokens, w_kv, wanted):
+    rows, features = tokens.shape
+    half = features // (2 * BLOCK)
+    return pl.pallas_call(
+        functools.partial(project_kernel, wanted),
+        out_shape=[jax.ShapeDtypeStruct((rows, w_kv.shape[1]), F32)]
+        + [jax.ShapeDtypeStruct((rows, half * len(halves)), BF16) for _, halves in wanted],
+        in_specs=[VMEM, ANY],
+        out_specs=[VMEM] * (1 + len(wanted)),
+        scratch_shapes=[
+            pltpu.SemaphoreType.DMA((sum(2 * len(halves) for _, halves in wanted),)),
+            pltpu.VMEM(w_kv.shape, BF16),
+            pltpu.SemaphoreType.DMA((CHUNKS,)),
+        ],
         compiler_params=LIMIT,
         name="project",
     )(tokens, w_kv)
@@ -328,11 +357,10 @@
     near = (Y, Z1, Y | Z1)
     flat = tokens[0]
     both = (True, False)
-    own, tok_y, tok_z, far_d = slice_tokens(
-        flat, [(0, both), (1, both), (2, both), (3, (True,))], "slice_first"
+    partial, own, tok_y, tok_z, far_d = project(
+        flat, w_kv, [(0, both), (1, both), (2, both), (3, (True,))]
     )
     tok_y, tok_z, far_d = hop(tok_y, Y), hop(tok_z, Z1), hop(far_d, Y | Z1)
-    partial = project(flat, w_kv)
     other = lax.ppermute(partial, "seq", swap)
     docs = doc_ids.reshape(-1, rows_dev)
     attention, query_grad, terms, done = attend(

time: 73.2 us -> 73.2 us (level)
  Pallas kernels: 7.54 us -> 9.25 us
  local copies, waits for them, and re-layouts: 3.21 us -> 1.6 us
    pallas_call x1, Pallas kernels: 0.7 us -> 2.85 us  [project(): pl.pallas_call(functools.partial(project_kernel, wanted), out_shape=[jax....]
    ppermute x1, waiting for transfers between devices: 1.96 us -> 0.01 us  [per_device_16x2(): lax.ppermute(terms, 'seq', swap)]
    unnamed x14 -> x12, local copies, waits for them, and re-layouts: 3.21 us -> 1.6 us
    ppermute x19, waiting for transfers between devices: 29.5 us -> 31 us  [hop(): return lax.ppermute(value, 'dp', [(i, i ^ bits) for i in range(count)])]
where the time goes in v5:
time: 73.2 us; the launch traced here: 73 us
  waiting for transfers between devices  34.2 us (47%)
  starting transfers between devices  27.2 us (37%)
  Pallas kernels  9.25 us (13%)
  local copies, waits for them, and re-layouts  1.6 us (2%)
  between operations  0.8 us (1%)
    ppermute x19, waiting for transfers between devices, hop(): return lax.ppermute(value, 'dp', [(i, i ^ bits) for i in range(count)])  31 us
    ppermute x19, starting transfers between devices, hop(): return lax.ppermute(value, 'dp', [(i, i ^ bits) for i in range(count)])  22.4 us
    ppermute x1, waiting for transfers between devices, per_device_16x2(): other = lax.ppermute(partial, 'seq', swap)  3.21 us
    ppermute x1, starting transfers between devices, per_device_16x2(): other = lax.ppermute(partial, 'seq', swap)  3 us
    pallas_call x1, Pallas kernels, project(): pl.pallas_call(functools.partial(project_kernel, wanted), out_shape=[jax....  2.85 us
    pallas_call x2, Pallas kernels, assemble(): pl.pallas_call(functools.partial(assemble_kernel, held, rows), out_shape=...  2.08 us
    ppermute x1, starting transfers between devices, per_device_16x2(): lax.ppermute(terms, 'seq', swap)  1.81 us
    pallas_call x1, Pallas kernels, attend(): pl.pallas_call(functools.partial(terms_kernel, len(kvs), 'seq'), out_shap...  1.8 us
  transfers between devices with their start and end apart: 21, of which 14 were waited for; matrix products, arithmetic and copies ran while one was open for 0% of the time, Pallas kernels for 7%

profile of v5, /device:TPU:0, one launch (start us, length us, event | category | flops | bytes accessed | tf_op | source)
XLA Modules:
  0.0 73.0 jit_solution(584172768119798893)
XLA Ops:
  0.6 1.6 %copy-done = bf16[1,256,4096]{2,1,0:T(8,128)(2,1)S(1)} copy-done((bf16[1,256,4096]{2,1,0:T(8,128)(2,1)S(1)}, bf16[1,256,4096]{2,1,0:T(8,128)(2,1)}, u32[]{:S(2)}) %copy-start) | copy-done | bytes 2097176
  2.2 2.9 %project.1 = (f32[256,256]{1,0:T(8,128)S(1)}, bf16[256,1024]{1,0:T(8,128)(2,1)S(1)}, bf16[256,1024]{1,0:T(8,128)(2,1)S(1)}, bf16[256,1024]{1,0:T(8,128)(2,1)S(1)}, bf16[256,512]{1,0:T(8,128)(2,1)S(1)}) custom-call(bf16[256,4096]{1,0:T(8,128)(2,1)S(1)} %bitcast.6, bf16[4096,256]{1,0:T(8,128)(2,1)} %w_ref.1), custom_call_target="tpu_custom_call" | custom-call | tf_op jit(solution)/shard_map/project/pallas_call | solution.py:200
  5.1 3.0 %collective-permute-start = (f32[256,256]{1,0:T(8,128)S(1)}, f32[256,256]{1,0:T(8,128)S(1)}, u32[]{:S(2)}, u32[]{:S(2)}) collective-permute-start(f32[256,256]{1,0:T(8,128)S(1)} %get-tuple-element.19.refs_0_), channel_id=1, source_target_pairs={{0,1},{1,0},{2,3},{3,2},{4,5},{5,4},{6,7},{7,6},{8,9},{9,8},{10,11... | collective-permute-start | bytes 786440 | tf_op jit(solution)/shard_map/ppermute | solution.py:364
  8.1 1.5 %collective-permute-start.1 = (bf16[256,1024]{1,0:T(8,128)(2,1)S(1)}, bf16[256,1024]{1,0:T(8,128)(2,1)S(1)}, u32[]{:S(2)}, u32[]{:S(2)}) collective-permute-start(bf16[256,1024]{1,0:T(8,128)(2,1)S(1)} %get-tuple-element.26), channel_id=1, source_target_pairs={{0,4},{2,6},{4,0},{6,2},{8,12},{10,14},{12,8},{14,10},{16,20},{18,... | collective-permute-start | bytes 1572872 | tf_op jit(solution)/shard_map/ppermute | solution.py:350
  9.6 1.6 %collective-permute-start.2 = (bf16[256,1024]{1,0:T(8,128)(2,1)S(1)}, bf16[256,1024]{1,0:T(8,128)(2,1)S(1)}, u32[]{:S(2)}, u32[]{:S(2)}) collective-permute-start(bf16[256,1024]{1,0:T(8,128)(2,1)S(1)} %get-tuple-element.27), channel_id=1, source_target_pairs={{0,8},{2,10},{4,12},{6,14},{8,0},{10,2},{12,4},{14,6},{16,24},{18,... | collective-permute-start | bytes 1572872 | tf_op jit(solution)/shard_map/ppermute | solution.py:350
  11.2 3.2 %collective-permute-done.refs_1_ = f32[256,256]{1,0:T(8,128)S(1)} collective-permute-done((f32[256,256]{1,0:T(8,128)S(1)}, f32[256,256]{1,0:T(8,128)S(1)}, u32[]{:S(2)}, u32[]{:S(2)}) %collective-permute-start) | collective-permute-done | bytes 262176 | tf_op jit(solution)/shard_map/ppermute | solution.py:364
  14.4 1.8 %attention_terms.1 = (bf16[256,256]{1,0:T(8,128)(2,1)S(1)}, bf16[256,1024]{1,0:T(8,128)(2,1)S(1)}, bf16[256,1024]{1,0:T(8,128)(2,1)S(1)}, f32[256,256]{1,0:T(8,128)S(1)}) custom-call(s32[2]{0:T(128)S(1)} %copy-done.5, s32[2,128]{1,0:T(2,128)S(1)} %bitcast.10, bf16[128,1024]{1,0:T(8,128)(2,1)S(1)} %bitcast.8, bf16[128,1024]{1,0:T(8,128)(2,1)S(1)} %bitcast.9, ...), custom_call_target="tpu_custom_call" | custom-call | tf_op jit(solution)/shard_map/attention_terms/pallas_call | solution.py:100
  16.2 1.8 %collective-permute-start.4 = (f32[256,256]{1,0:T(8,128)S(1)}, f32[256,256]{1,0:T(8,128)S(1)}, u32[]{:S(2)}, u32[]{:S(2)}) collective-permute-start(f32[256,256]{1,0:T(8,128)S(1)} %get-tuple-element.28.a_ref), channel_id=1, source_target_pairs={{0,1},{1,0},{2,3},{3,2},{4,5},{5,4},{6,7},{7,6},{8,9},{9,8},{10,11... | collective-permute-start | bytes 786440 | tf_op jit(solution)/shard_map/ppermute | solution.py:369
  18.0 2.5 %collective-permute-start.8 = (bf16[256,512]{1,0:T(8,128)(2,1)S(1)}, bf16[256,512]{1,0:T(8,128)(2,1)S(1)}, u32[]{:S(2)}, u32[]{:S(2)}) collective-permute-start(bf16[256,512]{1,0:T(8,128)(2,1)S(1)} %get-tuple-element.31), channel_id=1, source_target_pairs={{0,12},{2,14},{4,8},{6,10},{8,4},{10,6},{12,0},{14,2},{16,28},{18,... | collective-permute-start | bytes 786440 | tf_op jit(solution)/shard_map/ppermute | solution.py:350
  20.6 1.2 %attention_outputs.1 = (bf16[128,1024]{1,0:T(8,128)(2,1)}, bf16[128,1024]{1,0:T(8,128)(2,1)}, f32[8,128]{1,0:T(8,128)S(1)}) custom-call(bf16[256,256]{1,0:T(8,128)(2,1)S(1)} %get-tuple-element.20.kv_ref, bf16[256,1024]{1,0:T(8,128)(2,1)S(1)} %get-tuple-element.21.low_ref, bf16[256,1024]{1,0:T(8,128)(2,1)S(1)} %get-tuple-element.22.ds_ref), custom_call_target="tpu_custom_call" | custom-call | tf_op jit(solution)/shard_map/attention_outputs/pallas_call | solution.py:113
  22.1 2.4 %collective-permute-done.2.refs_2_ = bf16[256,1024]{1,0:T(8,128)(2,1)S(1)} collective-permute-done((bf16[256,1024]{1,0:T(8,128)(2,1)S(1)}, bf16[256,1024]{1,0:T(8,128)(2,1)S(1)}, u32[]{:S(2)}, u32[]{:S(2)}) %collective-permute-start.2) | collective-permute-done | bytes 524320 | tf_op jit(solution)/shard_map/ppermute | solution.py:350
  24.5 1.8 %collective-permute-start.7 = (bf16[256,256]{1,0:T(8,128)(2,1)S(1)}, bf16[256,256]{1,0:T(8,128)(2,1)S(1)}, u32[]{:S(2)}, u32[]{:S(2)}) collective-permute-start(bf16[256,256]{1,0:T(8,128)(2,1)S(1)} %round_grad.1.refs_4_), channel_id=1, source_target_pairs={{0,12},{2,14},{4,8},{6,10},{8,4},{10,6},{12,0},{14,2},{16,28},{18,... | collective-permute-start | bytes 393224 | tf_op jit(solution)/shard_map/ppermute | solution.py:350
  26.8 1.3 %collective-permute-start.5 = (bf16[256,256]{1,0:T(8,128)(2,1)S(1)}, bf16[256,256]{1,0:T(8,128)(2,1)S(1)}, u32[]{:S(2)}, u32[]{:S(2)}) collective-permute-start(bf16[256,256]{1,0:T(8,128)(2,1)S(1)} %round_grad.1.refs_4_), channel_id=1, source_target_pairs={{0,4},{2,6},{4,0},{6,2},{8,12},{10,14},{12,8},{14,10},{16,20},{18,... | collective-permute-start | bytes 393224 | tf_op jit(solution)/shard_map/ppermute | solution.py:350
  28.1 2.0 %collective-permute-done.8.refs_3_ = bf16[256,512]{1,0:T(8,128)(2,1)S(1)} collective-permute-done((bf16[256,512]{1,0:T(8,128)(2,1)S(1)}, bf16[256,512]{1,0:T(8,128)(2,1)S(1)}, u32[]{:S(2)}, u32[]{:S(2)}) %collective-permute-start.8) | collective-permute-done | bytes 262176 | tf_op jit(solution)/shard_map/ppermute | solution.py:350
  30.1 2.5 %collective-permute-done.7.refs_7_ = bf16[256,256]{1,0:T(8,128)(2,1)S(1)} collective-permute-done((bf16[256,256]{1,0:T(8,128)(2,1)S(1)}, bf16[256,256]{1,0:T(8,128)(2,1)S(1)}, u32[]{:S(2)}, u32[]{:S(2)}) %collective-permute-start.7) | collective-permute-done | bytes 131104 | tf_op jit(solution)/shard_map/ppermute | solution.py:350
  32.6 1.4 %collective-permute-done.6.refs_6_ = bf16[256,256]{1,0:T(8,128)(2,1)S(1)} collective-permute-done((bf16[256,256]{1,0:T(8,128)(2,1)S(1)}, bf16[256,256]{1,0:T(8,128)(2,1)S(1)}, u32[]{:S(2)}, u32[]{:S(2)}) %collective-permute-start.6) | collective-permute-done | bytes 131104 | tf_op jit(solution)/shard_map/ppermute | solution.py:350
  34.6 2.5 %collective-permute-start.3 = (bf16[256,512]{1,0:T(8,128)(2,1)S(1)}, bf16[256,512]{1,0:T(8,128)(2,1)S(1)}, u32[]{:S(2)}, u32[]{:S(2)}) collective-permute-start(bf16[256,512]{1,0:T(8,128)(2,1)S(1)} %slice_near_diagonal.1), channel_id=1, source_target_pairs={{0,12},{2,14},{4,8},{6,10},{8,4},{10,6},{12,0},{14,2},{16,28},{18,... | collective-permute-start | bytes 786440 | tf_op jit(solution)/shard_map/ppermute | solution.py:350
  37.2 2.7 %collective-permute-start.10 = (f32[256,256]{1,0:T(8,128)S(1)}, f32[256,256]{1,0:T(8,128)S(1)}, u32[]{:S(2)}, u32[]{:S(2)}) collective-permute-start(f32[256,256]{1,0:T(8,128)S(1)} %weight_fold.2), channel_id=1, source_target_pairs={{0,16},{2,18},{4,20},{6,22},{8,24},{10,26},{12,28},{14,30},{16,0},... | collective-permute-start | bytes 786440 | tf_op jit(solution)/shard_map/ppermute | solution.py:350
  39.8 9.9 %collective-permute-done.3.refs_3_ = bf16[256,512]{1,0:T(8,128)(2,1)S(1)} collective-permute-done((bf16[256,512]{1,0:T(8,128)(2,1)S(1)}, bf16[256,512]{1,0:T(8,128)(2,1)S(1)}, u32[]{:S(2)}, u32[]{:S(2)}) %collective-permute-start.3) | collective-permute-done | bytes 262176 | tf_op jit(solution)/shard_map/ppermute | solution.py:350
  49.7 0.5 weight_part.2
  50.2 2.0 %collective-permute-done.10.b_ref = f32[256,256]{1,0:T(8,128)S(1)} collective-permute-done((f32[256,256]{1,0:T(8,128)S(1)}, f32[256,256]{1,0:T(8,128)S(1)}, u32[]{:S(2)}, u32[]{:S(2)}) %collective-permute-start.10) | collective-permute-done | bytes 262176 | tf_op jit(solution)/shard_map/ppermute | solution.py:350
  52.6 3.7 %collective-permute-start.19 = (bf16[256,256]{1,0:T(8,128)(2,1)S(1)}, bf16[256,256]{1,0:T(8,128)(2,1)S(1)}, u32[]{:S(2)}, u32[]{:S(2)}) collective-permute-start(bf16[256,256]{1,0:T(8,128)(2,1)S(1)} %weight_finish.1.refs_0_), channel_id=1, source_target_pairs={{0,12},{2,14},{4,8},{6,10},{8,4},{10,6},{12,0},{14,2},{16,28},{18,... | collective-permute-start | bytes 393224 | tf_op jit(solution)/shard_map/ppermute | solution.py:350
  56.3 0.6 collective-permute-start.18
  56.9 4.1 %collective-permute-done.12.refs_0_.refs_4_ = bf16[256,256]{1,0:T(8,128)(2,1)S(1)} collective-permute-done((bf16[256,256]{1,0:T(8,128)(2,1)S(1)}, bf16[256,256]{1,0:T(8,128)(2,1)S(1)}, u32[]{:S(2)}, u32[]{:S(2)}) %collective-permute-start.12) | collective-permute-done | bytes 131104 | tf_op jit(solution)/shard_map/ppermute | solution.py:350
  61.0 1.5 %collective-permute-start.14 = (bf16[256,256]{1,0:T(8,128)(2,1)S(1)}, bf16[256,256]{1,0:T(8,128)(2,1)S(1)}, u32[]{:S(2)}, u32[]{:S(2)}) collective-permute-start(bf16[256,256]{1,0:T(8,128)(2,1)S(1)} %collective-permute-done.12.refs_0_.refs_4_), channel_id=1, source_target_pairs={{0,4},{2,6},{4,0},{6,2},{8,12},{10,14},{12,8},{14,10},{16,20},{18,... | collective-permute-start | bytes 393224 | tf_op jit(solution)/shard_map/ppermute | solution.py:350
  62.8 1.7 %collective-permute-start.13 = (bf16[256,256]{1,0:T(8,128)(2,1)S(1)}, bf16[256,256]{1,0:T(8,128)(2,1)S(1)}, u32[]{:S(2)}, u32[]{:S(2)}) collective-permute-start(bf16[256,256]{1,0:T(8,128)(2,1)S(1)} %collective-permute-done.12.refs_0_.refs_4_), channel_id=1, source_target_pairs={{0,8},{2,10},{4,12},{6,14},{8,0},{10,2},{12,4},{14,6},{16,24},{18,... | collective-permute-start | bytes 393224 | tf_op jit(solution)/shard_map/ppermute | solution.py:350
  64.7 3.7 %collective-permute-done.15.refs_3_.refs_7_ = bf16[256,256]{1,0:T(8,128)(2,1)S(1)} collective-permute-done((bf16[256,256]{1,0:T(8,128)(2,1)S(1)}, bf16[256,256]{1,0:T(8,128)(2,1)S(1)}, u32[]{:S(2)}, u32[]{:S(2)}) %collective-permute-start.15) | collective-permute-done | bytes 131104 | tf_op jit(solution)/shard_map/ppermute | solution.py:350
  68.4 0.9 %collective-permute-done.14.refs_2_.refs_6_ = bf16[256,256]{1,0:T(8,128)(2,1)S(1)} collective-permute-done((bf16[256,256]{1,0:T(8,128)(2,1)S(1)}, bf16[256,256]{1,0:T(8,128)(2,1)S(1)}, u32[]{:S(2)}, u32[]{:S(2)}) %collective-permute-start.14) | collective-permute-done | bytes 131104 | tf_op jit(solution)/shard_map/ppermute | solution.py:350
  69.2 1.0 %collective-permute-done.13.refs_1_.refs_5_ = bf16[256,256]{1,0:T(8,128)(2,1)S(1)} collective-permute-done((bf16[256,256]{1,0:T(8,128)(2,1)S(1)}, bf16[256,256]{1,0:T(8,128)(2,1)S(1)}, u32[]{:S(2)}, u32[]{:S(2)}) %collective-permute-start.13) | collective-permute-done | bytes 131104 | tf_op jit(solution)/shard_map/ppermute | solution.py:350
  70.3 1.3 %weight_assemble.1.refs_1_ = bf16[4096,256]{1,0:T(8,128)(2,1)} custom-call(bf16[256,256]{1,0:T(8,128)(2,1)S(1)} %weight_finish.1.refs_0_, bf16[256,256]{1,0:T(8,128)(2,1)S(1)} %collective-permute-done.17.refs_1_, bf16[256,256]{1,0:T(8,128)(2,1)S(1)} %collective-permute-done.18.refs_2_, bf16[256,256]{1,0:T(8,128)(2,1)S(1)} %collective-permute-done.19.refs_3_, ...), custom_call_target="tpu_custom_call" | custom-call | tf_op jit(solution)/shard_map/weight_assemble/pallas_call | solution.py:336
  71.6 0.6 collective-permute-done.16.refs_0_
  72.2 0.8 %weight_complete.1 = bf16[4096,256]{1,0:T(8,128)(2,1)} custom-call(bf16[1024,256]{1,0:T(8,128)(2,1)S(1)} %collective-permute-done.16.refs_0_, bf16[4096,256]{1,0:T(8,128)(2,1)} %weight_assemble.1.refs_1_), custom_call_target="tpu_custom_call", output_to_operand_aliasing={{}: (1, {})} | custom-call | tf_op jit(solution)/shard_map/weight_complete/pallas_call | solution.py:336
  (36 shorter events, 2.4 us)
Async XLA Ops:
  0.6 1.6 %copy-start = (bf16[1,256,4096]{2,1,0:T(8,128)(2,1)S(1)}, bf16[1,256,4096]{2,1,0:T(8,128)(2,1)}, u32[]{:S(2)}) copy-start(bf16[1,256,4096]{2,1,0:T(8,128)(2,1)} %param.6) | copy-start | bytes 6291460
  2.2 12.2 %copy-start.2 = (bf16[1,128,1024]{2,1,0:T(8,128)(2,1)S(1)}, bf16[1,128,1024]{2,1,0:T(8,128)(2,1)}, u32[]{:S(2)}) copy-start(bf16[1,128,1024]{2,1,0:T(8,128)(2,1)} %param.7) | copy-start | bytes 786436
  2.2 12.2 %copy-start.3 = (bf16[1,128,1024]{2,1,0:T(8,128)(2,1)S(1)}, bf16[1,128,1024]{2,1,0:T(8,128)(2,1)}, u32[]{:S(2)}) copy-start(bf16[1,128,1024]{2,1,0:T(8,128)(2,1)} %param.8) | copy-start | bytes 786436
  2.2 12.2 %copy-start.4 = (s32[1,256]{1,0:T(1,128)S(1)}, s32[1,256]{1,0:T(1,128)}, u32[]{:S(2)}) copy-start(s32[1,256]{1,0:T(1,128)} %param.10) | copy-start | bytes 3076
  2.2 12.2 %copy-start.5 = (s32[2]{0:T(128)S(1)}, s32[2]{0:T(128)}, u32[]{:S(2)}) copy-start(s32[2]{0:T(128)} %order_ref.1) | copy-start | bytes 28
  5.1 9.3 %collective-permute-start = (f32[256,256]{1,0:T(8,128)S(1)}, f32[256,256]{1,0:T(8,128)S(1)}, u32[]{:S(2)}, u32[]{:S(2)}) collective-permute-start(f32[256,256]{1,0:T(8,128)S(1)} %get-tuple-element.19.refs_0_), channel_id=1, source_target_pairs={{0,1},{1,0},{2,3},{3,2},{4,5},{5,4},{6,7},{7,6},{8,9},{9,8},{10,11... | collective-permute-start | bytes 786440 | tf_op jit(solution)/shard_map/ppermute | solution.py:364
  8.1 14.0 %collective-permute-start.1 = (bf16[256,1024]{1,0:T(8,128)(2,1)S(1)}, bf16[256,1024]{1,0:T(8,128)(2,1)S(1)}, u32[]{:S(2)}, u32[]{:S(2)}) collective-permute-start(bf16[256,1024]{1,0:T(8,128)(2,1)S(1)} %get-tuple-element.26), channel_id=1, source_target_pairs={{0,4},{2,6},{4,0},{6,2},{8,12},{10,14},{12,8},{14,10},{16,20},{18,... | collective-permute-start | bytes 1572872 | tf_op jit(solution)/shard_map/ppermute | solution.py:350
  9.6 14.9 %collective-permute-start.2 = (bf16[256,1024]{1,0:T(8,128)(2,1)S(1)}, bf16[256,1024]{1,0:T(8,128)(2,1)S(1)}, u32[]{:S(2)}, u32[]{:S(2)}) collective-permute-start(bf16[256,1024]{1,0:T(8,128)(2,1)S(1)} %get-tuple-element.27), channel_id=1, source_target_pairs={{0,8},{2,10},{4,12},{6,14},{8,0},{10,2},{12,4},{14,6},{16,24},{18,... | collective-permute-start | bytes 1572872 | tf_op jit(solution)/shard_map/ppermute | solution.py:350
  16.2 8.3 %collective-permute-start.4 = (f32[256,256]{1,0:T(8,128)S(1)}, f32[256,256]{1,0:T(8,128)S(1)}, u32[]{:S(2)}, u32[]{:S(2)}) collective-permute-start(f32[256,256]{1,0:T(8,128)S(1)} %get-tuple-element.28.a_ref), channel_id=1, source_target_pairs={{0,1},{1,0},{2,3},{3,2},{4,5},{5,4},{6,7},{7,6},{8,9},{9,8},{10,11... | collective-permute-start | bytes 786440 | tf_op jit(solution)/shard_map/ppermute | solution.py:369
  18.0 12.0 %collective-permute-start.8 = (bf16[256,512]{1,0:T(8,128)(2,1)S(1)}, bf16[256,512]{1,0:T(8,128)(2,1)S(1)}, u32[]{:S(2)}, u32[]{:S(2)}) collective-permute-start(bf16[256,512]{1,0:T(8,128)(2,1)S(1)} %get-tuple-element.31), channel_id=1, source_target_pairs={{0,12},{2,14},{4,8},{6,10},{8,4},{10,6},{12,0},{14,2},{16,28},{18,... | collective-permute-start | bytes 786440 | tf_op jit(solution)/shard_map/ppermute | solution.py:350
  21.8 12.7 %copy-start.1 = (bf16[1,256,4096]{2,1,0:T(8,128)(2,1)S(1)}, bf16[1,256,4096]{2,1,0:T(8,128)(2,1)}, u32[]{:S(2)}) copy-start(bf16[1,256,4096]{2,1,0:T(8,128)(2,1)} %param.6) | copy-start | bytes 6291460
  24.5 8.0 %collective-permute-start.7 = (bf16[256,256]{1,0:T(8,128)(2,1)S(1)}, bf16[256,256]{1,0:T(8,128)(2,1)S(1)}, u32[]{:S(2)}, u32[]{:S(2)}) collective-permute-start(bf16[256,256]{1,0:T(8,128)(2,1)S(1)} %round_grad.1.refs_4_), channel_id=1, source_target_pairs={{0,12},{2,14},{4,8},{6,10},{8,4},{10,6},{12,0},{14,2},{16,28},{18,... | collective-permute-start | bytes 393224 | tf_op jit(solution)/shard_map/ppermute | solution.py:350
  26.4 7.6 %collective-permute-start.6 = (bf16[256,256]{1,0:T(8,128)(2,1)S(1)}, bf16[256,256]{1,0:T(8,128)(2,1)S(1)}, u32[]{:S(2)}, u32[]{:S(2)}) collective-permute-start(bf16[256,256]{1,0:T(8,128)(2,1)S(1)} %round_grad.1.refs_4_), channel_id=1, source_target_pairs={{0,8},{2,10},{4,12},{6,14},{8,0},{10,2},{12,4},{14,6},{16,24},{18,... | collective-permute-start | bytes 393224 | tf_op jit(solution)/shard_map/ppermute | solution.py:350
  26.8 7.2 %collective-permute-start.5 = (bf16[256,256]{1,0:T(8,128)(2,1)S(1)}, bf16[256,256]{1,0:T(8,128)(2,1)S(1)}, u32[]{:S(2)}, u32[]{:S(2)}) collective-permute-start(bf16[256,256]{1,0:T(8,128)(2,1)S(1)} %round_grad.1.refs_4_), channel_id=1, source_target_pairs={{0,4},{2,6},{4,0},{6,2},{8,12},{10,14},{12,8},{14,10},{16,20},{18,... | collective-permute-start | bytes 393224 | tf_op jit(solution)/shard_map/ppermute | solution.py:350
  34.5 2.7 %collective-permute-start.9 = (f32[256,256]{1,0:T(8,128)S(1)}, f32[256,256]{1,0:T(8,128)S(1)}, u32[]{:S(2)}, u32[]{:S(2)}) collective-permute-start(f32[256,256]{1,0:T(8,128)S(1)} %get-tuple-element.33), channel_id=1, source_target_pairs={{0,2},{2,0},{4,6},{6,4},{8,10},{10,8},{12,14},{14,12},{16,18},{18,... | collective-permute-start | bytes 786440 | tf_op jit(solution)/shard_map/ppermute | solution.py:350
  34.6 15.0 %collective-permute-start.3 = (bf16[256,512]{1,0:T(8,128)(2,1)S(1)}, bf16[256,512]{1,0:T(8,128)(2,1)S(1)}, u32[]{:S(2)}, u32[]{:S(2)}) collective-permute-start(bf16[256,512]{1,0:T(8,128)(2,1)S(1)} %slice_near_diagonal.1), channel_id=1, source_target_pairs={{0,12},{2,14},{4,8},{6,10},{8,4},{10,6},{12,0},{14,2},{16,28},{18,... | collective-permute-start | bytes 786440 | tf_op jit(solution)/shard_map/ppermute | solution.py:350
  37.2 15.0 %collective-permute-start.10 = (f32[256,256]{1,0:T(8,128)S(1)}, f32[256,256]{1,0:T(8,128)S(1)}, u32[]{:S(2)}, u32[]{:S(2)}) collective-permute-start(f32[256,256]{1,0:T(8,128)S(1)} %weight_fold.2), channel_id=1, source_target_pairs={{0,16},{2,18},{4,20},{6,22},{8,24},{10,26},{12,28},{14,30},{16,0},... | collective-permute-start | bytes 786440 | tf_op jit(solution)/shard_map/ppermute | solution.py:350
  50.2 2.1 %collective-permute-start.11 = (f32[256,256]{1,0:T(8,128)S(1)}, f32[256,256]{1,0:T(8,128)S(1)}, u32[]{:S(2)}, u32[]{:S(2)}) collective-permute-start(f32[256,256]{1,0:T(8,128)S(1)} %get-tuple-element.34), channel_id=1, source_target_pairs={{0,2},{2,0},{4,6},{6,4},{8,10},{10,8},{12,14},{14,12},{16,18},{18,... | collective-permute-start | bytes 786440 | tf_op jit(solution)/shard_map/ppermute | solution.py:350
  52.3 8.7 %collective-permute-start.12 = (bf16[256,256]{1,0:T(8,128)(2,1)S(1)}, bf16[256,256]{1,0:T(8,128)(2,1)S(1)}, u32[]{:S(2)}, u32[]{:S(2)}) collective-permute-start(bf16[256,256]{1,0:T(8,128)(2,1)S(1)} %weight_finish.1.refs_0_), channel_id=1, source_target_pairs={{0,16},{2,18},{4,20},{6,22},{8,24},{10,26},{12,28},{14,30},{16,0},... | collective-permute-start | bytes 393224 | tf_op jit(solution)/shard_map/ppermute | solution.py:350
  52.6 10.2 %collective-permute-start.19 = (bf16[256,256]{1,0:T(8,128)(2,1)S(1)}, bf16[256,256]{1,0:T(8,128)(2,1)S(1)}, u32[]{:S(2)}, u32[]{:S(2)}) collective-permute-start(bf16[256,256]{1,0:T(8,128)(2,1)S(1)} %weight_finish.1.refs_0_), channel_id=1, source_target_pairs={{0,12},{2,14},{4,8},{6,10},{8,4},{10,6},{12,0},{14,2},{16,28},{18,... | collective-permute-start | bytes 393224 | tf_op jit(solution)/shard_map/ppermute | solution.py:350
  56.3 8.2 %collective-permute-start.18 = (bf16[256,256]{1,0:T(8,128)(2,1)S(1)}, bf16[256,256]{1,0:T(8,128)(2,1)S(1)}, u32[]{:S(2)}, u32[]{:S(2)}) collective-permute-start(bf16[256,256]{1,0:T(8,128)(2,1)S(1)} %weight_finish.1.refs_0_), channel_id=1, source_target_pairs={{0,4},{2,6},{4,0},{6,2},{8,12},{10,14},{12,8},{14,10},{16,20},{18,... | collective-permute-start | bytes 393224 | tf_op jit(solution)/shard_map/ppermute | solution.py:350
  56.9 7.6 %collective-permute-start.17 = (bf16[256,256]{1,0:T(8,128)(2,1)S(1)}, bf16[256,256]{1,0:T(8,128)(2,1)S(1)}, u32[]{:S(2)}, u32[]{:S(2)}) collective-permute-start(bf16[256,256]{1,0:T(8,128)(2,1)S(1)} %weight_finish.1.refs_0_), channel_id=1, source_target_pairs={{0,8},{2,10},{4,12},{6,14},{8,0},{10,2},{12,4},{14,6},{16,24},{18,... | collective-permute-start | bytes 393224 | tf_op jit(solution)/shard_map/ppermute | solution.py:350
  61.0 7.3 %collective-permute-start.15 = (bf16[256,256]{1,0:T(8,128)(2,1)S(1)}, bf16[256,256]{1,0:T(8,128)(2,1)S(1)}, u32[]{:S(2)}, u32[]{:S(2)}) collective-permute-start(bf16[256,256]{1,0:T(8,128)(2,1)S(1)} %collective-permute-done.12.refs_0_.refs_4_), channel_id=1, source_target_pairs={{0,12},{2,14},{4,8},{6,10},{8,4},{10,6},{12,0},{14,2},{16,28},{18,... | collective-permute-start | bytes 393224 | tf_op jit(solution)/shard_map/ppermute | solution.py:350
  61.0 8.2 %collective-permute-start.14 = (bf16[256,256]{1,0:T(8,128)(2,1)S(1)}, bf16[256,256]{1,0:T(8,128)(2,1)S(1)}, u32[]{:S(2)}, u32[]{:S(2)}) collective-permute-start(bf16[256,256]{1,0:T(8,128)(2,1)S(1)} %collective-permute-done.12.refs_0_.refs_4_), channel_id=1, source_target_pairs={{0,4},{2,6},{4,0},{6,2},{8,12},{10,14},{12,8},{14,10},{16,20},{18,... | collective-permute-start | bytes 393224 | tf_op jit(solution)/shard_map/ppermute | solution.py:350
  62.8 7.3 %collective-permute-start.13 = (bf16[256,256]{1,0:T(8,128)(2,1)S(1)}, bf16[256,256]{1,0:T(8,128)(2,1)S(1)}, u32[]{:S(2)}, u32[]{:S(2)}) collective-permute-start(bf16[256,256]{1,0:T(8,128)(2,1)S(1)} %collective-permute-done.12.refs_0_.refs_4_), channel_id=1, source_target_pairs={{0,8},{2,10},{4,12},{6,14},{8,0},{10,2},{12,4},{14,6},{16,24},{18,... | collective-permute-start | bytes 393224 | tf_op jit(solution)/shard_map/ppermute | solution.py:350
  64.6 5.7 %collective-permute-start.20 = (bf16[1024,256]{1,0:T(8,128)(2,1)S(1)}, bf16[1024,256]{1,0:T(8,128)(2,1)S(1)}, u32[]{:S(2)}, u32[]{:S(2)}) collective-permute-start(bf16[1024,256]{1,0:T(8,128)(2,1)S(1)} %stack.3), channel_id=1, source_target_pairs={{0,2},{2,0},{4,6},{6,4},{8,10},{10,8},{12,14},{14,12},{16,18},{18,... | collective-permute-start | bytes 1572872 | tf_op jit(solution)/shard_map/ppermute | solution.py:350
  70.2 2.0 %collective-permute-start.16 = (bf16[1024,256]{1,0:T(8,128)(2,1)S(1)}, bf16[1024,256]{1,0:T(8,128)(2,1)S(1)}, u32[]{:S(2)}, u32[]{:S(2)}) collective-permute-start(bf16[1024,256]{1,0:T(8,128)(2,1)S(1)} %stack.2), channel_id=1, source_target_pairs={{0,2},{2,0},{4,6},{6,4},{8,10},{10,8},{12,14},{14,12},{16,18},{18,... | collective-permute-start | bytes 1572872 | tf_op jit(solution)/shard_map/ppermute | solution.py:350

commit v6 on v4

--- a/solution.py
+++ b/solution.py
@@ -37,7 +37,9 @@
     if parts == 1:
         kv = kv_refs[0][...]
     else:
-        kv = (kv_refs[0][...] + kv_refs[1][...]).astype(BF16)
+        kv = jnp.concatenate(
+            [(kv_refs[n][...] + kv_refs[n + 1][...]).astype(BF16) for n in (0, 2)], axis=1
+        )
     kv_ref[...] = kv
     keys = kv[:, :HEAD]
     values = kv[:, HEAD:]
@@ -80,7 +82,8 @@
     terms_ref[HEAD:, :] = value_grad.T
 
 
-def outputs_kernel(kv_ref, low_ref, ds_ref, att_ref, qg_ref, done_ref):
+def outputs_kernel(kv_ref, low_ref, ds_ref, *refs):
+    att_ref, qg_ref, done_ref = refs[-3:]
     rows = att_ref.shape[0]
     done_ref[...] = jnp.zeros_like(done_ref)
     keys_t = kv_ref[:, :HEAD].T
@@ -95,7 +98,7 @@
             qg_ref[:, head] = qg[:, i * rows : (i + 1) * rows].T.astype(BF16)
 
 
-def attend(order, docs, q, g, kvs):
+def attend(order, docs, q, g, kvs, arrived=()):
     seq_len, rows = kvs[0].shape[0], q.shape[0]
     kv, low, grad_scores, terms = pl.pallas_call(
         functools.partial(terms_kernel, len(kvs), "seq"),
@@ -113,11 +116,11 @@
     attention, query_grad, done = pl.pallas_call(
         outputs_kernel,
         out_shape=[jax.ShapeDtypeStruct(q.shape, BF16)] * 2 + [jax.ShapeDtypeStruct((8, HEAD), F32)],
-        in_specs=[VMEM] * 3,
+        in_specs=[VMEM] * 3 + [ANY] * len(arrived),
         out_specs=[VMEM] * 3,
         compiler_params=LIMIT,
         name="attention_outputs",
-    )(kv, low, grad_scores)
+    )(kv, low, grad_scores, *arrived)
     return attention, query_grad, terms, done
 
 
@@ -169,16 +172,19 @@
     )(tokens, *after)
 
 
-def project_kernel(tok_ref, w_ref, out_ref):
-    out_ref[...] = _mm(tok_ref[...], w_ref[...], NN)
+def project_kernel(tok_ref, w_ref, key_ref, value_ref):
+    total = _mm(tok_ref[...], w_ref[...], NN)
+    key_ref[...] = total[:, :HEAD]
+    value_ref[...] = total[:, HEAD:]
 
 
 def project(tokens, w_kv):
+    half = jax.ShapeDtypeStruct((tokens.shape[0], w_kv.shape[1] // 2), F32)
     return pl.pallas_call(
         project_kernel,
-        out_shape=jax.ShapeDtypeStruct((tokens.shape[0], w_kv.shape[1]), F32),
+        out_shape=[half, half],
         in_specs=[VMEM, VMEM],
-        out_specs=VMEM,
+        out_specs=[VMEM, VMEM],
         compiler_params=LIMIT,
         name="project",
     )(tokens, w_kv)
@@ -332,13 +338,13 @@
         flat, [(0, both), (1, both), (2, both), (3, (True,))], "slice_first"
     )
     tok_y, tok_z, far_d = hop(tok_y, Y), hop(tok_z, Z1), hop(far_d, Y | Z1)
-    partial = project(flat, w_kv)
-    other = lax.ppermute(partial, "seq", swap)
+    keys, values = project(flat, w_kv)
+    keys_in, values_in = lax.ppermute(keys, "seq", swap), lax.ppermute(values, "seq", swap)
     docs = doc_ids.reshape(-1, rows_dev)
     attention, query_grad, terms, done = attend(
-        span_order, docs, queries[0], grad_out[0], [partial, other]
+        span_order, docs, queries[0], grad_out[0], [keys, keys_in, values, values_in], [tok_y, tok_z]
     )
-    grad = round_grad(terms, lax.ppermute(terms, "seq", swap), [done, tok_y, tok_z])
+    grad = round_grad(terms, lax.ppermute(terms, "seq", swap), [done])
     grads = [grad] + [hop(grad, bits) for bits in near]
     keep, send = weight_part([own, tok_y, tok_z, far_d], grads, dp_size, [0, 0, 0, 0])
     part = fold(keep, hop(send, CORE))

time: 73.2 us -> 70.2 us (0.959)
  starting transfers between devices: 27.3 us -> 24.5 us
  local copies, waits for them, and re-layouts: 3.21 us -> 1.61 us
  waiting for transfers between devices: 34.2 us -> 35.6 us
    ppermute x2 -> x3, waiting for transfers between devices: 4.66 us -> 8.27 us  [the longest x1 4.06 us: per_device_16x2(): lax.ppermute(keys, 'seq', swap)]
    ppermute x19, waiting for transfers between devices: 29.5 us -> 27.3 us  [hop(): return lax.ppermute(value, 'dp', [(i, i ^ bits) for i in range(count)])]
    ppermute x19, starting transfers between devices: 22.5 us -> 20.8 us  [hop(): return lax.ppermute(value, 'dp', [(i, i ^ bits) for i in range(count)])]
    unnamed x14, local copies, waits for them, and re-layouts: 3.21 us -> 1.61 us
    ppermute x2 -> x3, starting transfers between devices: 4.81 us -> 3.65 us  [the longest x1 1.56 us: per_device_16x2(): grad = round_grad(terms, lax.ppermute(terms, 'seq', swap), [done])]
  transfers between devices with their start and end apart: 21 -> 22, of which waited for: 14 -> 15; matrix products, arithmetic and copies ran while one was open for 0% -> 0% of each run, Pallas kernels for 7% -> 8%
where the time goes in v6:
time: 70.2 us; the launch traced here: 70 us
  waiting for transfers between devices  35.6 us (51%)
  starting transfers between devices  24.5 us (35%)
  Pallas kernels  7.51 us (11%)
  local copies, waits for them, and re-layouts  1.61 us (2%)
  between operations  0.81 us (1%)
    ppermute x19, waiting for transfers between devices, hop(): return lax.ppermute(value, 'dp', [(i, i ^ bits) for i in range(count)])  27.3 us
    ppermute x19, starting transfers between devices, hop(): return lax.ppermute(value, 'dp', [(i, i ^ bits) for i in range(count)])  20.8 us
    ppermute x1, waiting for transfers between devices, per_device_16x2(): lax.ppermute(keys, 'seq', swap)  4.06 us
    ppermute x1, waiting for transfers between devices, per_device_16x2(): grad = round_grad(terms, lax.ppermute(terms, 'seq', swap), [done])  2.82 us
    pallas_call x2, Pallas kernels, assemble(): pl.pallas_call(functools.partial(assemble_kernel, held, rows), out_shape=...  2.08 us
    pallas_call x1, Pallas kernels, attend(): pl.pallas_call(functools.partial(terms_kernel, len(kvs), 'seq'), out_shap...  1.81 us
    unnamed x14, local copies, waits for them, and re-layouts  1.61 us
    ppermute x1, starting transfers between devices, per_device_16x2(): grad = round_grad(terms, lax.ppermute(terms, 'seq', swap), [done])  1.56 us
  transfers between devices with their start and end apart: 22, of which 15 were waited for; matrix products, arithmetic and copies ran while one was open for 0% of the time, Pallas kernels for 8%

profile of v6, /device:TPU:0, one launch (start us, length us, event | category | flops | bytes accessed | tf_op | source)
XLA Modules:
  0.0 70.0 jit_solution(14208984605903617674)
XLA Ops:
  0.6 1.6 %copy-done = bf16[1,256,4096]{2,1,0:T(8,128)(2,1)S(1)} copy-done((bf16[1,256,4096]{2,1,0:T(8,128)(2,1)S(1)}, bf16[1,256,4096]{2,1,0:T(8,128)(2,1)}, u32[]{:S(2)}) %copy-start) | copy-done | bytes 2097176
  2.7 3.0 %collective-permute-start.2 = (bf16[256,1024]{1,0:T(8,128)(2,1)S(1)}, bf16[256,1024]{1,0:T(8,128)(2,1)S(1)}, u32[]{:S(2)}, u32[]{:S(2)}) collective-permute-start(bf16[256,1024]{1,0:T(8,128)(2,1)S(1)} %get-tuple-element.25), channel_id=1, source_target_pairs={{0,4},{2,6},{4,0},{6,2},{8,12},{10,14},{12,8},{14,10},{16,20},{18,... | collective-permute-start | bytes 1572872 | tf_op jit(solution)/shard_map/ppermute | solution.py:327
  5.7 1.6 %collective-permute-start.3 = (bf16[256,1024]{1,0:T(8,128)(2,1)S(1)}, bf16[256,1024]{1,0:T(8,128)(2,1)S(1)}, u32[]{:S(2)}, u32[]{:S(2)}) collective-permute-start(bf16[256,1024]{1,0:T(8,128)(2,1)S(1)} %get-tuple-element.26), channel_id=1, source_target_pairs={{0,8},{2,10},{4,12},{6,14},{8,0},{10,2},{12,4},{14,6},{16,24},{18,... | collective-permute-start | bytes 1572872 | tf_op jit(solution)/shard_map/ppermute | solution.py:327
  7.4 0.7 %project.1 = (f32[256,128]{1,0:T(8,128)S(1)}, f32[256,128]{1,0:T(8,128)S(1)}) custom-call(bf16[256,4096]{1,0:T(8,128)(2,1)S(1)} %bitcast.7, bf16[4096,256]{1,0:T(8,128)(2,1)S(1)} %copy-done.2), custom_call_target="tpu_custom_call" | custom-call | tf_op jit(solution)/shard_map/project/pallas_call | solution.py:183
  8.1 1.6 %collective-permute-start = (f32[256,128]{1,0:T(8,128)S(1)}, f32[256,128]{1,0:T(8,128)S(1)}, u32[]{:S(2)}, u32[]{:S(2)}) collective-permute-start(f32[256,128]{1,0:T(8,128)S(1)} %get-tuple-element.20.refs_0_), channel_id=1, source_target_pairs={{0,1},{1,0},{2,3},{3,2},{4,5},{5,4},{6,7},{7,6},{8,9},{9,8},{10,11... | collective-permute-start | bytes 393224 | tf_op jit(solution)/shard_map/ppermute | solution.py:342
  10.2 4.1 %collective-permute-done.refs_1_ = f32[256,128]{1,0:T(8,128)S(1)} collective-permute-done((f32[256,128]{1,0:T(8,128)S(1)}, f32[256,128]{1,0:T(8,128)S(1)}, u32[]{:S(2)}, u32[]{:S(2)}) %collective-permute-start) | collective-permute-done | bytes 131104 | tf_op jit(solution)/shard_map/ppermute | solution.py:342
  14.2 1.4 %collective-permute-done.1.refs_3_ = f32[256,128]{1,0:T(8,128)S(1)} collective-permute-done((f32[256,128]{1,0:T(8,128)S(1)}, f32[256,128]{1,0:T(8,128)S(1)}, u32[]{:S(2)}, u32[]{:S(2)}) %collective-permute-start.1) | collective-permute-done | bytes 131104 | tf_op jit(solution)/shard_map/ppermute | solution.py:342
  15.6 1.8 %attention_terms.1 = (bf16[256,256]{1,0:T(8,128)(2,1)S(1)}, bf16[256,1024]{1,0:T(8,128)(2,1)S(1)}, bf16[256,1024]{1,0:T(8,128)(2,1)S(1)}, f32[256,256]{1,0:T(8,128)S(1)}) custom-call(s32[2]{0:T(128)S(1)} %copy-done.6, s32[2,128]{1,0:T(2,128)S(1)} %bitcast.11, bf16[128,1024]{1,0:T(8,128)(2,1)S(1)} %bitcast.9, bf16[128,1024]{1,0:T(8,128)(2,1)S(1)} %bitcast.10, ...), custom_call_target="tpu_custom_call" | custom-call | tf_op jit(solution)/shard_map/attention_terms/pallas_call | solution.py:103
  17.5 1.6 %collective-permute-start.5 = (f32[256,256]{1,0:T(8,128)S(1)}, f32[256,256]{1,0:T(8,128)S(1)}, u32[]{:S(2)}, u32[]{:S(2)}) collective-permute-start(f32[256,256]{1,0:T(8,128)S(1)} %get-tuple-element.30.a_ref), channel_id=1, source_target_pairs={{0,1},{1,0},{2,3},{3,2},{4,5},{5,4},{6,7},{7,6},{8,9},{9,8},{10,11... | collective-permute-start | bytes 786440 | tf_op jit(solution)/shard_map/ppermute | solution.py:347
  19.0 1.0 %collective-permute-start.9 = (bf16[256,512]{1,0:T(8,128)(2,1)S(1)}, bf16[256,512]{1,0:T(8,128)(2,1)S(1)}, u32[]{:S(2)}, u32[]{:S(2)}) collective-permute-start(bf16[256,512]{1,0:T(8,128)(2,1)S(1)} %get-tuple-element.33), channel_id=1, source_target_pairs={{0,12},{2,14},{4,8},{6,10},{8,4},{10,6},{12,0},{14,2},{16,28},{18,... | collective-permute-start | bytes 786440 | tf_op jit(solution)/shard_map/ppermute | solution.py:327
  20.0 1.2 %attention_outputs.1 = (bf16[128,1024]{1,0:T(8,128)(2,1)}, bf16[128,1024]{1,0:T(8,128)(2,1)}, f32[8,128]{1,0:T(8,128)S(1)}) custom-call(bf16[256,256]{1,0:T(8,128)(2,1)S(1)} %get-tuple-element.22.kv_ref, bf16[256,1024]{1,0:T(8,128)(2,1)S(1)} %get-tuple-element.23.low_ref, bf16[256,1024]{1,0:T(8,128)(2,1)S(1)} %get-tuple-element.24.ds_ref, ...), custom_call_target="tpu_custom_call" | custom-call | tf_op jit(solution)/shard_map/attention_outputs/pallas_call | solution.py:116
  21.3 2.8 %collective-permute-done.5.b_ref = f32[256,256]{1,0:T(8,128)S(1)} collective-permute-done((f32[256,256]{1,0:T(8,128)S(1)}, f32[256,256]{1,0:T(8,128)S(1)}, u32[]{:S(2)}, u32[]{:S(2)}) %collective-permute-start.5) | collective-permute-done | bytes 262176 | tf_op jit(solution)/shard_map/ppermute | solution.py:347
  24.1 1.7 %collective-permute-start.8 = (bf16[256,256]{1,0:T(8,128)(2,1)S(1)}, bf16[256,256]{1,0:T(8,128)(2,1)S(1)}, u32[]{:S(2)}, u32[]{:S(2)}) collective-permute-start(bf16[256,256]{1,0:T(8,128)(2,1)S(1)} %round_grad.1.refs_4_), channel_id=1, source_target_pairs={{0,12},{2,14},{4,8},{6,10},{8,4},{10,6},{12,0},{14,2},{16,28},{18,... | collective-permute-start | bytes 393224 | tf_op jit(solution)/shard_map/ppermute | solution.py:327
  26.1 1.5 %collective-permute-start.6 = (bf16[256,256]{1,0:T(8,128)(2,1)S(1)}, bf16[256,256]{1,0:T(8,128)(2,1)S(1)}, u32[]{:S(2)}, u32[]{:S(2)}) collective-permute-start(bf16[256,256]{1,0:T(8,128)(2,1)S(1)} %round_grad.1.refs_4_), channel_id=1, source_target_pairs={{0,4},{2,6},{4,0},{6,2},{8,12},{10,14},{12,8},{14,10},{16,20},{18,... | collective-permute-start | bytes 393224 | tf_op jit(solution)/shard_map/ppermute | solution.py:327
  27.7 2.9 %collective-permute-done.8.refs_7_ = bf16[256,256]{1,0:T(8,128)(2,1)S(1)} collective-permute-done((bf16[256,256]{1,0:T(8,128)(2,1)S(1)}, bf16[256,256]{1,0:T(8,128)(2,1)S(1)}, u32[]{:S(2)}, u32[]{:S(2)}) %collective-permute-start.8) | collective-permute-done | bytes 131104 | tf_op jit(solution)/shard_map/ppermute | solution.py:327
  30.9 1.0 %collective-permute-done.6.refs_5_ = bf16[256,256]{1,0:T(8,128)(2,1)S(1)} collective-permute-done((bf16[256,256]{1,0:T(8,128)(2,1)S(1)}, bf16[256,256]{1,0:T(8,128)(2,1)S(1)}, u32[]{:S(2)}, u32[]{:S(2)}) %collective-permute-start.6) | collective-permute-done | bytes 131104 | tf_op jit(solution)/shard_map/ppermute | solution.py:327
  32.5 1.6 %collective-permute-start.4 = (bf16[256,512]{1,0:T(8,128)(2,1)S(1)}, bf16[256,512]{1,0:T(8,128)(2,1)S(1)}, u32[]{:S(2)}, u32[]{:S(2)}) collective-permute-start(bf16[256,512]{1,0:T(8,128)(2,1)S(1)} %slice_near_diagonal.1), channel_id=1, source_target_pairs={{0,12},{2,14},{4,8},{6,10},{8,4},{10,6},{12,0},{14,2},{16,28},{18,... | collective-permute-start | bytes 786440 | tf_op jit(solution)/shard_map/ppermute | solution.py:327
  34.2 2.6 %collective-permute-start.11 = (f32[256,256]{1,0:T(8,128)S(1)}, f32[256,256]{1,0:T(8,128)S(1)}, u32[]{:S(2)}, u32[]{:S(2)}) collective-permute-start(f32[256,256]{1,0:T(8,128)S(1)} %weight_fold.2), channel_id=1, source_target_pairs={{0,16},{2,18},{4,20},{6,22},{8,24},{10,26},{12,28},{14,30},{16,0},... | collective-permute-start | bytes 786440 | tf_op jit(solution)/shard_map/ppermute | solution.py:327
  36.8 11.0 %collective-permute-done.4.refs_3_ = bf16[256,512]{1,0:T(8,128)(2,1)S(1)} collective-permute-done((bf16[256,512]{1,0:T(8,128)(2,1)S(1)}, bf16[256,512]{1,0:T(8,128)(2,1)S(1)}, u32[]{:S(2)}, u32[]{:S(2)}) %collective-permute-start.4) | collective-permute-done | bytes 262176 | tf_op jit(solution)/shard_map/ppermute | solution.py:327
  48.3 0.9 %collective-permute-done.11.b_ref = f32[256,256]{1,0:T(8,128)S(1)} collective-permute-done((f32[256,256]{1,0:T(8,128)S(1)}, f32[256,256]{1,0:T(8,128)S(1)}, u32[]{:S(2)}, u32[]{:S(2)}) %collective-permute-start.11) | collective-permute-done | bytes 262176 | tf_op jit(solution)/shard_map/ppermute | solution.py:327
  49.2 0.6 collective-permute-done.12.b_ref
  50.1 3.3 %collective-permute-start.20 = (bf16[256,256]{1,0:T(8,128)(2,1)S(1)}, bf16[256,256]{1,0:T(8,128)(2,1)S(1)}, u32[]{:S(2)}, u32[]{:S(2)}) collective-permute-start(bf16[256,256]{1,0:T(8,128)(2,1)S(1)} %weight_finish.1.refs_0_), channel_id=1, source_target_pairs={{0,12},{2,14},{4,8},{6,10},{8,4},{10,6},{12,0},{14,2},{16,28},{18,... | collective-permute-start | bytes 393224 | tf_op jit(solution)/shard_map/ppermute | solution.py:327
  53.4 0.7 %collective-permute-start.19 = (bf16[256,256]{1,0:T(8,128)(2,1)S(1)}, bf16[256,256]{1,0:T(8,128)(2,1)S(1)}, u32[]{:S(2)}, u32[]{:S(2)}) collective-permute-start(bf16[256,256]{1,0:T(8,128)(2,1)S(1)} %weight_finish.1.refs_0_), channel_id=1, source_target_pairs={{0,4},{2,6},{4,0},{6,2},{8,12},{10,14},{12,8},{14,10},{16,20},{18,... | collective-permute-start | bytes 393224 | tf_op jit(solution)/shard_map/ppermute | solution.py:327
  54.1 4.1 %collective-permute-done.13.refs_0_.refs_4_ = bf16[256,256]{1,0:T(8,128)(2,1)S(1)} collective-permute-done((bf16[256,256]{1,0:T(8,128)(2,1)S(1)}, bf16[256,256]{1,0:T(8,128)(2,1)S(1)}, u32[]{:S(2)}, u32[]{:S(2)}) %collective-permute-start.13) | collective-permute-done | bytes 131104 | tf_op jit(solution)/shard_map/ppermute | solution.py:327
  58.3 1.2 %collective-permute-start.15 = (bf16[256,256]{1,0:T(8,128)(2,1)S(1)}, bf16[256,256]{1,0:T(8,128)(2,1)S(1)}, u32[]{:S(2)}, u32[]{:S(2)}) collective-permute-start(bf16[256,256]{1,0:T(8,128)(2,1)S(1)} %collective-permute-done.13.refs_0_.refs_4_), channel_id=1, source_target_pairs={{0,4},{2,6},{4,0},{6,2},{8,12},{10,14},{12,8},{14,10},{16,20},{18,... | collective-permute-start | bytes 393224 | tf_op jit(solution)/shard_map/ppermute | solution.py:327
  60.1 1.7 %collective-permute-start.14 = (bf16[256,256]{1,0:T(8,128)(2,1)S(1)}, bf16[256,256]{1,0:T(8,128)(2,1)S(1)}, u32[]{:S(2)}, u32[]{:S(2)}) collective-permute-start(bf16[256,256]{1,0:T(8,128)(2,1)S(1)} %collective-permute-done.13.refs_0_.refs_4_), channel_id=1, source_target_pairs={{0,8},{2,10},{4,12},{6,14},{8,0},{10,2},{12,4},{14,6},{16,24},{18,... | collective-permute-start | bytes 393224 | tf_op jit(solution)/shard_map/ppermute | solution.py:327
  61.9 3.7 %collective-permute-done.16.refs_3_.refs_7_ = bf16[256,256]{1,0:T(8,128)(2,1)S(1)} collective-permute-done((bf16[256,256]{1,0:T(8,128)(2,1)S(1)}, bf16[256,256]{1,0:T(8,128)(2,1)S(1)}, u32[]{:S(2)}, u32[]{:S(2)}) %collective-permute-start.16) | collective-permute-done | bytes 131104 | tf_op jit(solution)/shard_map/ppermute | solution.py:327
  65.6 0.9 %collective-permute-done.15.refs_2_.refs_6_ = bf16[256,256]{1,0:T(8,128)(2,1)S(1)} collective-permute-done((bf16[256,256]{1,0:T(8,128)(2,1)S(1)}, bf16[256,256]{1,0:T(8,128)(2,1)S(1)}, u32[]{:S(2)}, u32[]{:S(2)}) %collective-permute-start.15) | collective-permute-done | bytes 131104 | tf_op jit(solution)/shard_map/ppermute | solution.py:327
  66.4 0.7 %collective-permute-done.14.refs_1_.refs_5_ = bf16[256,256]{1,0:T(8,128)(2,1)S(1)} collective-permute-done((bf16[256,256]{1,0:T(8,128)(2,1)S(1)}, bf16[256,256]{1,0:T(8,128)(2,1)S(1)}, u32[]{:S(2)}, u32[]{:S(2)}) %collective-permute-start.14) | collective-permute-done | bytes 131104 | tf_op jit(solution)/shard_map/ppermute | solution.py:327
  67.3 1.3 %weight_assemble.1.refs_1_ = bf16[4096,256]{1,0:T(8,128)(2,1)} custom-call(bf16[256,256]{1,0:T(8,128)(2,1)S(1)} %weight_finish.1.refs_0_, bf16[256,256]{1,0:T(8,128)(2,1)S(1)} %collective-permute-done.18.refs_1_, bf16[256,256]{1,0:T(8,128)(2,1)S(1)} %collective-permute-done.19.refs_2_, bf16[256,256]{1,0:T(8,128)(2,1)S(1)} %collective-permute-done.20.refs_3_, ...), custom_call_target="tpu_custom_call" | custom-call | tf_op jit(solution)/shard_map/weight_assemble/pallas_call | solution.py:313
  68.6 0.6 collective-permute-done.17.refs_0_
  69.2 0.8 %weight_complete.1 = bf16[4096,256]{1,0:T(8,128)(2,1)} custom-call(bf16[1024,256]{1,0:T(8,128)(2,1)S(1)} %collective-permute-done.17.refs_0_, bf16[4096,256]{1,0:T(8,128)(2,1)} %weight_assemble.1.refs_1_), custom_call_target="tpu_custom_call", output_to_operand_aliasing={{}: (1, {})} | custom-call | tf_op jit(solution)/shard_map/weight_complete/pallas_call | solution.py:313
  (41 shorter events, 3.9 us)
Async XLA Ops:
  0.6 1.6 %copy-start = (bf16[1,256,4096]{2,1,0:T(8,128)(2,1)S(1)}, bf16[1,256,4096]{2,1,0:T(8,128)(2,1)}, u32[]{:S(2)}) copy-start(bf16[1,256,4096]{2,1,0:T(8,128)(2,1)} %param.6) | copy-start | bytes 6291460
  2.2 5.1 %copy-start.2 = (bf16[4096,256]{1,0:T(8,128)(2,1)S(1)}, bf16[4096,256]{1,0:T(8,128)(2,1)}, u32[]{:S(2)}) copy-start(bf16[4096,256]{1,0:T(8,128)(2,1)} %w_ref.1) | copy-start | bytes 6291460
  2.7 17.3 %collective-permute-start.2 = (bf16[256,1024]{1,0:T(8,128)(2,1)S(1)}, bf16[256,1024]{1,0:T(8,128)(2,1)S(1)}, u32[]{:S(2)}, u32[]{:S(2)}) collective-permute-start(bf16[256,1024]{1,0:T(8,128)(2,1)S(1)} %get-tuple-element.25), channel_id=1, source_target_pairs={{0,4},{2,6},{4,0},{6,2},{8,12},{10,14},{12,8},{14,10},{16,20},{18,... | collective-permute-start | bytes 1572872 | tf_op jit(solution)/shard_map/ppermute | solution.py:327
  5.7 9.9 %copy-start.3 = (bf16[1,128,1024]{2,1,0:T(8,128)(2,1)S(1)}, bf16[1,128,1024]{2,1,0:T(8,128)(2,1)}, u32[]{:S(2)}) copy-start(bf16[1,128,1024]{2,1,0:T(8,128)(2,1)} %param.7) | copy-start | bytes 786436
  5.7 9.9 %copy-start.4 = (bf16[1,128,1024]{2,1,0:T(8,128)(2,1)S(1)}, bf16[1,128,1024]{2,1,0:T(8,128)(2,1)}, u32[]{:S(2)}) copy-start(bf16[1,128,1024]{2,1,0:T(8,128)(2,1)} %param.8) | copy-start | bytes 786436
  5.7 9.9 %copy-start.5 = (s32[1,256]{1,0:T(1,128)S(1)}, s32[1,256]{1,0:T(1,128)}, u32[]{:S(2)}) copy-start(s32[1,256]{1,0:T(1,128)} %param.10) | copy-start | bytes 3076
  5.7 9.9 %copy-start.6 = (s32[2]{0:T(128)S(1)}, s32[2]{0:T(128)}, u32[]{:S(2)}) copy-start(s32[2]{0:T(128)} %order_ref.1) | copy-start | bytes 28
  5.7 14.3 %collective-permute-start.3 = (bf16[256,1024]{1,0:T(8,128)(2,1)S(1)}, bf16[256,1024]{1,0:T(8,128)(2,1)S(1)}, u32[]{:S(2)}, u32[]{:S(2)}) collective-permute-start(bf16[256,1024]{1,0:T(8,128)(2,1)S(1)} %get-tuple-element.26), channel_id=1, source_target_pairs={{0,8},{2,10},{4,12},{6,14},{8,0},{10,2},{12,4},{14,6},{16,24},{18,... | collective-permute-start | bytes 1572872 | tf_op jit(solution)/shard_map/ppermute | solution.py:327
  8.1 6.1 %collective-permute-start = (f32[256,128]{1,0:T(8,128)S(1)}, f32[256,128]{1,0:T(8,128)S(1)}, u32[]{:S(2)}, u32[]{:S(2)}) collective-permute-start(f32[256,128]{1,0:T(8,128)S(1)} %get-tuple-element.20.refs_0_), channel_id=1, source_target_pairs={{0,1},{1,0},{2,3},{3,2},{4,5},{5,4},{6,7},{7,6},{8,9},{9,8},{10,11... | collective-permute-start | bytes 393224 | tf_op jit(solution)/shard_map/ppermute | solution.py:342
  9.6 6.0 %collective-permute-start.1 = (f32[256,128]{1,0:T(8,128)S(1)}, f32[256,128]{1,0:T(8,128)S(1)}, u32[]{:S(2)}, u32[]{:S(2)}) collective-permute-start(f32[256,128]{1,0:T(8,128)S(1)} %get-tuple-element.21.refs_2_), channel_id=1, source_target_pairs={{0,1},{1,0},{2,3},{3,2},{4,5},{5,4},{6,7},{7,6},{8,9},{9,8},{10,11... | collective-permute-start | bytes 393224 | tf_op jit(solution)/shard_map/ppermute | solution.py:342
  17.5 6.6 %collective-permute-start.5 = (f32[256,256]{1,0:T(8,128)S(1)}, f32[256,256]{1,0:T(8,128)S(1)}, u32[]{:S(2)}, u32[]{:S(2)}) collective-permute-start(f32[256,256]{1,0:T(8,128)S(1)} %get-tuple-element.30.a_ref), channel_id=1, source_target_pairs={{0,1},{1,0},{2,3},{3,2},{4,5},{5,4},{6,7},{7,6},{8,9},{9,8},{10,11... | collective-permute-start | bytes 786440 | tf_op jit(solution)/shard_map/ppermute | solution.py:347
  19.0 8.7 %collective-permute-start.9 = (bf16[256,512]{1,0:T(8,128)(2,1)S(1)}, bf16[256,512]{1,0:T(8,128)(2,1)S(1)}, u32[]{:S(2)}, u32[]{:S(2)}) collective-permute-start(bf16[256,512]{1,0:T(8,128)(2,1)S(1)} %get-tuple-element.33), channel_id=1, source_target_pairs={{0,12},{2,14},{4,8},{6,10},{8,4},{10,6},{12,0},{14,2},{16,28},{18,... | collective-permute-start | bytes 786440 | tf_op jit(solution)/shard_map/ppermute | solution.py:327
  20.0 12.4 %copy-start.1 = (bf16[1,256,4096]{2,1,0:T(8,128)(2,1)S(1)}, bf16[1,256,4096]{2,1,0:T(8,128)(2,1)}, u32[]{:S(2)}) copy-start(bf16[1,256,4096]{2,1,0:T(8,128)(2,1)} %param.6) | copy-start | bytes 6291460
  24.1 6.5 %collective-permute-start.8 = (bf16[256,256]{1,0:T(8,128)(2,1)S(1)}, bf16[256,256]{1,0:T(8,128)(2,1)S(1)}, u32[]{:S(2)}, u32[]{:S(2)}) collective-permute-start(bf16[256,256]{1,0:T(8,128)(2,1)S(1)} %round_grad.1.refs_4_), channel_id=1, source_target_pairs={{0,12},{2,14},{4,8},{6,10},{8,4},{10,6},{12,0},{14,2},{16,28},{18,... | collective-permute-start | bytes 393224 | tf_op jit(solution)/shard_map/ppermute | solution.py:327
  25.8 5.2 %collective-permute-start.7 = (bf16[256,256]{1,0:T(8,128)(2,1)S(1)}, bf16[256,256]{1,0:T(8,128)(2,1)S(1)}, u32[]{:S(2)}, u32[]{:S(2)}) collective-permute-start(bf16[256,256]{1,0:T(8,128)(2,1)S(1)} %round_grad.1.refs_4_), channel_id=1, source_target_pairs={{0,8},{2,10},{4,12},{6,14},{8,0},{10,2},{12,4},{14,6},{16,24},{18,... | collective-permute-start | bytes 393224 | tf_op jit(solution)/shard_map/ppermute | solution.py:327
  26.1 5.8 %collective-permute-start.6 = (bf16[256,256]{1,0:T(8,128)(2,1)S(1)}, bf16[256,256]{1,0:T(8,128)(2,1)S(1)}, u32[]{:S(2)}, u32[]{:S(2)}) collective-permute-start(bf16[256,256]{1,0:T(8,128)(2,1)S(1)} %round_grad.1.refs_4_), channel_id=1, source_target_pairs={{0,4},{2,6},{4,0},{6,2},{8,12},{10,14},{12,8},{14,10},{16,20},{18,... | collective-permute-start | bytes 393224 | tf_op jit(solution)/shard_map/ppermute | solution.py:327
  32.4 1.8 %collective-permute-start.10 = (f32[256,256]{1,0:T(8,128)S(1)}, f32[256,256]{1,0:T(8,128)S(1)}, u32[]{:S(2)}, u32[]{:S(2)}) collective-permute-start(f32[256,256]{1,0:T(8,128)S(1)} %get-tuple-element.35), channel_id=1, source_target_pairs={{0,2},{2,0},{4,6},{6,4},{8,10},{10,8},{12,14},{14,12},{16,18},{18,... | collective-permute-start | bytes 786440 | tf_op jit(solution)/shard_map/ppermute | solution.py:327
  32.5 15.3 %collective-permute-start.4 = (bf16[256,512]{1,0:T(8,128)(2,1)S(1)}, bf16[256,512]{1,0:T(8,128)(2,1)S(1)}, u32[]{:S(2)}, u32[]{:S(2)}) collective-permute-start(bf16[256,512]{1,0:T(8,128)(2,1)S(1)} %slice_near_diagonal.1), channel_id=1, source_target_pairs={{0,12},{2,14},{4,8},{6,10},{8,4},{10,6},{12,0},{14,2},{16,28},{18,... | collective-permute-start | bytes 786440 | tf_op jit(solution)/shard_map/ppermute | solution.py:327
  34.2 15.0 %collective-permute-start.11 = (f32[256,256]{1,0:T(8,128)S(1)}, f32[256,256]{1,0:T(8,128)S(1)}, u32[]{:S(2)}, u32[]{:S(2)}) collective-permute-start(f32[256,256]{1,0:T(8,128)S(1)} %weight_fold.2), channel_id=1, source_target_pairs={{0,16},{2,18},{4,20},{6,22},{8,24},{10,26},{12,28},{14,30},{16,0},... | collective-permute-start | bytes 786440 | tf_op jit(solution)/shard_map/ppermute | solution.py:327
  48.3 1.6 %collective-permute-start.12 = (f32[256,256]{1,0:T(8,128)S(1)}, f32[256,256]{1,0:T(8,128)S(1)}, u32[]{:S(2)}, u32[]{:S(2)}) collective-permute-start(f32[256,256]{1,0:T(8,128)S(1)} %get-tuple-element.36), channel_id=1, source_target_pairs={{0,2},{2,0},{4,6},{6,4},{8,10},{10,8},{12,14},{14,12},{16,18},{18,... | collective-permute-start | bytes 786440 | tf_op jit(solution)/shard_map/ppermute | solution.py:327
  50.0 8.3 %collective-permute-start.13 = (bf16[256,256]{1,0:T(8,128)(2,1)S(1)}, bf16[256,256]{1,0:T(8,128)(2,1)S(1)}, u32[]{:S(2)}, u32[]{:S(2)}) collective-permute-start(bf16[256,256]{1,0:T(8,128)(2,1)S(1)} %weight_finish.1.refs_0_), channel_id=1, source_target_pairs={{0,16},{2,18},{4,20},{6,22},{8,24},{10,26},{12,28},{14,30},{16,0},... | collective-permute-start | bytes 393224 | tf_op jit(solution)/shard_map/ppermute | solution.py:327
  50.1 10.0 %collective-permute-start.20 = (bf16[256,256]{1,0:T(8,128)(2,1)S(1)}, bf16[256,256]{1,0:T(8,128)(2,1)S(1)}, u32[]{:S(2)}, u32[]{:S(2)}) collective-permute-start(bf16[256,256]{1,0:T(8,128)(2,1)S(1)} %weight_finish.1.refs_0_), channel_id=1, source_target_pairs={{0,12},{2,14},{4,8},{6,10},{8,4},{10,6},{12,0},{14,2},{16,28},{18,... | collective-permute-start | bytes 393224 | tf_op jit(solution)/shard_map/ppermute | solution.py:327
  53.4 8.4 %collective-permute-start.19 = (bf16[256,256]{1,0:T(8,128)(2,1)S(1)}, bf16[256,256]{1,0:T(8,128)(2,1)S(1)}, u32[]{:S(2)}, u32[]{:S(2)}) collective-permute-start(bf16[256,256]{1,0:T(8,128)(2,1)S(1)} %weight_finish.1.refs_0_), channel_id=1, source_target_pairs={{0,4},{2,6},{4,0},{6,2},{8,12},{10,14},{12,8},{14,10},{16,20},{18,... | collective-permute-start | bytes 393224 | tf_op jit(solution)/shard_map/ppermute | solution.py:327
  54.1 7.6 %collective-permute-start.18 = (bf16[256,256]{1,0:T(8,128)(2,1)S(1)}, bf16[256,256]{1,0:T(8,128)(2,1)S(1)}, u32[]{:S(2)}, u32[]{:S(2)}) collective-permute-start(bf16[256,256]{1,0:T(8,128)(2,1)S(1)} %weight_finish.1.refs_0_), channel_id=1, source_target_pairs={{0,8},{2,10},{4,12},{6,14},{8,0},{10,2},{12,4},{14,6},{16,24},{18,... | collective-permute-start | bytes 393224 | tf_op jit(solution)/shard_map/ppermute | solution.py:327
  58.3 7.3 %collective-permute-start.16 = (bf16[256,256]{1,0:T(8,128)(2,1)S(1)}, bf16[256,256]{1,0:T(8,128)(2,1)S(1)}, u32[]{:S(2)}, u32[]{:S(2)}) collective-permute-start(bf16[256,256]{1,0:T(8,128)(2,1)S(1)} %collective-permute-done.13.refs_0_.refs_4_), channel_id=1, source_target_pairs={{0,12},{2,14},{4,8},{6,10},{8,4},{10,6},{12,0},{14,2},{16,28},{18,... | collective-permute-start | bytes 393224 | tf_op jit(solution)/shard_map/ppermute | solution.py:327
  58.3 8.2 %collective-permute-start.15 = (bf16[256,256]{1,0:T(8,128)(2,1)S(1)}, bf16[256,256]{1,0:T(8,128)(2,1)S(1)}, u32[]{:S(2)}, u32[]{:S(2)}) collective-permute-start(bf16[256,256]{1,0:T(8,128)(2,1)S(1)} %collective-permute-done.13.refs_0_.refs_4_), channel_id=1, source_target_pairs={{0,4},{2,6},{4,0},{6,2},{8,12},{10,14},{12,8},{14,10},{16,20},{18,... | collective-permute-start | bytes 393224 | tf_op jit(solution)/shard_map/ppermute | solution.py:327
  60.1 7.1 %collective-permute-start.14 = (bf16[256,256]{1,0:T(8,128)(2,1)S(1)}, bf16[256,256]{1,0:T(8,128)(2,1)S(1)}, u32[]{:S(2)}, u32[]{:S(2)}) collective-permute-start(bf16[256,256]{1,0:T(8,128)(2,1)S(1)} %collective-permute-done.13.refs_0_.refs_4_), channel_id=1, source_target_pairs={{0,8},{2,10},{4,12},{6,14},{8,0},{10,2},{12,4},{14,6},{16,24},{18,... | collective-permute-start | bytes 393224 | tf_op jit(solution)/shard_map/ppermute | solution.py:327
  61.8 5.5 %collective-permute-start.21 = (bf16[1024,256]{1,0:T(8,128)(2,1)S(1)}, bf16[1024,256]{1,0:T(8,128)(2,1)S(1)}, u32[]{:S(2)}, u32[]{:S(2)}) collective-permute-start(bf16[1024,256]{1,0:T(8,128)(2,1)S(1)} %stack.3), channel_id=1, source_target_pairs={{0,2},{2,0},{4,6},{6,4},{8,10},{10,8},{12,14},{14,12},{16,18},{18,... | collective-permute-start | bytes 1572872 | tf_op jit(solution)/shard_map/ppermute | solution.py:327
  67.2 2.0 %collective-permute-start.17 = (bf16[1024,256]{1,0:T(8,128)(2,1)S(1)}, bf16[1024,256]{1,0:T(8,128)(2,1)S(1)}, u32[]{:S(2)}, u32[]{:S(2)}) collective-permute-start(bf16[1024,256]{1,0:T(8,128)(2,1)S(1)} %stack.2), channel_id=1, source_target_pairs={{0,2},{2,0},{4,6},{6,4},{8,10},{10,8},{12,14},{14,12},{16,18},{18,... | collective-permute-start | bytes 1572872 | tf_op jit(solution)/shard_map/ppermute | solution.py:327

commit v7 on v6

--- a/solution.py
+++ b/solution.py
@@ -11,7 +11,7 @@
 HEAD = 128
 LOG2E = math.log2(math.e)
 QH = 8
-GROUP = 4
+GROUP = 8
 F32 = jnp.float32
 BF16 = jnp.bfloat16
 NT = (((1,), (1,)), ((), ()))

time: 70.2 us -> 70.2 us (level)
  transfers between devices with their start and end apart: 22 -> 22, of which waited for: 15 -> 14; matrix products, arithmetic and copies ran while one was open for 0% -> 0% of each run, Pallas kernels for 8% -> 8%
where the time goes in v7:
time: 70.2 us; the launch traced here: 70 us
  waiting for transfers between devices  35.5 us (51%)
  starting transfers between devices  24.5 us (35%)
  Pallas kernels  7.54 us (11%)
  local copies, waits for them, and re-layouts  1.61 us (2%)
  between operations  0.82 us (1%)
    ppermute x19, waiting for transfers between devices, hop(): return lax.ppermute(value, 'dp', [(i, i ^ bits) for i in range(count)])  27.3 us
    ppermute x19, starting transfers between devices, hop(): return lax.ppermute(value, 'dp', [(i, i ^ bits) for i in range(count)])  20.9 us
    ppermute x1, waiting for transfers between devices, per_device_16x2(): lax.ppermute(keys, 'seq', swap)  4.06 us
    ppermute x1, waiting for transfers between devices, per_device_16x2(): grad = round_grad(terms, lax.ppermute(terms, 'seq', swap), [done])  2.78 us
    pallas_call x2, Pallas kernels, assemble(): pl.pallas_call(functools.partial(assemble_kernel, held, rows), out_shape=...  2.08 us
    pallas_call x1, Pallas kernels, attend(): pl.pallas_call(functools.partial(terms_kernel, len(kvs), 'seq'), out_shap...  1.8 us
    unnamed x14, local copies, waits for them, and re-layouts  1.61 us
    ppermute x1, starting transfers between devices, per_device_16x2(): lax.ppermute(keys, 'seq', swap)  1.56 us
  transfers between devices with their start and end apart: 22, of which 14 were waited for; matrix products, arithmetic and copies ran while one was open for 0% of the time, Pallas kernels for 8%

profile of v7, /device:TPU:0, one launch (start us, length us, event | category | flops | bytes accessed | tf_op | source)
XLA Modules:
  0.0 70.0 jit_solution(1645587199747741504)
XLA Ops:
  0.6 1.6 %copy-done = bf16[1,256,4096]{2,1,0:T(8,128)(2,1)S(1)} copy-done((bf16[1,256,4096]{2,1,0:T(8,128)(2,1)S(1)}, bf16[1,256,4096]{2,1,0:T(8,128)(2,1)}, u32[]{:S(2)}) %copy-start) | copy-done | bytes 2097176
  2.7 3.0 %collective-permute-start.2 = (bf16[256,1024]{1,0:T(8,128)(2,1)S(1)}, bf16[256,1024]{1,0:T(8,128)(2,1)S(1)}, u32[]{:S(2)}, u32[]{:S(2)}) collective-permute-start(bf16[256,1024]{1,0:T(8,128)(2,1)S(1)} %get-tuple-element.25), channel_id=1, source_target_pairs={{0,4},{2,6},{4,0},{6,2},{8,12},{10,14},{12,8},{14,10},{16,20},{18,... | collective-permute-start | bytes 1572872 | tf_op jit(solution)/shard_map/ppermute | solution.py:327
  5.7 1.6 %collective-permute-start.3 = (bf16[256,1024]{1,0:T(8,128)(2,1)S(1)}, bf16[256,1024]{1,0:T(8,128)(2,1)S(1)}, u32[]{:S(2)}, u32[]{:S(2)}) collective-permute-start(bf16[256,1024]{1,0:T(8,128)(2,1)S(1)} %get-tuple-element.26), channel_id=1, source_target_pairs={{0,8},{2,10},{4,12},{6,14},{8,0},{10,2},{12,4},{14,6},{16,24},{18,... | collective-permute-start | bytes 1572872 | tf_op jit(solution)/shard_map/ppermute | solution.py:327
  7.4 0.7 %project.1 = (f32[256,128]{1,0:T(8,128)S(1)}, f32[256,128]{1,0:T(8,128)S(1)}) custom-call(bf16[256,4096]{1,0:T(8,128)(2,1)S(1)} %bitcast.7, bf16[4096,256]{1,0:T(8,128)(2,1)S(1)} %copy-done.2), custom_call_target="tpu_custom_call" | custom-call | tf_op jit(solution)/shard_map/project/pallas_call | solution.py:183
  8.1 1.6 %collective-permute-start = (f32[256,128]{1,0:T(8,128)S(1)}, f32[256,128]{1,0:T(8,128)S(1)}, u32[]{:S(2)}, u32[]{:S(2)}) collective-permute-start(f32[256,128]{1,0:T(8,128)S(1)} %get-tuple-element.20.refs_0_), channel_id=1, source_target_pairs={{0,1},{1,0},{2,3},{3,2},{4,5},{5,4},{6,7},{7,6},{8,9},{9,8},{10,11... | collective-permute-start | bytes 393224 | tf_op jit(solution)/shard_map/ppermute | solution.py:342
  10.2 4.1 %collective-permute-done.refs_1_ = f32[256,128]{1,0:T(8,128)S(1)} collective-permute-done((f32[256,128]{1,0:T(8,128)S(1)}, f32[256,128]{1,0:T(8,128)S(1)}, u32[]{:S(2)}, u32[]{:S(2)}) %collective-permute-start) | collective-permute-done | bytes 131104 | tf_op jit(solution)/shard_map/ppermute | solution.py:342
  14.2 1.4 %collective-permute-done.1.refs_3_ = f32[256,128]{1,0:T(8,128)S(1)} collective-permute-done((f32[256,128]{1,0:T(8,128)S(1)}, f32[256,128]{1,0:T(8,128)S(1)}, u32[]{:S(2)}, u32[]{:S(2)}) %collective-permute-start.1) | collective-permute-done | bytes 131104 | tf_op jit(solution)/shard_map/ppermute | solution.py:342
  15.6 1.8 %attention_terms.1 = (bf16[256,256]{1,0:T(8,128)(2,1)S(1)}, bf16[256,1024]{1,0:T(8,128)(2,1)S(1)}, bf16[256,1024]{1,0:T(8,128)(2,1)S(1)}, f32[256,256]{1,0:T(8,128)S(1)}) custom-call(s32[2]{0:T(128)S(1)} %copy-done.6, s32[2,128]{1,0:T(2,128)S(1)} %bitcast.11, bf16[128,1024]{1,0:T(8,128)(2,1)S(1)} %bitcast.9, bf16[128,1024]{1,0:T(8,128)(2,1)S(1)} %bitcast.10, ...), custom_call_target="tpu_custom_call" | custom-call | tf_op jit(solution)/shard_map/attention_terms/pallas_call | solution.py:103
  17.4 1.6 %collective-permute-start.5 = (f32[256,256]{1,0:T(8,128)S(1)}, f32[256,256]{1,0:T(8,128)S(1)}, u32[]{:S(2)}, u32[]{:S(2)}) collective-permute-start(f32[256,256]{1,0:T(8,128)S(1)} %get-tuple-element.30.a_ref), channel_id=1, source_target_pairs={{0,1},{1,0},{2,3},{3,2},{4,5},{5,4},{6,7},{7,6},{8,9},{9,8},{10,11... | collective-permute-start | bytes 786440 | tf_op jit(solution)/shard_map/ppermute | solution.py:347
  19.0 1.0 %collective-permute-start.9 = (bf16[256,512]{1,0:T(8,128)(2,1)S(1)}, bf16[256,512]{1,0:T(8,128)(2,1)S(1)}, u32[]{:S(2)}, u32[]{:S(2)}) collective-permute-start(bf16[256,512]{1,0:T(8,128)(2,1)S(1)} %get-tuple-element.33), channel_id=1, source_target_pairs={{0,12},{2,14},{4,8},{6,10},{8,4},{10,6},{12,0},{14,2},{16,28},{18,... | collective-permute-start | bytes 786440 | tf_op jit(solution)/shard_map/ppermute | solution.py:327
  20.0 1.3 %attention_outputs.1 = (bf16[128,1024]{1,0:T(8,128)(2,1)}, bf16[128,1024]{1,0:T(8,128)(2,1)}, f32[8,128]{1,0:T(8,128)S(1)}) custom-call(bf16[256,256]{1,0:T(8,128)(2,1)S(1)} %get-tuple-element.22.kv_ref, bf16[256,1024]{1,0:T(8,128)(2,1)S(1)} %get-tuple-element.23.low_ref, bf16[256,1024]{1,0:T(8,128)(2,1)S(1)} %get-tuple-element.24.ds_ref, ...), custom_call_target="tpu_custom_call" | custom-call | tf_op jit(solution)/shard_map/attention_outputs/pallas_call | solution.py:116
  21.3 2.8 %collective-permute-done.5.b_ref = f32[256,256]{1,0:T(8,128)S(1)} collective-permute-done((f32[256,256]{1,0:T(8,128)S(1)}, f32[256,256]{1,0:T(8,128)S(1)}, u32[]{:S(2)}, u32[]{:S(2)}) %collective-permute-start.5) | collective-permute-done | bytes 262176 | tf_op jit(solution)/shard_map/ppermute | solution.py:347
  24.1 1.7 %collective-permute-start.8 = (bf16[256,256]{1,0:T(8,128)(2,1)S(1)}, bf16[256,256]{1,0:T(8,128)(2,1)S(1)}, u32[]{:S(2)}, u32[]{:S(2)}) collective-permute-start(bf16[256,256]{1,0:T(8,128)(2,1)S(1)} %round_grad.1.refs_4_), channel_id=1, source_target_pairs={{0,12},{2,14},{4,8},{6,10},{8,4},{10,6},{12,0},{14,2},{16,28},{18,... | collective-permute-start | bytes 393224 | tf_op jit(solution)/shard_map/ppermute | solution.py:327
  26.1 1.5 %collective-permute-start.6 = (bf16[256,256]{1,0:T(8,128)(2,1)S(1)}, bf16[256,256]{1,0:T(8,128)(2,1)S(1)}, u32[]{:S(2)}, u32[]{:S(2)}) collective-permute-start(bf16[256,256]{1,0:T(8,128)(2,1)S(1)} %round_grad.1.refs_4_), channel_id=1, source_target_pairs={{0,4},{2,6},{4,0},{6,2},{8,12},{10,14},{12,8},{14,10},{16,20},{18,... | collective-permute-start | bytes 393224 | tf_op jit(solution)/shard_map/ppermute | solution.py:327
  27.7 2.9 %collective-permute-done.8.refs_7_ = bf16[256,256]{1,0:T(8,128)(2,1)S(1)} collective-permute-done((bf16[256,256]{1,0:T(8,128)(2,1)S(1)}, bf16[256,256]{1,0:T(8,128)(2,1)S(1)}, u32[]{:S(2)}, u32[]{:S(2)}) %collective-permute-start.8) | collective-permute-done | bytes 131104 | tf_op jit(solution)/shard_map/ppermute | solution.py:327
  30.9 1.0 %collective-permute-done.6.refs_5_ = bf16[256,256]{1,0:T(8,128)(2,1)S(1)} collective-permute-done((bf16[256,256]{1,0:T(8,128)(2,1)S(1)}, bf16[256,256]{1,0:T(8,128)(2,1)S(1)}, u32[]{:S(2)}, u32[]{:S(2)}) %collective-permute-start.6) | collective-permute-done | bytes 131104 | tf_op jit(solution)/shard_map/ppermute | solution.py:327
  32.5 1.6 %collective-permute-start.4 = (bf16[256,512]{1,0:T(8,128)(2,1)S(1)}, bf16[256,512]{1,0:T(8,128)(2,1)S(1)}, u32[]{:S(2)}, u32[]{:S(2)}) collective-permute-start(bf16[256,512]{1,0:T(8,128)(2,1)S(1)} %slice_near_diagonal.1), channel_id=1, source_target_pairs={{0,12},{2,14},{4,8},{6,10},{8,4},{10,6},{12,0},{14,2},{16,28},{18,... | collective-permute-start | bytes 786440 | tf_op jit(solution)/shard_map/ppermute | solution.py:327
  34.2 2.7 %collective-permute-start.11 = (f32[256,256]{1,0:T(8,128)S(1)}, f32[256,256]{1,0:T(8,128)S(1)}, u32[]{:S(2)}, u32[]{:S(2)}) collective-permute-start(f32[256,256]{1,0:T(8,128)S(1)} %weight_fold.2), channel_id=1, source_target_pairs={{0,16},{2,18},{4,20},{6,22},{8,24},{10,26},{12,28},{14,30},{16,0},... | collective-permute-start | bytes 786440 | tf_op jit(solution)/shard_map/ppermute | solution.py:327
  36.8 11.0 %collective-permute-done.4.refs_3_ = bf16[256,512]{1,0:T(8,128)(2,1)S(1)} collective-permute-done((bf16[256,512]{1,0:T(8,128)(2,1)S(1)}, bf16[256,512]{1,0:T(8,128)(2,1)S(1)}, u32[]{:S(2)}, u32[]{:S(2)}) %collective-permute-start.4) | collective-permute-done | bytes 262176 | tf_op jit(solution)/shard_map/ppermute | solution.py:327
  48.4 1.5 %collective-permute-done.12.b_ref = f32[256,256]{1,0:T(8,128)S(1)} collective-permute-done((f32[256,256]{1,0:T(8,128)S(1)}, f32[256,256]{1,0:T(8,128)S(1)}, u32[]{:S(2)}, u32[]{:S(2)}) %collective-permute-start.12) | collective-permute-done | bytes 262176 | tf_op jit(solution)/shard_map/ppermute | solution.py:327
  50.0 3.4 %collective-permute-start.20 = (bf16[256,256]{1,0:T(8,128)(2,1)S(1)}, bf16[256,256]{1,0:T(8,128)(2,1)S(1)}, u32[]{:S(2)}, u32[]{:S(2)}) collective-permute-start(bf16[256,256]{1,0:T(8,128)(2,1)S(1)} %weight_finish.1.refs_0_), channel_id=1, source_target_pairs={{0,12},{2,14},{4,8},{6,10},{8,4},{10,6},{12,0},{14,2},{16,28},{18,... | collective-permute-start | bytes 393224 | tf_op jit(solution)/shard_map/ppermute | solution.py:327
  53.4 0.7 %collective-permute-start.19 = (bf16[256,256]{1,0:T(8,128)(2,1)S(1)}, bf16[256,256]{1,0:T(8,128)(2,1)S(1)}, u32[]{:S(2)}, u32[]{:S(2)}) collective-permute-start(bf16[256,256]{1,0:T(8,128)(2,1)S(1)} %weight_finish.1.refs_0_), channel_id=1, source_target_pairs={{0,4},{2,6},{4,0},{6,2},{8,12},{10,14},{12,8},{14,10},{16,20},{18,... | collective-permute-start | bytes 393224 | tf_op jit(solution)/shard_map/ppermute | solution.py:327
  54.1 4.1 %collective-permute-done.13.refs_0_.refs_4_ = bf16[256,256]{1,0:T(8,128)(2,1)S(1)} collective-permute-done((bf16[256,256]{1,0:T(8,128)(2,1)S(1)}, bf16[256,256]{1,0:T(8,128)(2,1)S(1)}, u32[]{:S(2)}, u32[]{:S(2)}) %collective-permute-start.13) | collective-permute-done | bytes 131104 | tf_op jit(solution)/shard_map/ppermute | solution.py:327
  58.2 1.3 %collective-permute-start.15 = (bf16[256,256]{1,0:T(8,128)(2,1)S(1)}, bf16[256,256]{1,0:T(8,128)(2,1)S(1)}, u32[]{:S(2)}, u32[]{:S(2)}) collective-permute-start(bf16[256,256]{1,0:T(8,128)(2,1)S(1)} %collective-permute-done.13.refs_0_.refs_4_), channel_id=1, source_target_pairs={{0,4},{2,6},{4,0},{6,2},{8,12},{10,14},{12,8},{14,10},{16,20},{18,... | collective-permute-start | bytes 393224 | tf_op jit(solution)/shard_map/ppermute | solution.py:327
  59.5 0.6 collective-permute-done.20.refs_3_
  60.1 1.7 %collective-permute-start.14 = (bf16[256,256]{1,0:T(8,128)(2,1)S(1)}, bf16[256,256]{1,0:T(8,128)(2,1)S(1)}, u32[]{:S(2)}, u32[]{:S(2)}) collective-permute-start(bf16[256,256]{1,0:T(8,128)(2,1)S(1)} %collective-permute-done.13.refs_0_.refs_4_), channel_id=1, source_target_pairs={{0,8},{2,10},{4,12},{6,14},{8,0},{10,2},{12,4},{14,6},{16,24},{18,... | collective-permute-start | bytes 393224 | tf_op jit(solution)/shard_map/ppermute | solution.py:327
  61.9 3.7 %collective-permute-done.16.refs_3_.refs_7_ = bf16[256,256]{1,0:T(8,128)(2,1)S(1)} collective-permute-done((bf16[256,256]{1,0:T(8,128)(2,1)S(1)}, bf16[256,256]{1,0:T(8,128)(2,1)S(1)}, u32[]{:S(2)}, u32[]{:S(2)}) %collective-permute-start.16) | collective-permute-done | bytes 131104 | tf_op jit(solution)/shard_map/ppermute | solution.py:327
  65.5 0.9 %collective-permute-done.15.refs_2_.refs_6_ = bf16[256,256]{1,0:T(8,128)(2,1)S(1)} collective-permute-done((bf16[256,256]{1,0:T(8,128)(2,1)S(1)}, bf16[256,256]{1,0:T(8,128)(2,1)S(1)}, u32[]{:S(2)}, u32[]{:S(2)}) %collective-permute-start.15) | collective-permute-done | bytes 131104 | tf_op jit(solution)/shard_map/ppermute | solution.py:327
  66.4 0.7 %collective-permute-done.14.refs_1_.refs_5_ = bf16[256,256]{1,0:T(8,128)(2,1)S(1)} collective-permute-done((bf16[256,256]{1,0:T(8,128)(2,1)S(1)}, bf16[256,256]{1,0:T(8,128)(2,1)S(1)}, u32[]{:S(2)}, u32[]{:S(2)}) %collective-permute-start.14) | collective-permute-done | bytes 131104 | tf_op jit(solution)/shard_map/ppermute | solution.py:327
  67.3 1.3 %weight_assemble.1.refs_1_ = bf16[4096,256]{1,0:T(8,128)(2,1)} custom-call(bf16[256,256]{1,0:T(8,128)(2,1)S(1)} %weight_finish.1.refs_0_, bf16[256,256]{1,0:T(8,128)(2,1)S(1)} %collective-permute-done.18.refs_1_, bf16[256,256]{1,0:T(8,128)(2,1)S(1)} %collective-permute-done.19.refs_2_, bf16[256,256]{1,0:T(8,128)(2,1)S(1)} %collective-permute-done.20.refs_3_, ...), custom_call_target="tpu_custom_call" | custom-call | tf_op jit(solution)/shard_map/weight_assemble/pallas_call | solution.py:313
  68.6 0.6 collective-permute-done.17.refs_0_
  69.2 0.8 %weight_complete.1 = bf16[4096,256]{1,0:T(8,128)(2,1)} custom-call(bf16[1024,256]{1,0:T(8,128)(2,1)S(1)} %collective-permute-done.17.refs_0_, bf16[4096,256]{1,0:T(8,128)(2,1)} %weight_assemble.1.refs_1_), custom_call_target="tpu_custom_call", output_to_operand_aliasing={{}: (1, {})} | custom-call | tf_op jit(solution)/shard_map/weight_complete/pallas_call | solution.py:313
  (41 shorter events, 3.3 us)
Async XLA Ops:
  0.6 1.6 %copy-start = (bf16[1,256,4096]{2,1,0:T(8,128)(2,1)S(1)}, bf16[1,256,4096]{2,1,0:T(8,128)(2,1)}, u32[]{:S(2)}) copy-start(bf16[1,256,4096]{2,1,0:T(8,128)(2,1)} %param.6) | copy-start | bytes 6291460
  2.2 5.1 %copy-start.2 = (bf16[4096,256]{1,0:T(8,128)(2,1)S(1)}, bf16[4096,256]{1,0:T(8,128)(2,1)}, u32[]{:S(2)}) copy-start(bf16[4096,256]{1,0:T(8,128)(2,1)} %w_ref.1) | copy-start | bytes 6291460
  2.7 17.3 %collective-permute-start.2 = (bf16[256,1024]{1,0:T(8,128)(2,1)S(1)}, bf16[256,1024]{1,0:T(8,128)(2,1)S(1)}, u32[]{:S(2)}, u32[]{:S(2)}) collective-permute-start(bf16[256,1024]{1,0:T(8,128)(2,1)S(1)} %get-tuple-element.25), channel_id=1, source_target_pairs={{0,4},{2,6},{4,0},{6,2},{8,12},{10,14},{12,8},{14,10},{16,20},{18,... | collective-permute-start | bytes 1572872 | tf_op jit(solution)/shard_map/ppermute | solution.py:327
  5.7 9.9 %copy-start.3 = (bf16[1,128,1024]{2,1,0:T(8,128)(2,1)S(1)}, bf16[1,128,1024]{2,1,0:T(8,128)(2,1)}, u32[]{:S(2)}) copy-start(bf16[1,128,1024]{2,1,0:T(8,128)(2,1)} %param.7) | copy-start | bytes 786436
  5.7 9.9 %copy-start.4 = (bf16[1,128,1024]{2,1,0:T(8,128)(2,1)S(1)}, bf16[1,128,1024]{2,1,0:T(8,128)(2,1)}, u32[]{:S(2)}) copy-start(bf16[1,128,1024]{2,1,0:T(8,128)(2,1)} %param.8) | copy-start | bytes 786436
  5.7 9.9 %copy-start.5 = (s32[1,256]{1,0:T(1,128)S(1)}, s32[1,256]{1,0:T(1,128)}, u32[]{:S(2)}) copy-start(s32[1,256]{1,0:T(1,128)} %param.10) | copy-start | bytes 3076
  5.7 9.9 %copy-start.6 = (s32[2]{0:T(128)S(1)}, s32[2]{0:T(128)}, u32[]{:S(2)}) copy-start(s32[2]{0:T(128)} %order_ref.1) | copy-start | bytes 28
  5.7 14.3 %collective-permute-start.3 = (bf16[256,1024]{1,0:T(8,128)(2,1)S(1)}, bf16[256,1024]{1,0:T(8,128)(2,1)S(1)}, u32[]{:S(2)}, u32[]{:S(2)}) collective-permute-start(bf16[256,1024]{1,0:T(8,128)(2,1)S(1)} %get-tuple-element.26), channel_id=1, source_target_pairs={{0,8},{2,10},{4,12},{6,14},{8,0},{10,2},{12,4},{14,6},{16,24},{18,... | collective-permute-start | bytes 1572872 | tf_op jit(solution)/shard_map/ppermute | solution.py:327
  8.1 6.1 %collective-permute-start = (f32[256,128]{1,0:T(8,128)S(1)}, f32[256,128]{1,0:T(8,128)S(1)}, u32[]{:S(2)}, u32[]{:S(2)}) collective-permute-start(f32[256,128]{1,0:T(8,128)S(1)} %get-tuple-element.20.refs_0_), channel_id=1, source_target_pairs={{0,1},{1,0},{2,3},{3,2},{4,5},{5,4},{6,7},{7,6},{8,9},{9,8},{10,11... | collective-permute-start | bytes 393224 | tf_op jit(solution)/shard_map/ppermute | solution.py:342
  9.6 6.0 %collective-permute-start.1 = (f32[256,128]{1,0:T(8,128)S(1)}, f32[256,128]{1,0:T(8,128)S(1)}, u32[]{:S(2)}, u32[]{:S(2)}) collective-permute-start(f32[256,128]{1,0:T(8,128)S(1)} %get-tuple-element.21.refs_2_), channel_id=1, source_target_pairs={{0,1},{1,0},{2,3},{3,2},{4,5},{5,4},{6,7},{7,6},{8,9},{9,8},{10,11... | collective-permute-start | bytes 393224 | tf_op jit(solution)/shard_map/ppermute | solution.py:342
  17.4 6.6 %collective-permute-start.5 = (f32[256,256]{1,0:T(8,128)S(1)}, f32[256,256]{1,0:T(8,128)S(1)}, u32[]{:S(2)}, u32[]{:S(2)}) collective-permute-start(f32[256,256]{1,0:T(8,128)S(1)} %get-tuple-element.30.a_ref), channel_id=1, source_target_pairs={{0,1},{1,0},{2,3},{3,2},{4,5},{5,4},{6,7},{7,6},{8,9},{9,8},{10,11... | collective-permute-start | bytes 786440 | tf_op jit(solution)/shard_map/ppermute | solution.py:347
  19.0 8.7 %collective-permute-start.9 = (bf16[256,512]{1,0:T(8,128)(2,1)S(1)}, bf16[256,512]{1,0:T(8,128)(2,1)S(1)}, u32[]{:S(2)}, u32[]{:S(2)}) collective-permute-start(bf16[256,512]{1,0:T(8,128)(2,1)S(1)} %get-tuple-element.33), channel_id=1, source_target_pairs={{0,12},{2,14},{4,8},{6,10},{8,4},{10,6},{12,0},{14,2},{16,28},{18,... | collective-permute-start | bytes 786440 | tf_op jit(solution)/shard_map/ppermute | solution.py:327
  20.0 12.4 %copy-start.1 = (bf16[1,256,4096]{2,1,0:T(8,128)(2,1)S(1)}, bf16[1,256,4096]{2,1,0:T(8,128)(2,1)}, u32[]{:S(2)}) copy-start(bf16[1,256,4096]{2,1,0:T(8,128)(2,1)} %param.6) | copy-start | bytes 6291460
  24.1 6.5 %collective-permute-start.8 = (bf16[256,256]{1,0:T(8,128)(2,1)S(1)}, bf16[256,256]{1,0:T(8,128)(2,1)S(1)}, u32[]{:S(2)}, u32[]{:S(2)}) collective-permute-start(bf16[256,256]{1,0:T(8,128)(2,1)S(1)} %round_grad.1.refs_4_), channel_id=1, source_target_pairs={{0,12},{2,14},{4,8},{6,10},{8,4},{10,6},{12,0},{14,2},{16,28},{18,... | collective-permute-start | bytes 393224 | tf_op jit(solution)/shard_map/ppermute | solution.py:327
  25.8 5.2 %collective-permute-start.7 = (bf16[256,256]{1,0:T(8,128)(2,1)S(1)}, bf16[256,256]{1,0:T(8,128)(2,1)S(1)}, u32[]{:S(2)}, u32[]{:S(2)}) collective-permute-start(bf16[256,256]{1,0:T(8,128)(2,1)S(1)} %round_grad.1.refs_4_), channel_id=1, source_target_pairs={{0,8},{2,10},{4,12},{6,14},{8,0},{10,2},{12,4},{14,6},{16,24},{18,... | collective-permute-start | bytes 393224 | tf_op jit(solution)/shard_map/ppermute | solution.py:327
  26.1 5.8 %collective-permute-start.6 = (bf16[256,256]{1,0:T(8,128)(2,1)S(1)}, bf16[256,256]{1,0:T(8,128)(2,1)S(1)}, u32[]{:S(2)}, u32[]{:S(2)}) collective-permute-start(bf16[256,256]{1,0:T(8,128)(2,1)S(1)} %round_grad.1.refs_4_), channel_id=1, source_target_pairs={{0,4},{2,6},{4,0},{6,2},{8,12},{10,14},{12,8},{14,10},{16,20},{18,... | collective-permute-start | bytes 393224 | tf_op jit(solution)/shard_map/ppermute | solution.py:327
  32.3 1.8 %collective-permute-start.10 = (f32[256,256]{1,0:T(8,128)S(1)}, f32[256,256]{1,0:T(8,128)S(1)}, u32[]{:S(2)}, u32[]{:S(2)}) collective-permute-start(f32[256,256]{1,0:T(8,128)S(1)} %get-tuple-element.35), channel_id=1, source_target_pairs={{0,2},{2,0},{4,6},{6,4},{8,10},{10,8},{12,14},{14,12},{16,18},{18,... | collective-permute-start | bytes 786440 | tf_op jit(solution)/shard_map/ppermute | solution.py:327
  32.5 15.3 %collective-permute-start.4 = (bf16[256,512]{1,0:T(8,128)(2,1)S(1)}, bf16[256,512]{1,0:T(8,128)(2,1)S(1)}, u32[]{:S(2)}, u32[]{:S(2)}) collective-permute-start(bf16[256,512]{1,0:T(8,128)(2,1)S(1)} %slice_near_diagonal.1), channel_id=1, source_target_pairs={{0,12},{2,14},{4,8},{6,10},{8,4},{10,6},{12,0},{14,2},{16,28},{18,... | collective-permute-start | bytes 786440 | tf_op jit(solution)/shard_map/ppermute | solution.py:327
  34.2 14.2 %collective-permute-start.11 = (f32[256,256]{1,0:T(8,128)S(1)}, f32[256,256]{1,0:T(8,128)S(1)}, u32[]{:S(2)}, u32[]{:S(2)}) collective-permute-start(f32[256,256]{1,0:T(8,128)S(1)} %weight_fold.2), channel_id=1, source_target_pairs={{0,16},{2,18},{4,20},{6,22},{8,24},{10,26},{12,28},{14,30},{16,0},... | collective-permute-start | bytes 786440 | tf_op jit(solution)/shard_map/ppermute | solution.py:327
  48.3 1.6 %collective-permute-start.12 = (f32[256,256]{1,0:T(8,128)S(1)}, f32[256,256]{1,0:T(8,128)S(1)}, u32[]{:S(2)}, u32[]{:S(2)}) collective-permute-start(f32[256,256]{1,0:T(8,128)S(1)} %get-tuple-element.36), channel_id=1, source_target_pairs={{0,2},{2,0},{4,6},{6,4},{8,10},{10,8},{12,14},{14,12},{16,18},{18,... | collective-permute-start | bytes 786440 | tf_op jit(solution)/shard_map/ppermute | solution.py:327
  50.0 8.3 %collective-permute-start.13 = (bf16[256,256]{1,0:T(8,128)(2,1)S(1)}, bf16[256,256]{1,0:T(8,128)(2,1)S(1)}, u32[]{:S(2)}, u32[]{:S(2)}) collective-permute-start(bf16[256,256]{1,0:T(8,128)(2,1)S(1)} %weight_finish.1.refs_0_), channel_id=1, source_target_pairs={{0,16},{2,18},{4,20},{6,22},{8,24},{10,26},{12,28},{14,30},{16,0},... | collective-permute-start | bytes 393224 | tf_op jit(solution)/shard_map/ppermute | solution.py:327
  50.0 10.0 %collective-permute-start.20 = (bf16[256,256]{1,0:T(8,128)(2,1)S(1)}, bf16[256,256]{1,0:T(8,128)(2,1)S(1)}, u32[]{:S(2)}, u32[]{:S(2)}) collective-permute-start(bf16[256,256]{1,0:T(8,128)(2,1)S(1)} %weight_finish.1.refs_0_), channel_id=1, source_target_pairs={{0,12},{2,14},{4,8},{6,10},{8,4},{10,6},{12,0},{14,2},{16,28},{18,... | collective-permute-start | bytes 393224 | tf_op jit(solution)/shard_map/ppermute | solution.py:327
  53.4 8.3 %collective-permute-start.19 = (bf16[256,256]{1,0:T(8,128)(2,1)S(1)}, bf16[256,256]{1,0:T(8,128)(2,1)S(1)}, u32[]{:S(2)}, u32[]{:S(2)}) collective-permute-start(bf16[256,256]{1,0:T(8,128)(2,1)S(1)} %weight_finish.1.refs_0_), channel_id=1, source_target_pairs={{0,4},{2,6},{4,0},{6,2},{8,12},{10,14},{12,8},{14,10},{16,20},{18,... | collective-permute-start | bytes 393224 | tf_op jit(solution)/shard_map/ppermute | solution.py:327
  54.1 7.6 %collective-permute-start.18 = (bf16[256,256]{1,0:T(8,128)(2,1)S(1)}, bf16[256,256]{1,0:T(8,128)(2,1)S(1)}, u32[]{:S(2)}, u32[]{:S(2)}) collective-permute-start(bf16[256,256]{1,0:T(8,128)(2,1)S(1)} %weight_finish.1.refs_0_), channel_id=1, source_target_pairs={{0,8},{2,10},{4,12},{6,14},{8,0},{10,2},{12,4},{14,6},{16,24},{18,... | collective-permute-start | bytes 393224 | tf_op jit(solution)/shard_map/ppermute | solution.py:327
  58.2 7.3 %collective-permute-start.16 = (bf16[256,256]{1,0:T(8,128)(2,1)S(1)}, bf16[256,256]{1,0:T(8,128)(2,1)S(1)}, u32[]{:S(2)}, u32[]{:S(2)}) collective-permute-start(bf16[256,256]{1,0:T(8,128)(2,1)S(1)} %collective-permute-done.13.refs_0_.refs_4_), channel_id=1, source_target_pairs={{0,12},{2,14},{4,8},{6,10},{8,4},{10,6},{12,0},{14,2},{16,28},{18,... | collective-permute-start | bytes 393224 | tf_op jit(solution)/shard_map/ppermute | solution.py:327
  58.2 8.2 %collective-permute-start.15 = (bf16[256,256]{1,0:T(8,128)(2,1)S(1)}, bf16[256,256]{1,0:T(8,128)(2,1)S(1)}, u32[]{:S(2)}, u32[]{:S(2)}) collective-permute-start(bf16[256,256]{1,0:T(8,128)(2,1)S(1)} %collective-permute-done.13.refs_0_.refs_4_), channel_id=1, source_target_pairs={{0,4},{2,6},{4,0},{6,2},{8,12},{10,14},{12,8},{14,10},{16,20},{18,... | collective-permute-start | bytes 393224 | tf_op jit(solution)/shard_map/ppermute | solution.py:327
  60.1 7.1 %collective-permute-start.14 = (bf16[256,256]{1,0:T(8,128)(2,1)S(1)}, bf16[256,256]{1,0:T(8,128)(2,1)S(1)}, u32[]{:S(2)}, u32[]{:S(2)}) collective-permute-start(bf16[256,256]{1,0:T(8,128)(2,1)S(1)} %collective-permute-done.13.refs_0_.refs_4_), channel_id=1, source_target_pairs={{0,8},{2,10},{4,12},{6,14},{8,0},{10,2},{12,4},{14,6},{16,24},{18,... | collective-permute-start | bytes 393224 | tf_op jit(solution)/shard_map/ppermute | solution.py:327
  61.8 5.5 %collective-permute-start.21 = (bf16[1024,256]{1,0:T(8,128)(2,1)S(1)}, bf16[1024,256]{1,0:T(8,128)(2,1)S(1)}, u32[]{:S(2)}, u32[]{:S(2)}) collective-permute-start(bf16[1024,256]{1,0:T(8,128)(2,1)S(1)} %stack.3), channel_id=1, source_target_pairs={{0,2},{2,0},{4,6},{6,4},{8,10},{10,8},{12,14},{14,12},{16,18},{18,... | collective-permute-start | bytes 1572872 | tf_op jit(solution)/shard_map/ppermute | solution.py:327
  67.2 2.0 %collective-permute-start.17 = (bf16[1024,256]{1,0:T(8,128)(2,1)S(1)}, bf16[1024,256]{1,0:T(8,128)(2,1)S(1)}, u32[]{:S(2)}, u32[]{:S(2)}) collective-permute-start(bf16[1024,256]{1,0:T(8,128)(2,1)S(1)} %stack.2), channel_id=1, source_target_pairs={{0,2},{2,0},{4,6},{6,4},{8,10},{10,8},{12,14},{14,12},{16,18},{18,... | collective-permute-start | bytes 1572872 | tf_op jit(solution)/shard_map/ppermute | solution.py:327

commit v8 on v7

--- a/solution.py
+++ b/solution.py
@@ -342,9 +342,9 @@
     keys_in, values_in = lax.ppermute(keys, "seq", swap), lax.ppermute(values, "seq", swap)
     docs = doc_ids.reshape(-1, rows_dev)
     attention, query_grad, terms, done = attend(
-        span_order, docs, queries[0], grad_out[0], [keys, keys_in, values, values_in], [tok_y, tok_z]
+        span_order, docs, queries[0], grad_out[0], [keys, keys_in, values, values_in], [tok_y]
     )
-    grad = round_grad(terms, lax.ppermute(terms, "seq", swap), [done])
+    grad = round_grad(terms, lax.ppermute(terms, "seq", swap), [done, tok_z])
     grads = [grad] + [hop(grad, bits) for bits in near]
     keep, send = weight_part([own, tok_y, tok_z, far_d], grads, dp_size, [0, 0, 0, 0])
     part = fold(keep, hop(send, CORE))

time: 70.2 us -> 70.1 us (level)
  transfers between devices with their start and end apart: 22 -> 22, of which waited for: 14 -> 15; matrix products, arithmetic and copies ran while one was open for 0% -> 0% of each run, Pallas kernels for 8% -> 8%
where the time goes in v8:
time: 70.1 us; the launch traced here: 70 us
  waiting for transfers between devices  35.6 us (51%)
  starting transfers between devices  24.4 us (35%)
  Pallas kernels  7.53 us (11%)
  local copies, waits for them, and re-layouts  1.61 us (2%)
  between operations  0.81 us (1%)
    ppermute x19, waiting for transfers between devices, hop(): return lax.ppermute(value, 'dp', [(i, i ^ bits) for i in range(count)])  27.4 us
    ppermute x19, starting transfers between devices, hop(): return lax.ppermute(value, 'dp', [(i, i ^ bits) for i in range(count)])  20.8 us
    ppermute x1, waiting for transfers between devices, per_device_16x2(): lax.ppermute(keys, 'seq', swap)  4.06 us
    ppermute x1, waiting for transfers between devices, per_device_16x2(): grad = round_grad(terms, lax.ppermute(terms, 'seq', swap), [done, tok_z])  2.79 us
    pallas_call x2, Pallas kernels, assemble(): pl.pallas_call(functools.partial(assemble_kernel, held, rows), out_shape=...  2.08 us
    pallas_call x1, Pallas kernels, attend(): pl.pallas_call(functools.partial(terms_kernel, len(kvs), 'seq'), out_shap...  1.79 us
    unnamed x14, local copies, waits for them, and re-layouts  1.61 us
    ppermute x1, starting transfers between devices, per_device_16x2(): grad = round_grad(terms, lax.ppermute(terms, 'seq', swap), [done, tok_z])  1.56 us
  transfers between devices with their start and end apart: 22, of which 15 were waited for; matrix products, arithmetic and copies ran while one was open for 0% of the time, Pallas kernels for 8%

profile of v8, /device:TPU:0, one launch (start us, length us, event | category | flops | bytes accessed | tf_op | source)
XLA Modules:
  0.0 70.0 jit_solution(6779663209887072101)
XLA Ops:
  0.6 1.6 %copy-done = bf16[1,256,4096]{2,1,0:T(8,128)(2,1)S(1)} copy-done((bf16[1,256,4096]{2,1,0:T(8,128)(2,1)S(1)}, bf16[1,256,4096]{2,1,0:T(8,128)(2,1)}, u32[]{:S(2)}) %copy-start) | copy-done | bytes 2097176
  2.7 3.0 %collective-permute-start.2 = (bf16[256,1024]{1,0:T(8,128)(2,1)S(1)}, bf16[256,1024]{1,0:T(8,128)(2,1)S(1)}, u32[]{:S(2)}, u32[]{:S(2)}) collective-permute-start(bf16[256,1024]{1,0:T(8,128)(2,1)S(1)} %get-tuple-element.25), channel_id=1, source_target_pairs={{0,4},{2,6},{4,0},{6,2},{8,12},{10,14},{12,8},{14,10},{16,20},{18,... | collective-permute-start | bytes 1572872 | tf_op jit(solution)/shard_map/ppermute | solution.py:327
  5.7 1.6 %collective-permute-start.3 = (bf16[256,1024]{1,0:T(8,128)(2,1)S(1)}, bf16[256,1024]{1,0:T(8,128)(2,1)S(1)}, u32[]{:S(2)}, u32[]{:S(2)}) collective-permute-start(bf16[256,1024]{1,0:T(8,128)(2,1)S(1)} %get-tuple-element.29), channel_id=1, source_target_pairs={{0,8},{2,10},{4,12},{6,14},{8,0},{10,2},{12,4},{14,6},{16,24},{18,... | collective-permute-start | bytes 1572872 | tf_op jit(solution)/shard_map/ppermute | solution.py:327
  7.4 0.7 %project.1 = (f32[256,128]{1,0:T(8,128)S(1)}, f32[256,128]{1,0:T(8,128)S(1)}) custom-call(bf16[256,4096]{1,0:T(8,128)(2,1)S(1)} %bitcast.7, bf16[4096,256]{1,0:T(8,128)(2,1)S(1)} %copy-done.2), custom_call_target="tpu_custom_call" | custom-call | tf_op jit(solution)/shard_map/project/pallas_call | solution.py:183
  8.1 1.6 %collective-permute-start = (f32[256,128]{1,0:T(8,128)S(1)}, f32[256,128]{1,0:T(8,128)S(1)}, u32[]{:S(2)}, u32[]{:S(2)}) collective-permute-start(f32[256,128]{1,0:T(8,128)S(1)} %get-tuple-element.20.refs_0_), channel_id=1, source_target_pairs={{0,1},{1,0},{2,3},{3,2},{4,5},{5,4},{6,7},{7,6},{8,9},{9,8},{10,11... | collective-permute-start | bytes 393224 | tf_op jit(solution)/shard_map/ppermute | solution.py:342
  10.2 4.1 %collective-permute-done.refs_1_ = f32[256,128]{1,0:T(8,128)S(1)} collective-permute-done((f32[256,128]{1,0:T(8,128)S(1)}, f32[256,128]{1,0:T(8,128)S(1)}, u32[]{:S(2)}, u32[]{:S(2)}) %collective-permute-start) | collective-permute-done | bytes 131104 | tf_op jit(solution)/shard_map/ppermute | solution.py:342
  14.2 1.4 %collective-permute-done.1.refs_3_ = f32[256,128]{1,0:T(8,128)S(1)} collective-permute-done((f32[256,128]{1,0:T(8,128)S(1)}, f32[256,128]{1,0:T(8,128)S(1)}, u32[]{:S(2)}, u32[]{:S(2)}) %collective-permute-start.1) | collective-permute-done | bytes 131104 | tf_op jit(solution)/shard_map/ppermute | solution.py:342
  15.6 1.8 %attention_terms.1 = (bf16[256,256]{1,0:T(8,128)(2,1)S(1)}, bf16[256,1024]{1,0:T(8,128)(2,1)S(1)}, bf16[256,1024]{1,0:T(8,128)(2,1)S(1)}, f32[256,256]{1,0:T(8,128)S(1)}) custom-call(s32[2]{0:T(128)S(1)} %copy-done.6, s32[2,128]{1,0:T(2,128)S(1)} %bitcast.11, bf16[128,1024]{1,0:T(8,128)(2,1)S(1)} %bitcast.9, bf16[128,1024]{1,0:T(8,128)(2,1)S(1)} %bitcast.10, ...), custom_call_target="tpu_custom_call" | custom-call | tf_op jit(solution)/shard_map/attention_terms/pallas_call | solution.py:103
  17.4 1.6 %collective-permute-start.5 = (f32[256,256]{1,0:T(8,128)S(1)}, f32[256,256]{1,0:T(8,128)S(1)}, u32[]{:S(2)}, u32[]{:S(2)}) collective-permute-start(f32[256,256]{1,0:T(8,128)S(1)} %get-tuple-element.30.a_ref), channel_id=1, source_target_pairs={{0,1},{1,0},{2,3},{3,2},{4,5},{5,4},{6,7},{7,6},{8,9},{9,8},{10,11... | collective-permute-start | bytes 786440 | tf_op jit(solution)/shard_map/ppermute | solution.py:347
  19.0 1.0 %collective-permute-start.9 = (bf16[256,512]{1,0:T(8,128)(2,1)S(1)}, bf16[256,512]{1,0:T(8,128)(2,1)S(1)}, u32[]{:S(2)}, u32[]{:S(2)}) collective-permute-start(bf16[256,512]{1,0:T(8,128)(2,1)S(1)} %get-tuple-element.33), channel_id=1, source_target_pairs={{0,12},{2,14},{4,8},{6,10},{8,4},{10,6},{12,0},{14,2},{16,28},{18,... | collective-permute-start | bytes 786440 | tf_op jit(solution)/shard_map/ppermute | solution.py:327
  20.0 1.3 %attention_outputs.1 = (bf16[128,1024]{1,0:T(8,128)(2,1)}, bf16[128,1024]{1,0:T(8,128)(2,1)}, f32[8,128]{1,0:T(8,128)S(1)}) custom-call(bf16[256,256]{1,0:T(8,128)(2,1)S(1)} %get-tuple-element.22.kv_ref, bf16[256,1024]{1,0:T(8,128)(2,1)S(1)} %get-tuple-element.23.low_ref, bf16[256,1024]{1,0:T(8,128)(2,1)S(1)} %get-tuple-element.24.ds_ref, ...), custom_call_target="tpu_custom_call" | custom-call | tf_op jit(solution)/shard_map/attention_outputs/pallas_call | solution.py:116
  21.3 2.8 %collective-permute-done.5.b_ref = f32[256,256]{1,0:T(8,128)S(1)} collective-permute-done((f32[256,256]{1,0:T(8,128)S(1)}, f32[256,256]{1,0:T(8,128)S(1)}, u32[]{:S(2)}, u32[]{:S(2)}) %collective-permute-start.5) | collective-permute-done | bytes 262176 | tf_op jit(solution)/shard_map/ppermute | solution.py:347
  24.1 1.7 %collective-permute-start.8 = (bf16[256,256]{1,0:T(8,128)(2,1)S(1)}, bf16[256,256]{1,0:T(8,128)(2,1)S(1)}, u32[]{:S(2)}, u32[]{:S(2)}) collective-permute-start(bf16[256,256]{1,0:T(8,128)(2,1)S(1)} %round_grad.1.refs_4_), channel_id=1, source_target_pairs={{0,12},{2,14},{4,8},{6,10},{8,4},{10,6},{12,0},{14,2},{16,28},{18,... | collective-permute-start | bytes 393224 | tf_op jit(solution)/shard_map/ppermute | solution.py:327
  26.1 1.5 %collective-permute-start.6 = (bf16[256,256]{1,0:T(8,128)(2,1)S(1)}, bf16[256,256]{1,0:T(8,128)(2,1)S(1)}, u32[]{:S(2)}, u32[]{:S(2)}) collective-permute-start(bf16[256,256]{1,0:T(8,128)(2,1)S(1)} %round_grad.1.refs_4_), channel_id=1, source_target_pairs={{0,4},{2,6},{4,0},{6,2},{8,12},{10,14},{12,8},{14,10},{16,20},{18,... | collective-permute-start | bytes 393224 | tf_op jit(solution)/shard_map/ppermute | solution.py:327
  27.7 2.9 %collective-permute-done.8.refs_7_ = bf16[256,256]{1,0:T(8,128)(2,1)S(1)} collective-permute-done((bf16[256,256]{1,0:T(8,128)(2,1)S(1)}, bf16[256,256]{1,0:T(8,128)(2,1)S(1)}, u32[]{:S(2)}, u32[]{:S(2)}) %collective-permute-start.8) | collective-permute-done | bytes 131104 | tf_op jit(solution)/shard_map/ppermute | solution.py:327
  30.9 1.0 %collective-permute-done.6.refs_5_ = bf16[256,256]{1,0:T(8,128)(2,1)S(1)} collective-permute-done((bf16[256,256]{1,0:T(8,128)(2,1)S(1)}, bf16[256,256]{1,0:T(8,128)(2,1)S(1)}, u32[]{:S(2)}, u32[]{:S(2)}) %collective-permute-start.6) | collective-permute-done | bytes 131104 | tf_op jit(solution)/shard_map/ppermute | solution.py:327
  32.5 1.6 %collective-permute-start.4 = (bf16[256,512]{1,0:T(8,128)(2,1)S(1)}, bf16[256,512]{1,0:T(8,128)(2,1)S(1)}, u32[]{:S(2)}, u32[]{:S(2)}) collective-permute-start(bf16[256,512]{1,0:T(8,128)(2,1)S(1)} %slice_near_diagonal.1), channel_id=1, source_target_pairs={{0,12},{2,14},{4,8},{6,10},{8,4},{10,6},{12,0},{14,2},{16,28},{18,... | collective-permute-start | bytes 786440 | tf_op jit(solution)/shard_map/ppermute | solution.py:327
  34.2 2.6 %collective-permute-start.11 = (f32[256,256]{1,0:T(8,128)S(1)}, f32[256,256]{1,0:T(8,128)S(1)}, u32[]{:S(2)}, u32[]{:S(2)}) collective-permute-start(f32[256,256]{1,0:T(8,128)S(1)} %weight_fold.2), channel_id=1, source_target_pairs={{0,16},{2,18},{4,20},{6,22},{8,24},{10,26},{12,28},{14,30},{16,0},... | collective-permute-start | bytes 786440 | tf_op jit(solution)/shard_map/ppermute | solution.py:327
  36.8 11.0 %collective-permute-done.4.refs_3_ = bf16[256,512]{1,0:T(8,128)(2,1)S(1)} collective-permute-done((bf16[256,512]{1,0:T(8,128)(2,1)S(1)}, bf16[256,512]{1,0:T(8,128)(2,1)S(1)}, u32[]{:S(2)}, u32[]{:S(2)}) %collective-permute-start.4) | collective-permute-done | bytes 262176 | tf_op jit(solution)/shard_map/ppermute | solution.py:327
  48.3 0.9 %collective-permute-done.11.b_ref = f32[256,256]{1,0:T(8,128)S(1)} collective-permute-done((f32[256,256]{1,0:T(8,128)S(1)}, f32[256,256]{1,0:T(8,128)S(1)}, u32[]{:S(2)}, u32[]{:S(2)}) %collective-permute-start.11) | collective-permute-done | bytes 262176 | tf_op jit(solution)/shard_map/ppermute | solution.py:327
  49.2 0.6 collective-permute-done.12.b_ref
  50.0 3.3 %collective-permute-start.20 = (bf16[256,256]{1,0:T(8,128)(2,1)S(1)}, bf16[256,256]{1,0:T(8,128)(2,1)S(1)}, u32[]{:S(2)}, u32[]{:S(2)}) collective-permute-start(bf16[256,256]{1,0:T(8,128)(2,1)S(1)} %weight_finish.1.refs_0_), channel_id=1, source_target_pairs={{0,12},{2,14},{4,8},{6,10},{8,4},{10,6},{12,0},{14,2},{16,28},{18,... | collective-permute-start | bytes 393224 | tf_op jit(solution)/shard_map/ppermute | solution.py:327
  53.4 0.7 %collective-permute-start.19 = (bf16[256,256]{1,0:T(8,128)(2,1)S(1)}, bf16[256,256]{1,0:T(8,128)(2,1)S(1)}, u32[]{:S(2)}, u32[]{:S(2)}) collective-permute-start(bf16[256,256]{1,0:T(8,128)(2,1)S(1)} %weight_finish.1.refs_0_), channel_id=1, source_target_pairs={{0,4},{2,6},{4,0},{6,2},{8,12},{10,14},{12,8},{14,10},{16,20},{18,... | collective-permute-start | bytes 393224 | tf_op jit(solution)/shard_map/ppermute | solution.py:327
  54.1 4.1 %collective-permute-done.13.refs_0_.refs_4_ = bf16[256,256]{1,0:T(8,128)(2,1)S(1)} collective-permute-done((bf16[256,256]{1,0:T(8,128)(2,1)S(1)}, bf16[256,256]{1,0:T(8,128)(2,1)S(1)}, u32[]{:S(2)}, u32[]{:S(2)}) %collective-permute-start.13) | collective-permute-done | bytes 131104 | tf_op jit(solution)/shard_map/ppermute | solution.py:327
  58.2 1.3 %collective-permute-start.15 = (bf16[256,256]{1,0:T(8,128)(2,1)S(1)}, bf16[256,256]{1,0:T(8,128)(2,1)S(1)}, u32[]{:S(2)}, u32[]{:S(2)}) collective-permute-start(bf16[256,256]{1,0:T(8,128)(2,1)S(1)} %collective-permute-done.13.refs_0_.refs_4_), channel_id=1, source_target_pairs={{0,4},{2,6},{4,0},{6,2},{8,12},{10,14},{12,8},{14,10},{16,20},{18,... | collective-permute-start | bytes 393224 | tf_op jit(solution)/shard_map/ppermute | solution.py:327
  60.1 1.6 %collective-permute-start.14 = (bf16[256,256]{1,0:T(8,128)(2,1)S(1)}, bf16[256,256]{1,0:T(8,128)(2,1)S(1)}, u32[]{:S(2)}, u32[]{:S(2)}) collective-permute-start(bf16[256,256]{1,0:T(8,128)(2,1)S(1)} %collective-permute-done.13.refs_0_.refs_4_), channel_id=1, source_target_pairs={{0,8},{2,10},{4,12},{6,14},{8,0},{10,2},{12,4},{14,6},{16,24},{18,... | collective-permute-start | bytes 393224 | tf_op jit(solution)/shard_map/ppermute | solution.py:327
  61.8 3.7 %collective-permute-done.16.refs_3_.refs_7_ = bf16[256,256]{1,0:T(8,128)(2,1)S(1)} collective-permute-done((bf16[256,256]{1,0:T(8,128)(2,1)S(1)}, bf16[256,256]{1,0:T(8,128)(2,1)S(1)}, u32[]{:S(2)}, u32[]{:S(2)}) %collective-permute-start.16) | collective-permute-done | bytes 131104 | tf_op jit(solution)/shard_map/ppermute | solution.py:327
  65.5 0.9 %collective-permute-done.15.refs_2_.refs_6_ = bf16[256,256]{1,0:T(8,128)(2,1)S(1)} collective-permute-done((bf16[256,256]{1,0:T(8,128)(2,1)S(1)}, bf16[256,256]{1,0:T(8,128)(2,1)S(1)}, u32[]{:S(2)}, u32[]{:S(2)}) %collective-permute-start.15) | collective-permute-done | bytes 131104 | tf_op jit(solution)/shard_map/ppermute | solution.py:327
  66.4 0.7 %collective-permute-done.14.refs_1_.refs_5_ = bf16[256,256]{1,0:T(8,128)(2,1)S(1)} collective-permute-done((bf16[256,256]{1,0:T(8,128)(2,1)S(1)}, bf16[256,256]{1,0:T(8,128)(2,1)S(1)}, u32[]{:S(2)}, u32[]{:S(2)}) %collective-permute-start.14) | collective-permute-done | bytes 131104 | tf_op jit(solution)/shard_map/ppermute | solution.py:327
  67.3 1.3 %weight_assemble.1.refs_1_ = bf16[4096,256]{1,0:T(8,128)(2,1)} custom-call(bf16[256,256]{1,0:T(8,128)(2,1)S(1)} %weight_finish.1.refs_0_, bf16[256,256]{1,0:T(8,128)(2,1)S(1)} %collective-permute-done.18.refs_1_, bf16[256,256]{1,0:T(8,128)(2,1)S(1)} %collective-permute-done.19.refs_2_, bf16[256,256]{1,0:T(8,128)(2,1)S(1)} %collective-permute-done.20.refs_3_, ...), custom_call_target="tpu_custom_call" | custom-call | tf_op jit(solution)/shard_map/weight_assemble/pallas_call | solution.py:313
  68.6 0.6 collective-permute-done.17.refs_0_
  69.2 0.8 %weight_complete.1 = bf16[4096,256]{1,0:T(8,128)(2,1)} custom-call(bf16[1024,256]{1,0:T(8,128)(2,1)S(1)} %collective-permute-done.17.refs_0_, bf16[4096,256]{1,0:T(8,128)(2,1)} %weight_assemble.1.refs_1_), custom_call_target="tpu_custom_call", output_to_operand_aliasing={{}: (1, {})} | custom-call | tf_op jit(solution)/shard_map/weight_complete/pallas_call | solution.py:313
  (41 shorter events, 3.9 us)
Async XLA Ops:
  0.6 1.6 %copy-start = (bf16[1,256,4096]{2,1,0:T(8,128)(2,1)S(1)}, bf16[1,256,4096]{2,1,0:T(8,128)(2,1)}, u32[]{:S(2)}) copy-start(bf16[1,256,4096]{2,1,0:T(8,128)(2,1)} %param.6) | copy-start | bytes 6291460
  2.2 5.1 %copy-start.2 = (bf16[4096,256]{1,0:T(8,128)(2,1)S(1)}, bf16[4096,256]{1,0:T(8,128)(2,1)}, u32[]{:S(2)}) copy-start(bf16[4096,256]{1,0:T(8,128)(2,1)} %w_ref.1) | copy-start | bytes 6291460
  2.7 17.3 %collective-permute-start.2 = (bf16[256,1024]{1,0:T(8,128)(2,1)S(1)}, bf16[256,1024]{1,0:T(8,128)(2,1)S(1)}, u32[]{:S(2)}, u32[]{:S(2)}) collective-permute-start(bf16[256,1024]{1,0:T(8,128)(2,1)S(1)} %get-tuple-element.25), channel_id=1, source_target_pairs={{0,4},{2,6},{4,0},{6,2},{8,12},{10,14},{12,8},{14,10},{16,20},{18,... | collective-permute-start | bytes 1572872 | tf_op jit(solution)/shard_map/ppermute | solution.py:327
  5.7 9.9 %copy-start.3 = (bf16[1,128,1024]{2,1,0:T(8,128)(2,1)S(1)}, bf16[1,128,1024]{2,1,0:T(8,128)(2,1)}, u32[]{:S(2)}) copy-start(bf16[1,128,1024]{2,1,0:T(8,128)(2,1)} %param.7) | copy-start | bytes 786436
  5.7 9.9 %copy-start.4 = (bf16[1,128,1024]{2,1,0:T(8,128)(2,1)S(1)}, bf16[1,128,1024]{2,1,0:T(8,128)(2,1)}, u32[]{:S(2)}) copy-start(bf16[1,128,1024]{2,1,0:T(8,128)(2,1)} %param.8) | copy-start | bytes 786436
  5.7 9.9 %copy-start.5 = (s32[1,256]{1,0:T(1,128)S(1)}, s32[1,256]{1,0:T(1,128)}, u32[]{:S(2)}) copy-start(s32[1,256]{1,0:T(1,128)} %param.10) | copy-start | bytes 3076
  5.7 9.9 %copy-start.6 = (s32[2]{0:T(128)S(1)}, s32[2]{0:T(128)}, u32[]{:S(2)}) copy-start(s32[2]{0:T(128)} %order_ref.1) | copy-start | bytes 28
  5.7 18.4 %collective-permute-start.3 = (bf16[256,1024]{1,0:T(8,128)(2,1)S(1)}, bf16[256,1024]{1,0:T(8,128)(2,1)S(1)}, u32[]{:S(2)}, u32[]{:S(2)}) collective-permute-start(bf16[256,1024]{1,0:T(8,128)(2,1)S(1)} %get-tuple-element.29), channel_id=1, source_target_pairs={{0,8},{2,10},{4,12},{6,14},{8,0},{10,2},{12,4},{14,6},{16,24},{18,... | collective-permute-start | bytes 1572872 | tf_op jit(solution)/shard_map/ppermute | solution.py:327
  8.1 6.1 %collective-permute-start = (f32[256,128]{1,0:T(8,128)S(1)}, f32[256,128]{1,0:T(8,128)S(1)}, u32[]{:S(2)}, u32[]{:S(2)}) collective-permute-start(f32[256,128]{1,0:T(8,128)S(1)} %get-tuple-element.20.refs_0_), channel_id=1, source_target_pairs={{0,1},{1,0},{2,3},{3,2},{4,5},{5,4},{6,7},{7,6},{8,9},{9,8},{10,11... | collective-permute-start | bytes 393224 | tf_op jit(solution)/shard_map/ppermute | solution.py:342
  9.6 6.0 %collective-permute-start.1 = (f32[256,128]{1,0:T(8,128)S(1)}, f32[256,128]{1,0:T(8,128)S(1)}, u32[]{:S(2)}, u32[]{:S(2)}) collective-permute-start(f32[256,128]{1,0:T(8,128)S(1)} %get-tuple-element.21.refs_2_), channel_id=1, source_target_pairs={{0,1},{1,0},{2,3},{3,2},{4,5},{5,4},{6,7},{7,6},{8,9},{9,8},{10,11... | collective-permute-start | bytes 393224 | tf_op jit(solution)/shard_map/ppermute | solution.py:342
  17.4 6.6 %collective-permute-start.5 = (f32[256,256]{1,0:T(8,128)S(1)}, f32[256,256]{1,0:T(8,128)S(1)}, u32[]{:S(2)}, u32[]{:S(2)}) collective-permute-start(f32[256,256]{1,0:T(8,128)S(1)} %get-tuple-element.30.a_ref), channel_id=1, source_target_pairs={{0,1},{1,0},{2,3},{3,2},{4,5},{5,4},{6,7},{7,6},{8,9},{9,8},{10,11... | collective-permute-start | bytes 786440 | tf_op jit(solution)/shard_map/ppermute | solution.py:347
  19.0 8.7 %collective-permute-start.9 = (bf16[256,512]{1,0:T(8,128)(2,1)S(1)}, bf16[256,512]{1,0:T(8,128)(2,1)S(1)}, u32[]{:S(2)}, u32[]{:S(2)}) collective-permute-start(bf16[256,512]{1,0:T(8,128)(2,1)S(1)} %get-tuple-element.33), channel_id=1, source_target_pairs={{0,12},{2,14},{4,8},{6,10},{8,4},{10,6},{12,0},{14,2},{16,28},{18,... | collective-permute-start | bytes 786440 | tf_op jit(solution)/shard_map/ppermute | solution.py:327
  21.3 11.2 %copy-start.1 = (bf16[1,256,4096]{2,1,0:T(8,128)(2,1)S(1)}, bf16[1,256,4096]{2,1,0:T(8,128)(2,1)}, u32[]{:S(2)}) copy-start(bf16[1,256,4096]{2,1,0:T(8,128)(2,1)} %param.6) | copy-start | bytes 6291460
  24.1 6.5 %collective-permute-start.8 = (bf16[256,256]{1,0:T(8,128)(2,1)S(1)}, bf16[256,256]{1,0:T(8,128)(2,1)S(1)}, u32[]{:S(2)}, u32[]{:S(2)}) collective-permute-start(bf16[256,256]{1,0:T(8,128)(2,1)S(1)} %round_grad.1.refs_4_), channel_id=1, source_target_pairs={{0,12},{2,14},{4,8},{6,10},{8,4},{10,6},{12,0},{14,2},{16,28},{18,... | collective-permute-start | bytes 393224 | tf_op jit(solution)/shard_map/ppermute | solution.py:327
  25.8 5.2 %collective-permute-start.7 = (bf16[256,256]{1,0:T(8,128)(2,1)S(1)}, bf16[256,256]{1,0:T(8,128)(2,1)S(1)}, u32[]{:S(2)}, u32[]{:S(2)}) collective-permute-start(bf16[256,256]{1,0:T(8,128)(2,1)S(1)} %round_grad.1.refs_4_), channel_id=1, source_target_pairs={{0,8},{2,10},{4,12},{6,14},{8,0},{10,2},{12,4},{14,6},{16,24},{18,... | collective-permute-start | bytes 393224 | tf_op jit(solution)/shard_map/ppermute | solution.py:327
  26.1 5.8 %collective-permute-start.6 = (bf16[256,256]{1,0:T(8,128)(2,1)S(1)}, bf16[256,256]{1,0:T(8,128)(2,1)S(1)}, u32[]{:S(2)}, u32[]{:S(2)}) collective-permute-start(bf16[256,256]{1,0:T(8,128)(2,1)S(1)} %round_grad.1.refs_4_), channel_id=1, source_target_pairs={{0,4},{2,6},{4,0},{6,2},{8,12},{10,14},{12,8},{14,10},{16,20},{18,... | collective-permute-start | bytes 393224 | tf_op jit(solution)/shard_map/ppermute | solution.py:327
  32.3 1.8 %collective-permute-start.10 = (f32[256,256]{1,0:T(8,128)S(1)}, f32[256,256]{1,0:T(8,128)S(1)}, u32[]{:S(2)}, u32[]{:S(2)}) collective-permute-start(f32[256,256]{1,0:T(8,128)S(1)} %get-tuple-element.35), channel_id=1, source_target_pairs={{0,2},{2,0},{4,6},{6,4},{8,10},{10,8},{12,14},{14,12},{16,18},{18,... | collective-permute-start | bytes 786440 | tf_op jit(solution)/shard_map/ppermute | solution.py:327
  32.5 15.3 %collective-permute-start.4 = (bf16[256,512]{1,0:T(8,128)(2,1)S(1)}, bf16[256,512]{1,0:T(8,128)(2,1)S(1)}, u32[]{:S(2)}, u32[]{:S(2)}) collective-permute-start(bf16[256,512]{1,0:T(8,128)(2,1)S(1)} %slice_near_diagonal.1), channel_id=1, source_target_pairs={{0,12},{2,14},{4,8},{6,10},{8,4},{10,6},{12,0},{14,2},{16,28},{18,... | collective-permute-start | bytes 786440 | tf_op jit(solution)/shard_map/ppermute | solution.py:327
  34.2 15.0 %collective-permute-start.11 = (f32[256,256]{1,0:T(8,128)S(1)}, f32[256,256]{1,0:T(8,128)S(1)}, u32[]{:S(2)}, u32[]{:S(2)}) collective-permute-start(f32[256,256]{1,0:T(8,128)S(1)} %weight_fold.2), channel_id=1, source_target_pairs={{0,16},{2,18},{4,20},{6,22},{8,24},{10,26},{12,28},{14,30},{16,0},... | collective-permute-start | bytes 786440 | tf_op jit(solution)/shard_map/ppermute | solution.py:327
  48.3 1.6 %collective-permute-start.12 = (f32[256,256]{1,0:T(8,128)S(1)}, f32[256,256]{1,0:T(8,128)S(1)}, u32[]{:S(2)}, u32[]{:S(2)}) collective-permute-start(f32[256,256]{1,0:T(8,128)S(1)} %get-tuple-element.36), channel_id=1, source_target_pairs={{0,2},{2,0},{4,6},{6,4},{8,10},{10,8},{12,14},{14,12},{16,18},{18,... | collective-permute-start | bytes 786440 | tf_op jit(solution)/shard_map/ppermute | solution.py:327
  50.0 8.3 %collective-permute-start.13 = (bf16[256,256]{1,0:T(8,128)(2,1)S(1)}, bf16[256,256]{1,0:T(8,128)(2,1)S(1)}, u32[]{:S(2)}, u32[]{:S(2)}) collective-permute-start(bf16[256,256]{1,0:T(8,128)(2,1)S(1)} %weight_finish.1.refs_0_), channel_id=1, source_target_pairs={{0,16},{2,18},{4,20},{6,22},{8,24},{10,26},{12,28},{14,30},{16,0},... | collective-permute-start | bytes 393224 | tf_op jit(solution)/shard_map/ppermute | solution.py:327
  50.0 10.0 %collective-permute-start.20 = (bf16[256,256]{1,0:T(8,128)(2,1)S(1)}, bf16[256,256]{1,0:T(8,128)(2,1)S(1)}, u32[]{:S(2)}, u32[]{:S(2)}) collective-permute-start(bf16[256,256]{1,0:T(8,128)(2,1)S(1)} %weight_finish.1.refs_0_), channel_id=1, source_target_pairs={{0,12},{2,14},{4,8},{6,10},{8,4},{10,6},{12,0},{14,2},{16,28},{18,... | collective-permute-start | bytes 393224 | tf_op jit(solution)/shard_map/ppermute | solution.py:327
  53.4 8.3 %collective-permute-start.19 = (bf16[256,256]{1,0:T(8,128)(2,1)S(1)}, bf16[256,256]{1,0:T(8,128)(2,1)S(1)}, u32[]{:S(2)}, u32[]{:S(2)}) collective-permute-start(bf16[256,256]{1,0:T(8,128)(2,1)S(1)} %weight_finish.1.refs_0_), channel_id=1, source_target_pairs={{0,4},{2,6},{4,0},{6,2},{8,12},{10,14},{12,8},{14,10},{16,20},{18,... | collective-permute-start | bytes 393224 | tf_op jit(solution)/shard_map/ppermute | solution.py:327
  54.1 7.6 %collective-permute-start.18 = (bf16[256,256]{1,0:T(8,128)(2,1)S(1)}, bf16[256,256]{1,0:T(8,128)(2,1)S(1)}, u32[]{:S(2)}, u32[]{:S(2)}) collective-permute-start(bf16[256,256]{1,0:T(8,128)(2,1)S(1)} %weight_finish.1.refs_0_), channel_id=1, source_target_pairs={{0,8},{2,10},{4,12},{6,14},{8,0},{10,2},{12,4},{14,6},{16,24},{18,... | collective-permute-start | bytes 393224 | tf_op jit(solution)/shard_map/ppermute | solution.py:327
  58.2 7.3 %collective-permute-start.16 = (bf16[256,256]{1,0:T(8,128)(2,1)S(1)}, bf16[256,256]{1,0:T(8,128)(2,1)S(1)}, u32[]{:S(2)}, u32[]{:S(2)}) collective-permute-start(bf16[256,256]{1,0:T(8,128)(2,1)S(1)} %collective-permute-done.13.refs_0_.refs_4_), channel_id=1, source_target_pairs={{0,12},{2,14},{4,8},{6,10},{8,4},{10,6},{12,0},{14,2},{16,28},{18,... | collective-permute-start | bytes 393224 | tf_op jit(solution)/shard_map/ppermute | solution.py:327
  58.2 8.2 %collective-permute-start.15 = (bf16[256,256]{1,0:T(8,128)(2,1)S(1)}, bf16[256,256]{1,0:T(8,128)(2,1)S(1)}, u32[]{:S(2)}, u32[]{:S(2)}) collective-permute-start(bf16[256,256]{1,0:T(8,128)(2,1)S(1)} %collective-permute-done.13.refs_0_.refs_4_), channel_id=1, source_target_pairs={{0,4},{2,6},{4,0},{6,2},{8,12},{10,14},{12,8},{14,10},{16,20},{18,... | collective-permute-start | bytes 393224 | tf_op jit(solution)/shard_map/ppermute | solution.py:327
  60.1 7.1 %collective-permute-start.14 = (bf16[256,256]{1,0:T(8,128)(2,1)S(1)}, bf16[256,256]{1,0:T(8,128)(2,1)S(1)}, u32[]{:S(2)}, u32[]{:S(2)}) collective-permute-start(bf16[256,256]{1,0:T(8,128)(2,1)S(1)} %collective-permute-done.13.refs_0_.refs_4_), channel_id=1, source_target_pairs={{0,8},{2,10},{4,12},{6,14},{8,0},{10,2},{12,4},{14,6},{16,24},{18,... | collective-permute-start | bytes 393224 | tf_op jit(solution)/shard_map/ppermute | solution.py:327
  61.8 5.5 %collective-permute-start.21 = (bf16[1024,256]{1,0:T(8,128)(2,1)S(1)}, bf16[1024,256]{1,0:T(8,128)(2,1)S(1)}, u32[]{:S(2)}, u32[]{:S(2)}) collective-permute-start(bf16[1024,256]{1,0:T(8,128)(2,1)S(1)} %stack.3), channel_id=1, source_target_pairs={{0,2},{2,0},{4,6},{6,4},{8,10},{10,8},{12,14},{14,12},{16,18},{18,... | collective-permute-start | bytes 1572872 | tf_op jit(solution)/shard_map/ppermute | solution.py:327
  67.2 2.0 %collective-permute-start.17 = (bf16[1024,256]{1,0:T(8,128)(2,1)S(1)}, bf16[1024,256]{1,0:T(8,128)(2,1)S(1)}, u32[]{:S(2)}, u32[]{:S(2)}) collective-permute-start(bf16[1024,256]{1,0:T(8,128)(2,1)S(1)} %stack.2), channel_id=1, source_target_pairs={{0,2},{2,0},{4,6},{6,4},{8,10},{10,8},{12,14},{14,12},{16,18},{18,... | collective-permute-start | bytes 1572872 | tf_op jit(solution)/shard_map/ppermute | solution.py:327

commit v9 on v7

--- a/solution.py
+++ b/solution.py
@@ -139,37 +139,28 @@
     return pl.multiple_of((((block_of(device) ^ k) * CORES + core) * 2 + high) * width, width)
 
 
-def slice_kernel(wanted, tok_ref, *refs):
-    slices, sems = refs[-1 - len(wanted) : -1], refs[-1]
+def slice_kernel(wanted, tok_ref, *slices):
     me = lax.axis_index("dp")
-    copies = []
     for (k, halves), ref in zip(wanted, slices):
         width = ref.shape[1] // (CORES * len(halves))
         for n, far_half in enumerate(halves):
             for core in range(CORES):
-                copy = pltpu.make_async_copy(
-                    tok_ref.at[:, pl.ds(half_cols(me, k, core, far_half, width), width)],
-                    ref.at[:, pl.ds((n * CORES + core) * width, width)],
-                    sems.at[len(copies)],
-                )
-                copy.start()
-                copies.append(copy)
-    for copy in copies:
-        copy.wait()
-
-
-def slice_tokens(tokens, wanted, name, after=()):
+                first = (n * CORES + core) * width
+                source = pl.ds(half_cols(me, k, core, far_half, width), width)
+                ref[:, first : first + width] = tok_ref[:, source]
+
+
+def slice_tokens(tokens, wanted, name):
     rows, features = tokens.shape
     half = features // (2 * BLOCK)
     return pl.pallas_call(
         functools.partial(slice_kernel, wanted),
         out_shape=[jax.ShapeDtypeStruct((rows, half * len(halves)), BF16) for _, halves in wanted],
-        in_specs=[ANY] * (1 + len(after)),
+        in_specs=[VMEM],
         out_specs=[VMEM] * len(wanted),
-        scratch_shapes=[pltpu.SemaphoreType.DMA((sum(2 * len(halves) for _, halves in wanted),))],
         compiler_params=LIMIT,
         name=name,
-    )(tokens, *after)
+    )(tokens)
 
 
 def project_kernel(tok_ref, w_ref, key_ref, value_ref):

time: 70.2 us -> 70 us (level)
    ppermute x19, starting transfers between devices: 20.9 us -> 21.6 us  [hop(): return lax.ppermute(value, 'dp', [(i, i ^ bits) for i in range(count)])]
  transfers between devices with their start and end apart: 22 -> 22, of which waited for: 14 -> 15; matrix products, arithmetic and copies ran while one was open for 0% -> 0% of each run, Pallas kernels for 8% -> 8%
where the time goes in v9:
time: 70 us; the launch traced here: 69.8 us
  waiting for transfers between devices  34.9 us (50%)
  starting transfers between devices  25.2 us (36%)
  Pallas kernels  7.32 us (10%)
  local copies, waits for them, and re-layouts  1.61 us (2%)
  between operations  0.81 us (1%)
    ppermute x19, waiting for transfers between devices, hop(): return lax.ppermute(value, 'dp', [(i, i ^ bits) for i in range(count)])  26.8 us
    ppermute x19, starting transfers between devices, hop(): return lax.ppermute(value, 'dp', [(i, i ^ bits) for i in range(count)])  21.6 us
    ppermute x1, waiting for transfers between devices, per_device_16x2(): lax.ppermute(keys, 'seq', swap)  4.06 us
    ppermute x1, waiting for transfers between devices, per_device_16x2(): grad = round_grad(terms, lax.ppermute(terms, 'seq', swap), [done])  2.58 us
    pallas_call x2, Pallas kernels, assemble(): pl.pallas_call(functools.partial(assemble_kernel, held, rows), out_shape=...  2.08 us
    pallas_call x1, Pallas kernels, attend(): pl.pallas_call(functools.partial(terms_kernel, len(kvs), 'seq'), out_shap...  1.8 us
    unnamed x14, local copies, waits for them, and re-layouts  1.61 us
    ppermute x1, starting transfers between devices, per_device_16x2(): lax.ppermute(keys, 'seq', swap)  1.56 us
  transfers between devices with their start and end apart: 22, of which 15 were waited for; matrix products, arithmetic and copies ran while one was open for 0% of the time, Pallas kernels for 8%

profile of v9, /device:TPU:0, one launch (start us, length us, event | category | flops | bytes accessed | tf_op | source)
XLA Modules:
  0.0 69.8 jit_solution(16818215147820941599)
XLA Ops:
  0.6 1.6 %copy-done = bf16[1,256,4096]{2,1,0:T(8,128)(2,1)S(1)} copy-done((bf16[1,256,4096]{2,1,0:T(8,128)(2,1)S(1)}, bf16[1,256,4096]{2,1,0:T(8,128)(2,1)}, u32[]{:S(2)}) %copy-start) | copy-done | bytes 2097176
  2.5 3.0 %collective-permute-start.2 = (bf16[256,1024]{1,0:T(8,128)(2,1)S(1)}, bf16[256,1024]{1,0:T(8,128)(2,1)S(1)}, u32[]{:S(2)}, u32[]{:S(2)}) collective-permute-start(bf16[256,1024]{1,0:T(8,128)(2,1)S(1)} %get-tuple-element.25), channel_id=1, source_target_pairs={{0,4},{2,6},{4,0},{6,2},{8,12},{10,14},{12,8},{14,10},{16,20},{18,... | collective-permute-start | bytes 1572872 | tf_op jit(solution)/shard_map/ppermute | solution.py:318
  5.5 1.6 %collective-permute-start.3 = (bf16[256,1024]{1,0:T(8,128)(2,1)S(1)}, bf16[256,1024]{1,0:T(8,128)(2,1)S(1)}, u32[]{:S(2)}, u32[]{:S(2)}) collective-permute-start(bf16[256,1024]{1,0:T(8,128)(2,1)S(1)} %get-tuple-element.26), channel_id=1, source_target_pairs={{0,8},{2,10},{4,12},{6,14},{8,0},{10,2},{12,4},{14,6},{16,24},{18,... | collective-permute-start | bytes 1572872 | tf_op jit(solution)/shard_map/ppermute | solution.py:318
  7.2 0.7 %project.1 = (f32[256,128]{1,0:T(8,128)S(1)}, f32[256,128]{1,0:T(8,128)S(1)}) custom-call(bf16[256,4096]{1,0:T(8,128)(2,1)S(1)} %bitcast.7, bf16[4096,256]{1,0:T(8,128)(2,1)S(1)} %copy-done.2), custom_call_target="tpu_custom_call" | custom-call | tf_op jit(solution)/shard_map/project/pallas_call | solution.py:174
  7.9 1.6 %collective-permute-start = (f32[256,128]{1,0:T(8,128)S(1)}, f32[256,128]{1,0:T(8,128)S(1)}, u32[]{:S(2)}, u32[]{:S(2)}) collective-permute-start(f32[256,128]{1,0:T(8,128)S(1)} %get-tuple-element.20.refs_0_), channel_id=1, source_target_pairs={{0,1},{1,0},{2,3},{3,2},{4,5},{5,4},{6,7},{7,6},{8,9},{9,8},{10,11... | collective-permute-start | bytes 393224 | tf_op jit(solution)/shard_map/ppermute | solution.py:333
  9.4 0.5 collective-permute-start.1
  10.0 4.1 %collective-permute-done.refs_1_ = f32[256,128]{1,0:T(8,128)S(1)} collective-permute-done((f32[256,128]{1,0:T(8,128)S(1)}, f32[256,128]{1,0:T(8,128)S(1)}, u32[]{:S(2)}, u32[]{:S(2)}) %collective-permute-start) | collective-permute-done | bytes 131104 | tf_op jit(solution)/shard_map/ppermute | solution.py:333
  14.0 1.4 %collective-permute-done.1.refs_3_ = f32[256,128]{1,0:T(8,128)S(1)} collective-permute-done((f32[256,128]{1,0:T(8,128)S(1)}, f32[256,128]{1,0:T(8,128)S(1)}, u32[]{:S(2)}, u32[]{:S(2)}) %collective-permute-start.1) | collective-permute-done | bytes 131104 | tf_op jit(solution)/shard_map/ppermute | solution.py:333
  15.4 1.8 %attention_terms.1 = (bf16[256,256]{1,0:T(8,128)(2,1)S(1)}, bf16[256,1024]{1,0:T(8,128)(2,1)S(1)}, bf16[256,1024]{1,0:T(8,128)(2,1)S(1)}, f32[256,256]{1,0:T(8,128)S(1)}) custom-call(s32[2]{0:T(128)S(1)} %copy-done.6, s32[2,128]{1,0:T(2,128)S(1)} %bitcast.11, bf16[128,1024]{1,0:T(8,128)(2,1)S(1)} %bitcast.9, bf16[128,1024]{1,0:T(8,128)(2,1)S(1)} %bitcast.10, ...), custom_call_target="tpu_custom_call" | custom-call | tf_op jit(solution)/shard_map/attention_terms/pallas_call | solution.py:103
  17.2 1.6 %collective-permute-start.5 = (f32[256,256]{1,0:T(8,128)S(1)}, f32[256,256]{1,0:T(8,128)S(1)}, u32[]{:S(2)}, u32[]{:S(2)}) collective-permute-start(f32[256,256]{1,0:T(8,128)S(1)} %get-tuple-element.30.a_ref), channel_id=1, source_target_pairs={{0,1},{1,0},{2,3},{3,2},{4,5},{5,4},{6,7},{7,6},{8,9},{9,8},{10,11... | collective-permute-start | bytes 786440 | tf_op jit(solution)/shard_map/ppermute | solution.py:338
  18.8 1.2 %collective-permute-start.9 = (bf16[256,512]{1,0:T(8,128)(2,1)S(1)}, bf16[256,512]{1,0:T(8,128)(2,1)S(1)}, u32[]{:S(2)}, u32[]{:S(2)}) collective-permute-start(bf16[256,512]{1,0:T(8,128)(2,1)S(1)} %get-tuple-element.33), channel_id=1, source_target_pairs={{0,12},{2,14},{4,8},{6,10},{8,4},{10,6},{12,0},{14,2},{16,28},{18,... | collective-permute-start | bytes 786440 | tf_op jit(solution)/shard_map/ppermute | solution.py:318
  20.0 1.3 %attention_outputs.1 = (bf16[128,1024]{1,0:T(8,128)(2,1)}, bf16[128,1024]{1,0:T(8,128)(2,1)}, f32[8,128]{1,0:T(8,128)S(1)}) custom-call(bf16[256,256]{1,0:T(8,128)(2,1)S(1)} %get-tuple-element.22.kv_ref, bf16[256,1024]{1,0:T(8,128)(2,1)S(1)} %get-tuple-element.23.low_ref, bf16[256,1024]{1,0:T(8,128)(2,1)S(1)} %get-tuple-element.24.ds_ref, ...), custom_call_target="tpu_custom_call" | custom-call | tf_op jit(solution)/shard_map/attention_outputs/pallas_call | solution.py:116
  21.3 2.6 %collective-permute-done.5.b_ref = f32[256,256]{1,0:T(8,128)S(1)} collective-permute-done((f32[256,256]{1,0:T(8,128)S(1)}, f32[256,256]{1,0:T(8,128)S(1)}, u32[]{:S(2)}, u32[]{:S(2)}) %collective-permute-start.5) | collective-permute-done | bytes 262176 | tf_op jit(solution)/shard_map/ppermute | solution.py:338
  23.9 1.9 %collective-permute-start.8 = (bf16[256,256]{1,0:T(8,128)(2,1)S(1)}, bf16[256,256]{1,0:T(8,128)(2,1)S(1)}, u32[]{:S(2)}, u32[]{:S(2)}) collective-permute-start(bf16[256,256]{1,0:T(8,128)(2,1)S(1)} %round_grad.1.refs_4_), channel_id=1, source_target_pairs={{0,12},{2,14},{4,8},{6,10},{8,4},{10,6},{12,0},{14,2},{16,28},{18,... | collective-permute-start | bytes 393224 | tf_op jit(solution)/shard_map/ppermute | solution.py:318
  25.9 1.5 %collective-permute-start.6 = (bf16[256,256]{1,0:T(8,128)(2,1)S(1)}, bf16[256,256]{1,0:T(8,128)(2,1)S(1)}, u32[]{:S(2)}, u32[]{:S(2)}) collective-permute-start(bf16[256,256]{1,0:T(8,128)(2,1)S(1)} %round_grad.1.refs_4_), channel_id=1, source_target_pairs={{0,4},{2,6},{4,0},{6,2},{8,12},{10,14},{12,8},{14,10},{16,20},{18,... | collective-permute-start | bytes 393224 | tf_op jit(solution)/shard_map/ppermute | solution.py:318
  27.5 2.9 %collective-permute-done.8.refs_7_ = bf16[256,256]{1,0:T(8,128)(2,1)S(1)} collective-permute-done((bf16[256,256]{1,0:T(8,128)(2,1)S(1)}, bf16[256,256]{1,0:T(8,128)(2,1)S(1)}, u32[]{:S(2)}, u32[]{:S(2)}) %collective-permute-start.8) | collective-permute-done | bytes 131104 | tf_op jit(solution)/shard_map/ppermute | solution.py:318
  30.7 0.9 %collective-permute-done.6.refs_5_ = bf16[256,256]{1,0:T(8,128)(2,1)S(1)} collective-permute-done((bf16[256,256]{1,0:T(8,128)(2,1)S(1)}, bf16[256,256]{1,0:T(8,128)(2,1)S(1)}, u32[]{:S(2)}, u32[]{:S(2)}) %collective-permute-start.6) | collective-permute-done | bytes 131104 | tf_op jit(solution)/shard_map/ppermute | solution.py:318
  32.3 1.8 %collective-permute-start.4 = (bf16[256,512]{1,0:T(8,128)(2,1)S(1)}, bf16[256,512]{1,0:T(8,128)(2,1)S(1)}, u32[]{:S(2)}, u32[]{:S(2)}) collective-permute-start(bf16[256,512]{1,0:T(8,128)(2,1)S(1)} %slice_near_diagonal.1), channel_id=1, source_target_pairs={{0,12},{2,14},{4,8},{6,10},{8,4},{10,6},{12,0},{14,2},{16,28},{18,... | collective-permute-start | bytes 786440 | tf_op jit(solution)/shard_map/ppermute | solution.py:318
  34.1 2.7 %collective-permute-start.11 = (f32[256,256]{1,0:T(8,128)S(1)}, f32[256,256]{1,0:T(8,128)S(1)}, u32[]{:S(2)}, u32[]{:S(2)}) collective-permute-start(f32[256,256]{1,0:T(8,128)S(1)} %weight_fold.2), channel_id=1, source_target_pairs={{0,16},{2,18},{4,20},{6,22},{8,24},{10,26},{12,28},{14,30},{16,0},... | collective-permute-start | bytes 786440 | tf_op jit(solution)/shard_map/ppermute | solution.py:318
  36.8 10.8 %collective-permute-done.4.refs_3_ = bf16[256,512]{1,0:T(8,128)(2,1)S(1)} collective-permute-done((bf16[256,512]{1,0:T(8,128)(2,1)S(1)}, bf16[256,512]{1,0:T(8,128)(2,1)S(1)}, u32[]{:S(2)}, u32[]{:S(2)}) %collective-permute-start.4) | collective-permute-done | bytes 262176 | tf_op jit(solution)/shard_map/ppermute | solution.py:318
  48.1 1.0 %collective-permute-done.11.b_ref = f32[256,256]{1,0:T(8,128)S(1)} collective-permute-done((f32[256,256]{1,0:T(8,128)S(1)}, f32[256,256]{1,0:T(8,128)S(1)}, u32[]{:S(2)}, u32[]{:S(2)}) %collective-permute-start.11) | collective-permute-done | bytes 262176 | tf_op jit(solution)/shard_map/ppermute | solution.py:318
  49.8 3.5 %collective-permute-start.20 = (bf16[256,256]{1,0:T(8,128)(2,1)S(1)}, bf16[256,256]{1,0:T(8,128)(2,1)S(1)}, u32[]{:S(2)}, u32[]{:S(2)}) collective-permute-start(bf16[256,256]{1,0:T(8,128)(2,1)S(1)} %weight_finish.1.refs_0_), channel_id=1, source_target_pairs={{0,12},{2,14},{4,8},{6,10},{8,4},{10,6},{12,0},{14,2},{16,28},{18,... | collective-permute-start | bytes 393224 | tf_op jit(solution)/shard_map/ppermute | solution.py:318
  53.3 0.8 %collective-permute-start.19 = (bf16[256,256]{1,0:T(8,128)(2,1)S(1)}, bf16[256,256]{1,0:T(8,128)(2,1)S(1)}, u32[]{:S(2)}, u32[]{:S(2)}) collective-permute-start(bf16[256,256]{1,0:T(8,128)(2,1)S(1)} %weight_finish.1.refs_0_), channel_id=1, source_target_pairs={{0,4},{2,6},{4,0},{6,2},{8,12},{10,14},{12,8},{14,10},{16,20},{18,... | collective-permute-start | bytes 393224 | tf_op jit(solution)/shard_map/ppermute | solution.py:318
  54.1 3.9 %collective-permute-done.13.refs_0_.refs_4_ = bf16[256,256]{1,0:T(8,128)(2,1)S(1)} collective-permute-done((bf16[256,256]{1,0:T(8,128)(2,1)S(1)}, bf16[256,256]{1,0:T(8,128)(2,1)S(1)}, u32[]{:S(2)}, u32[]{:S(2)}) %collective-permute-start.13) | collective-permute-done | bytes 131104 | tf_op jit(solution)/shard_map/ppermute | solution.py:318
  58.1 1.2 %collective-permute-start.15 = (bf16[256,256]{1,0:T(8,128)(2,1)S(1)}, bf16[256,256]{1,0:T(8,128)(2,1)S(1)}, u32[]{:S(2)}, u32[]{:S(2)}) collective-permute-start(bf16[256,256]{1,0:T(8,128)(2,1)S(1)} %collective-permute-done.13.refs_0_.refs_4_), channel_id=1, source_target_pairs={{0,4},{2,6},{4,0},{6,2},{8,12},{10,14},{12,8},{14,10},{16,20},{18,... | collective-permute-start | bytes 393224 | tf_op jit(solution)/shard_map/ppermute | solution.py:318
  59.8 1.8 %collective-permute-start.14 = (bf16[256,256]{1,0:T(8,128)(2,1)S(1)}, bf16[256,256]{1,0:T(8,128)(2,1)S(1)}, u32[]{:S(2)}, u32[]{:S(2)}) collective-permute-start(bf16[256,256]{1,0:T(8,128)(2,1)S(1)} %collective-permute-done.13.refs_0_.refs_4_), channel_id=1, source_target_pairs={{0,8},{2,10},{4,12},{6,14},{8,0},{10,2},{12,4},{14,6},{16,24},{18,... | collective-permute-start | bytes 393224 | tf_op jit(solution)/shard_map/ppermute | solution.py:318
  61.7 3.7 %collective-permute-done.16.refs_3_.refs_7_ = bf16[256,256]{1,0:T(8,128)(2,1)S(1)} collective-permute-done((bf16[256,256]{1,0:T(8,128)(2,1)S(1)}, bf16[256,256]{1,0:T(8,128)(2,1)S(1)}, u32[]{:S(2)}, u32[]{:S(2)}) %collective-permute-start.16) | collective-permute-done | bytes 131104 | tf_op jit(solution)/shard_map/ppermute | solution.py:318
  65.4 0.9 %collective-permute-done.15.refs_2_.refs_6_ = bf16[256,256]{1,0:T(8,128)(2,1)S(1)} collective-permute-done((bf16[256,256]{1,0:T(8,128)(2,1)S(1)}, bf16[256,256]{1,0:T(8,128)(2,1)S(1)}, u32[]{:S(2)}, u32[]{:S(2)}) %collective-permute-start.15) | collective-permute-done | bytes 131104 | tf_op jit(solution)/shard_map/ppermute | solution.py:318
  66.2 0.7 %collective-permute-done.14.refs_1_.refs_5_ = bf16[256,256]{1,0:T(8,128)(2,1)S(1)} collective-permute-done((bf16[256,256]{1,0:T(8,128)(2,1)S(1)}, bf16[256,256]{1,0:T(8,128)(2,1)S(1)}, u32[]{:S(2)}, u32[]{:S(2)}) %collective-permute-start.14) | collective-permute-done | bytes 131104 | tf_op jit(solution)/shard_map/ppermute | solution.py:318
  67.1 1.3 %weight_assemble.1.refs_1_ = bf16[4096,256]{1,0:T(8,128)(2,1)} custom-call(bf16[256,256]{1,0:T(8,128)(2,1)S(1)} %weight_finish.1.refs_0_, bf16[256,256]{1,0:T(8,128)(2,1)S(1)} %collective-permute-done.18.refs_1_, bf16[256,256]{1,0:T(8,128)(2,1)S(1)} %collective-permute-done.19.refs_2_, bf16[256,256]{1,0:T(8,128)(2,1)S(1)} %collective-permute-done.20.refs_3_, ...), custom_call_target="tpu_custom_call" | custom-call | tf_op jit(solution)/shard_map/weight_assemble/pallas_call | solution.py:304
  68.4 0.6 collective-permute-done.17.refs_0_
  69.0 0.8 %weight_complete.1 = bf16[4096,256]{1,0:T(8,128)(2,1)} custom-call(bf16[1024,256]{1,0:T(8,128)(2,1)S(1)} %collective-permute-done.17.refs_0_, bf16[4096,256]{1,0:T(8,128)(2,1)} %weight_assemble.1.refs_1_), custom_call_target="tpu_custom_call", output_to_operand_aliasing={{}: (1, {})} | custom-call | tf_op jit(solution)/shard_map/weight_complete/pallas_call | solution.py:304
  (41 shorter events, 3.3 us)
Async XLA Ops:
  0.6 1.6 %copy-start = (bf16[1,256,4096]{2,1,0:T(8,128)(2,1)S(1)}, bf16[1,256,4096]{2,1,0:T(8,128)(2,1)}, u32[]{:S(2)}) copy-start(bf16[1,256,4096]{2,1,0:T(8,128)(2,1)} %param.6) | copy-start | bytes 6291460
  2.2 4.9 %copy-start.2 = (bf16[4096,256]{1,0:T(8,128)(2,1)S(1)}, bf16[4096,256]{1,0:T(8,128)(2,1)}, u32[]{:S(2)}) copy-start(bf16[4096,256]{1,0:T(8,128)(2,1)} %w_ref.1) | copy-start | bytes 6291460
  2.5 17.5 %collective-permute-start.2 = (bf16[256,1024]{1,0:T(8,128)(2,1)S(1)}, bf16[256,1024]{1,0:T(8,128)(2,1)S(1)}, u32[]{:S(2)}, u32[]{:S(2)}) collective-permute-start(bf16[256,1024]{1,0:T(8,128)(2,1)S(1)} %get-tuple-element.25), channel_id=1, source_target_pairs={{0,4},{2,6},{4,0},{6,2},{8,12},{10,14},{12,8},{14,10},{16,20},{18,... | collective-permute-start | bytes 1572872 | tf_op jit(solution)/shard_map/ppermute | solution.py:318
  5.5 9.9 %copy-start.3 = (bf16[1,128,1024]{2,1,0:T(8,128)(2,1)S(1)}, bf16[1,128,1024]{2,1,0:T(8,128)(2,1)}, u32[]{:S(2)}) copy-start(bf16[1,128,1024]{2,1,0:T(8,128)(2,1)} %param.7) | copy-start | bytes 786436
  5.5 9.9 %copy-start.4 = (bf16[1,128,1024]{2,1,0:T(8,128)(2,1)S(1)}, bf16[1,128,1024]{2,1,0:T(8,128)(2,1)}, u32[]{:S(2)}) copy-start(bf16[1,128,1024]{2,1,0:T(8,128)(2,1)} %param.8) | copy-start | bytes 786436
  5.5 9.9 %copy-start.5 = (s32[1,256]{1,0:T(1,128)S(1)}, s32[1,256]{1,0:T(1,128)}, u32[]{:S(2)}) copy-start(s32[1,256]{1,0:T(1,128)} %param.10) | copy-start | bytes 3076
  5.5 9.9 %copy-start.6 = (s32[2]{0:T(128)S(1)}, s32[2]{0:T(128)}, u32[]{:S(2)}) copy-start(s32[2]{0:T(128)} %order_ref.1) | copy-start | bytes 28
  5.5 14.5 %collective-permute-start.3 = (bf16[256,1024]{1,0:T(8,128)(2,1)S(1)}, bf16[256,1024]{1,0:T(8,128)(2,1)S(1)}, u32[]{:S(2)}, u32[]{:S(2)}) collective-permute-start(bf16[256,1024]{1,0:T(8,128)(2,1)S(1)} %get-tuple-element.26), channel_id=1, source_target_pairs={{0,8},{2,10},{4,12},{6,14},{8,0},{10,2},{12,4},{14,6},{16,24},{18,... | collective-permute-start | bytes 1572872 | tf_op jit(solution)/shard_map/ppermute | solution.py:318
  7.9 6.1 %collective-permute-start = (f32[256,128]{1,0:T(8,128)S(1)}, f32[256,128]{1,0:T(8,128)S(1)}, u32[]{:S(2)}, u32[]{:S(2)}) collective-permute-start(f32[256,128]{1,0:T(8,128)S(1)} %get-tuple-element.20.refs_0_), channel_id=1, source_target_pairs={{0,1},{1,0},{2,3},{3,2},{4,5},{5,4},{6,7},{7,6},{8,9},{9,8},{10,11... | collective-permute-start | bytes 393224 | tf_op jit(solution)/shard_map/ppermute | solution.py:333
  9.4 6.0 %collective-permute-start.1 = (f32[256,128]{1,0:T(8,128)S(1)}, f32[256,128]{1,0:T(8,128)S(1)}, u32[]{:S(2)}, u32[]{:S(2)}) collective-permute-start(f32[256,128]{1,0:T(8,128)S(1)} %get-tuple-element.21.refs_2_), channel_id=1, source_target_pairs={{0,1},{1,0},{2,3},{3,2},{4,5},{5,4},{6,7},{7,6},{8,9},{9,8},{10,11... | collective-permute-start | bytes 393224 | tf_op jit(solution)/shard_map/ppermute | solution.py:333
  17.2 6.6 %collective-permute-start.5 = (f32[256,256]{1,0:T(8,128)S(1)}, f32[256,256]{1,0:T(8,128)S(1)}, u32[]{:S(2)}, u32[]{:S(2)}) collective-permute-start(f32[256,256]{1,0:T(8,128)S(1)} %get-tuple-element.30.a_ref), channel_id=1, source_target_pairs={{0,1},{1,0},{2,3},{3,2},{4,5},{5,4},{6,7},{7,6},{8,9},{9,8},{10,11... | collective-permute-start | bytes 786440 | tf_op jit(solution)/shard_map/ppermute | solution.py:338
  18.8 8.7 %collective-permute-start.9 = (bf16[256,512]{1,0:T(8,128)(2,1)S(1)}, bf16[256,512]{1,0:T(8,128)(2,1)S(1)}, u32[]{:S(2)}, u32[]{:S(2)}) collective-permute-start(bf16[256,512]{1,0:T(8,128)(2,1)S(1)} %get-tuple-element.33), channel_id=1, source_target_pairs={{0,12},{2,14},{4,8},{6,10},{8,4},{10,6},{12,0},{14,2},{16,28},{18,... | collective-permute-start | bytes 786440 | tf_op jit(solution)/shard_map/ppermute | solution.py:318
  20.0 12.2 %copy-start.1 = (bf16[1,256,4096]{2,1,0:T(8,128)(2,1)S(1)}, bf16[1,256,4096]{2,1,0:T(8,128)(2,1)}, u32[]{:S(2)}) copy-start(bf16[1,256,4096]{2,1,0:T(8,128)(2,1)} %param.6) | copy-start | bytes 6291460
  23.9 6.5 %collective-permute-start.8 = (bf16[256,256]{1,0:T(8,128)(2,1)S(1)}, bf16[256,256]{1,0:T(8,128)(2,1)S(1)}, u32[]{:S(2)}, u32[]{:S(2)}) collective-permute-start(bf16[256,256]{1,0:T(8,128)(2,1)S(1)} %round_grad.1.refs_4_), channel_id=1, source_target_pairs={{0,12},{2,14},{4,8},{6,10},{8,4},{10,6},{12,0},{14,2},{16,28},{18,... | collective-permute-start | bytes 393224 | tf_op jit(solution)/shard_map/ppermute | solution.py:318
  25.8 5.0 %collective-permute-start.7 = (bf16[256,256]{1,0:T(8,128)(2,1)S(1)}, bf16[256,256]{1,0:T(8,128)(2,1)S(1)}, u32[]{:S(2)}, u32[]{:S(2)}) collective-permute-start(bf16[256,256]{1,0:T(8,128)(2,1)S(1)} %round_grad.1.refs_4_), channel_id=1, source_target_pairs={{0,8},{2,10},{4,12},{6,14},{8,0},{10,2},{12,4},{14,6},{16,24},{18,... | collective-permute-start | bytes 393224 | tf_op jit(solution)/shard_map/ppermute | solution.py:318
  25.9 5.8 %collective-permute-start.6 = (bf16[256,256]{1,0:T(8,128)(2,1)S(1)}, bf16[256,256]{1,0:T(8,128)(2,1)S(1)}, u32[]{:S(2)}, u32[]{:S(2)}) collective-permute-start(bf16[256,256]{1,0:T(8,128)(2,1)S(1)} %round_grad.1.refs_4_), channel_id=1, source_target_pairs={{0,4},{2,6},{4,0},{6,2},{8,12},{10,14},{12,8},{14,10},{16,20},{18,... | collective-permute-start | bytes 393224 | tf_op jit(solution)/shard_map/ppermute | solution.py:318
  32.2 1.9 %collective-permute-start.10 = (f32[256,256]{1,0:T(8,128)S(1)}, f32[256,256]{1,0:T(8,128)S(1)}, u32[]{:S(2)}, u32[]{:S(2)}) collective-permute-start(f32[256,256]{1,0:T(8,128)S(1)} %get-tuple-element.35), channel_id=1, source_target_pairs={{0,2},{2,0},{4,6},{6,4},{8,10},{10,8},{12,14},{14,12},{16,18},{18,... | collective-permute-start | bytes 786440 | tf_op jit(solution)/shard_map/ppermute | solution.py:318
  32.3 15.3 %collective-permute-start.4 = (bf16[256,512]{1,0:T(8,128)(2,1)S(1)}, bf16[256,512]{1,0:T(8,128)(2,1)S(1)}, u32[]{:S(2)}, u32[]{:S(2)}) collective-permute-start(bf16[256,512]{1,0:T(8,128)(2,1)S(1)} %slice_near_diagonal.1), channel_id=1, source_target_pairs={{0,12},{2,14},{4,8},{6,10},{8,4},{10,6},{12,0},{14,2},{16,28},{18,... | collective-permute-start | bytes 786440 | tf_op jit(solution)/shard_map/ppermute | solution.py:318
  34.1 15.0 %collective-permute-start.11 = (f32[256,256]{1,0:T(8,128)S(1)}, f32[256,256]{1,0:T(8,128)S(1)}, u32[]{:S(2)}, u32[]{:S(2)}) collective-permute-start(f32[256,256]{1,0:T(8,128)S(1)} %weight_fold.2), channel_id=1, source_target_pairs={{0,16},{2,18},{4,20},{6,22},{8,24},{10,26},{12,28},{14,30},{16,0},... | collective-permute-start | bytes 786440 | tf_op jit(solution)/shard_map/ppermute | solution.py:318
  48.0 1.6 %collective-permute-start.12 = (f32[256,256]{1,0:T(8,128)S(1)}, f32[256,256]{1,0:T(8,128)S(1)}, u32[]{:S(2)}, u32[]{:S(2)}) collective-permute-start(f32[256,256]{1,0:T(8,128)S(1)} %get-tuple-element.36), channel_id=1, source_target_pairs={{0,2},{2,0},{4,6},{6,4},{8,10},{10,8},{12,14},{14,12},{16,18},{18,... | collective-permute-start | bytes 786440 | tf_op jit(solution)/shard_map/ppermute | solution.py:318
  49.7 8.3 %collective-permute-start.13 = (bf16[256,256]{1,0:T(8,128)(2,1)S(1)}, bf16[256,256]{1,0:T(8,128)(2,1)S(1)}, u32[]{:S(2)}, u32[]{:S(2)}) collective-permute-start(bf16[256,256]{1,0:T(8,128)(2,1)S(1)} %weight_finish.1.refs_0_), channel_id=1, source_target_pairs={{0,16},{2,18},{4,20},{6,22},{8,24},{10,26},{12,28},{14,30},{16,0},... | collective-permute-start | bytes 393224 | tf_op jit(solution)/shard_map/ppermute | solution.py:318
  49.8 9.9 %collective-permute-start.20 = (bf16[256,256]{1,0:T(8,128)(2,1)S(1)}, bf16[256,256]{1,0:T(8,128)(2,1)S(1)}, u32[]{:S(2)}, u32[]{:S(2)}) collective-permute-start(bf16[256,256]{1,0:T(8,128)(2,1)S(1)} %weight_finish.1.refs_0_), channel_id=1, source_target_pairs={{0,12},{2,14},{4,8},{6,10},{8,4},{10,6},{12,0},{14,2},{16,28},{18,... | collective-permute-start | bytes 393224 | tf_op jit(solution)/shard_map/ppermute | solution.py:318
  53.3 8.2 %collective-permute-start.19 = (bf16[256,256]{1,0:T(8,128)(2,1)S(1)}, bf16[256,256]{1,0:T(8,128)(2,1)S(1)}, u32[]{:S(2)}, u32[]{:S(2)}) collective-permute-start(bf16[256,256]{1,0:T(8,128)(2,1)S(1)} %weight_finish.1.refs_0_), channel_id=1, source_target_pairs={{0,4},{2,6},{4,0},{6,2},{8,12},{10,14},{12,8},{14,10},{16,20},{18,... | collective-permute-start | bytes 393224 | tf_op jit(solution)/shard_map/ppermute | solution.py:318
  54.1 7.4 %collective-permute-start.18 = (bf16[256,256]{1,0:T(8,128)(2,1)S(1)}, bf16[256,256]{1,0:T(8,128)(2,1)S(1)}, u32[]{:S(2)}, u32[]{:S(2)}) collective-permute-start(bf16[256,256]{1,0:T(8,128)(2,1)S(1)} %weight_finish.1.refs_0_), channel_id=1, source_target_pairs={{0,8},{2,10},{4,12},{6,14},{8,0},{10,2},{12,4},{14,6},{16,24},{18,... | collective-permute-start | bytes 393224 | tf_op jit(solution)/shard_map/ppermute | solution.py:318
  58.0 7.3 %collective-permute-start.16 = (bf16[256,256]{1,0:T(8,128)(2,1)S(1)}, bf16[256,256]{1,0:T(8,128)(2,1)S(1)}, u32[]{:S(2)}, u32[]{:S(2)}) collective-permute-start(bf16[256,256]{1,0:T(8,128)(2,1)S(1)} %collective-permute-done.13.refs_0_.refs_4_), channel_id=1, source_target_pairs={{0,12},{2,14},{4,8},{6,10},{8,4},{10,6},{12,0},{14,2},{16,28},{18,... | collective-permute-start | bytes 393224 | tf_op jit(solution)/shard_map/ppermute | solution.py:318
  58.1 8.2 %collective-permute-start.15 = (bf16[256,256]{1,0:T(8,128)(2,1)S(1)}, bf16[256,256]{1,0:T(8,128)(2,1)S(1)}, u32[]{:S(2)}, u32[]{:S(2)}) collective-permute-start(bf16[256,256]{1,0:T(8,128)(2,1)S(1)} %collective-permute-done.13.refs_0_.refs_4_), channel_id=1, source_target_pairs={{0,4},{2,6},{4,0},{6,2},{8,12},{10,14},{12,8},{14,10},{16,20},{18,... | collective-permute-start | bytes 393224 | tf_op jit(solution)/shard_map/ppermute | solution.py:318
  59.8 7.2 %collective-permute-start.14 = (bf16[256,256]{1,0:T(8,128)(2,1)S(1)}, bf16[256,256]{1,0:T(8,128)(2,1)S(1)}, u32[]{:S(2)}, u32[]{:S(2)}) collective-permute-start(bf16[256,256]{1,0:T(8,128)(2,1)S(1)} %collective-permute-done.13.refs_0_.refs_4_), channel_id=1, source_target_pairs={{0,8},{2,10},{4,12},{6,14},{8,0},{10,2},{12,4},{14,6},{16,24},{18,... | collective-permute-start | bytes 393224 | tf_op jit(solution)/shard_map/ppermute | solution.py:318
  61.6 5.5 %collective-permute-start.21 = (bf16[1024,256]{1,0:T(8,128)(2,1)S(1)}, bf16[1024,256]{1,0:T(8,128)(2,1)S(1)}, u32[]{:S(2)}, u32[]{:S(2)}) collective-permute-start(bf16[1024,256]{1,0:T(8,128)(2,1)S(1)} %stack.3), channel_id=1, source_target_pairs={{0,2},{2,0},{4,6},{6,4},{8,10},{10,8},{12,14},{14,12},{16,18},{18,... | collective-permute-start | bytes 1572872 | tf_op jit(solution)/shard_map/ppermute | solution.py:318
  67.0 2.0 %collective-permute-start.17 = (bf16[1024,256]{1,0:T(8,128)(2,1)S(1)}, bf16[1024,256]{1,0:T(8,128)(2,1)S(1)}, u32[]{:S(2)}, u32[]{:S(2)}) collective-permute-start(bf16[1024,256]{1,0:T(8,128)(2,1)S(1)} %stack.2), channel_id=1, source_target_pairs={{0,2},{2,0},{4,6},{6,4},{8,10},{10,8},{12,14},{14,12},{16,18},{18,... | collective-permute-start | bytes 1572872 | tf_op jit(solution)/shard_map/ppermute | solution.py:318
